TPU v7x, 32 devices: a whole 2x2x4 slice. The times are simulated.
32 devices in a mesh: parts: 2 (over y), tmpl: 4 (over x, core), chan: 4 (over z).
Axes of the slice: x: 2, y: 2, z: 4, core: 2. Of those that a mesh axis runs over, the one named last changes fastest.
Arguments:
- waveforms: bfloat16 [384, 1536], P(('parts', 'tmpl', 'chan')), parts along dimension 0
- templates: bfloat16 [32, 8, 600], P(('parts', 'tmpl'), 'chan'), parts along dimension 0
- selection: int32 [8, 4, 4, 6], P(('parts', 'tmpl'), 'chan'), parts along dimension 0, may hold values from -1 to 11, as said below
- channel_list: int32 [32, 8], P(('parts', 'tmpl'), 'chan'), parts along dimension 0, may hold values from 0 to 23, as said below
- moveouts: int32 [32, 8], P(('parts', 'tmpl'), 'chan'), parts along dimension 0, may hold values from 0 to 424
- weights: int32 [32, 8], P(('parts', 'tmpl'), 'chan'), parts along dimension 0, may hold values from 1 to 3
Outputs:
- detection: float32 [32, 512], P(('parts', 'tmpl'), 'chan'), parts along dimension 0
There are 2 independent parts, one for each index of `parts`. A program takes and returns all parts, laid end to end along the dimension named above; each array names one. Nothing has to cross between parts.
Inputs may be any that keep to these rules, and one draw needn't show every extreme that they name: `selection`: in each group of 6 slots the live entries come first, are distinct local rows, and number 1 to 6; in every channel group one owner receives 6 live slots from every recording device. `channel_list`: every entry names a live slot sent to the template's owner in the entry's channel group.
All inputs are finite; a program needn't handle non-finite values.
Results may differ from a plain program's by a relative error of at most 0.0003.
Values may be sent and summed in bfloat16 or wider, within the bound.
No kernel may reach another device: no remote copies, remote signals or barrier semaphores. Data moves between devices by JAX's collectives and lax.ppermute only.
A program may use at most 64 MiB of HBM per device.

v0:
```python
import jax
import jax.numpy as jnp
from jax import lax
from jax.sharding import PartitionSpec as P

LAGS = 512


EPS = 1e-06


def normalized_scores(segments, kernels):
    tlen = kernels.shape[-1]
    count = segments.shape[0]
    products = lax.conv_general_dilated(
        segments[None],
        kernels.reshape(count, 1, tlen),
        (1,),
        "VALID",
        feature_group_count=count,
        preferred_element_type=jnp.float32,
    )[0]
    seg = segments.astype(jnp.float32)
    running = jnp.concatenate(
        [jnp.zeros((count, 1), jnp.float32), jnp.cumsum(seg * seg, axis=1)], axis=1
    )
    lags = products.shape[1]
    energy = running[:, tlen : tlen + lags] - running[:, :lags]
    kerf = kernels.astype(jnp.float32)
    power = jnp.mean(kerf * kerf, axis=1, keepdims=True)
    return products / (
        jnp.sqrt(jnp.float32(tlen)) * jnp.sqrt((power + EPS) * (energy / tlen + EPS))
    )


def shards(waveforms, templates, selection, channel_list, moveouts, weights):
    owners = lax.axis_size("tmpl")
    capacity = selection.shape[3]
    width = waveforms.shape[1]
    outgoing = selection[0, 0]
    picked = waveforms[jnp.maximum(outgoing, 0).reshape(-1)]
    living = (outgoing.reshape(-1) >= 0)[:, None]
    packed = jnp.where(living, picked, jnp.zeros_like(picked)).reshape(owners, capacity, width)
    received = lax.all_to_all(packed, "tmpl", split_axis=0, concat_axis=0, tiled=True).reshape(
        owners * capacity, width
    )
    tmpl_count = templates.shape[0]
    slot_count = templates.shape[1]
    tlen = templates.shape[2]
    span = LAGS + tlen - 1
    rows = received[channel_list.reshape(-1)]

    def window(row, offset):
        return lax.dynamic_slice_in_dim(row, offset, span, 0)

    segments = jax.vmap(window)(rows, moveouts.reshape(-1))
    kernels = templates.reshape(-1, tlen)
    weight = weights.astype(jnp.float32)
    total = lax.psum(jnp.sum(weight * weight, axis=1), "chan")
    scores = normalized_scores(segments, kernels).reshape(tmpl_count, slot_count, LAGS)
    partial_value = jnp.sum(weight[:, :, None] * scores, axis=1)
    stacked = lax.psum_scatter(partial_value, "chan", scatter_dimension=1, tiled=True)
    return stacked / jnp.sqrt(total)[:, None]


def solution(mesh):
    placed = (
        P(("parts", "tmpl", "chan"), None),
        P(("parts", "tmpl"), "chan", None),
        P(("parts", "tmpl"), "chan", None, None),
        P(("parts", "tmpl"), "chan"),
        P(("parts", "tmpl"), "chan"),
        P(("parts", "tmpl"), "chan"),
    )
    return jax.shard_map(
        shards, mesh=mesh, in_specs=placed, out_specs=P(("parts", "tmpl"), "chan"), check_vma=False
    )
```

profile of v0, /device:TPU:0, one launch (start us, length us, event | category | flops | bytes accessed | tf_op | source)
XLA Modules:
  0.0 195.4 jit_solution(15712014905822410473)
XLA Ops:
  6.5 0.0 copy-start
  6.5 0.8 broadcast_maximum_fusion
  7.3 0.0 copy-done.2
  7.3 0.1 reshape.150
  7.4 0.0 copy-done
  7.4 0.6 gather_fusion
  8.1 0.7 broadcast_select_fusion
  8.8 4.3 %all-to-all-start = ((bf16[4,6,1536]{2,1,0:T(8,128)(2,1)}), bf16[4,6,1536]{2,1,0:T(8,128)(2,1)S(1)}, u32[]{:S(2)}, u32[]{:S(2)}) async-start(bf16[4,6,1536]{2,1,0:T(8,128)(2,1)} %broadcast_select_fusion), calls=%async_computation | async-start | bytes 196608 | tf_op jit(solution)/shard_map/all_to_all | solution.py:44
  13.1 0.0 reduce-scatter.4.cloned.1.call-start
  13.1 0.0 copy-done.3
  13.1 0.1 copy.38
  13.2 0.1 reshape.124
  13.3 0.7 copy-done.4
  14.0 0.1 copy.39
  14.1 0.1 reshape.125
  14.2 0.0 copy-done.1
  14.2 0.1 multiply_reduce_fusion
  14.3 0.2 copy.41
  14.5 0.0 copy-start.5
  14.6 0.1 add.50
  14.6 0.6 copy-done.5
  15.2 0.1 copy.37
  15.3 2.1 %all-to-all-done = bf16[4,6,1536]{2,1,0:T(8,128)(2,1)S(1)} async-done(((bf16[4,6,1536]{2,1,0:T(8,128)(2,1)}), bf16[4,6,1536]{2,1,0:T(8,128)(2,1)S(1)}, u32[]{:S(2)}, u32[]{:S(2)}) %all-to-all-start) | async-done | bytes 73760 | tf_op jit(solution)/shard_map/all_to_all | solution.py:44
  17.4 0.6 gather_fusion.1
  18.0 16.6 %while.1 = (s32[]{:T(128)}, bf16[8,1536]{1,0:T(8,128)(2,1)S(1)}, s32[8,2]{0,1:T(2,128)S(1)}, bf16[8,1111]{1,0:T(8,128)(2,1)S(1)}, s32[]{:T(128)}, /*index=5*/s32[]{:T(128)}) while((s32[]{:T(128)}, bf16[8,1536]{1,0:T(8,128)(2,1)S(1)}, s32[8,2]{0,1:T(2,128)S(1)}, bf16[8,1111]{1,0:T(8,128)(2,1)S(1)}, s32[]{:T(128)}, /*index=5*/s32[]{:T(128)}) %tuple.19), condition=%wide.while_cond, body=%wide.while_body.sunk | while | flops 2 | bytes 9001 | solution.py:54
  18.0 0.1 constant_dynamic-slice_fusion.2
  18.1 0.6 fusion.13
  18.7 1.3 dynamic-slice.7
  20.1 0.1 constant_dynamic-slice_fusion.2
  20.2 0.6 fusion.13
  20.8 1.3 dynamic-slice.7
  22.2 0.1 constant_dynamic-slice_fusion.2
  22.2 0.6 fusion.13
  22.8 1.3 dynamic-slice.7
  24.2 0.1 constant_dynamic-slice_fusion.2
  24.3 0.6 fusion.13
  24.9 1.3 dynamic-slice.7
  26.3 0.1 constant_dynamic-slice_fusion.2
  26.4 0.6 fusion.13
  27.0 1.3 dynamic-slice.7
  28.4 0.1 constant_dynamic-slice_fusion.2
  28.5 0.6 fusion.13
  29.1 1.3 dynamic-slice.7
  30.5 0.1 constant_dynamic-slice_fusion.2
  30.5 0.6 fusion.13
  31.1 1.3 dynamic-slice.7
  32.5 0.1 constant_dynamic-slice_fusion.2
  32.6 0.6 fusion.13
  33.2 1.3 dynamic-slice.7
  34.6 2.3 %reduce-window.6 = f32[8,9,128]{2,1,0:T(8,128)S(1)} reduce-window(f32[8,9,128]{2,1,0:T(8,128)S(1)} %copy.43, f32[]{:T(128)} %constant.12.clone.1), window={size=1x1x128 pad=0_0x0_0x127_0}, to_apply=%region_1.2 | reduce-window | flops 1170432 | bytes 73732 | tf_op jit(solution)/shard_map/reduce-window
  36.9 0.2 slice_reduce_fusion
  37.1 0.2 reduce-window.9
  37.3 0.1 add_bitcast_fusion
  37.4 1.0 copy.40
  38.4 126.9 %fusion.9 = f32[1,8,512]{1,0,2:T(1,128)S(1)} fusion(bf16[1,8,1111]{1,0,2:T(2,128)(2,1)S(1)} %copy.40, bf16[8,1,600]{0,1,2:T(2,128)(2,1)S(1)} %copy.41), kind=kOutput, calls=%fused_computation.31 | convolution fusion | flops 4915200 | bytes 43760 | tf_op jit(solution)/shard_map/conv_general_dilated | solution.py:15
  165.3 0.1 copy.42
  165.4 0.1 fusion.6
  165.5 0.1 multiply_reduce_fusion.1
  165.6 0.9 copy.44
  166.4 0.0 reduce-scatter.4.cloned.1.call-update
  166.5 12.5 %psum.7 = f32[4]{0:T(128)S(1)} all-reduce(f32[4]{0:T(128)S(1)} %multiply_reduce_fusion.2), channel_id=1, replica_groups=mesh['parts'=2,'tmpl'=4,'chan'=4] {'chan'}, use_global_device_ids=true, to_apply=%region_6.7 | all-reduce | flops 4 | bytes 32 | tf_op jit(solution)/shard_map/psum | solution.py:59
  179.0 8.0 %reduce-scatter.4.cloned.1.call-done = f32[128,4]{1,0:T(8,128)} async-done(((f32[512,4]{1,0:T(8,128)}), f32[128,4]{1,0:T(8,128)}) %reduce-scatter.4.cloned.1.call-update) | async-done | bytes 2064
  187.0 0.9 copy.45
  187.9 0.7 broadcast_divide_fusion
  (32 shorter events, 0.6 us)
Async XLA Ops:
  6.5 0.9 copy-start
  6.5 0.8 copy-start.2
  8.8 4.3 %copy-start.3 = (s32[4,2]{0,1:T(2,128)S(1)}, s32[4,2]{0,1:T(2,128)}, u32[]{:S(2)}) copy-start(s32[4,2]{0,1:T(2,128)} %param.9) | copy-start | bytes 100
  8.8 8.6 %all-to-all-start = ((bf16[4,6,1536]{2,1,0:T(8,128)(2,1)}), bf16[4,6,1536]{2,1,0:T(8,128)(2,1)S(1)}, u32[]{:S(2)}, u32[]{:S(2)}) async-start(bf16[4,6,1536]{2,1,0:T(8,128)(2,1)} %broadcast_select_fusion), calls=%async_computation | async-start | bytes 196608 | tf_op jit(solution)/shard_map/all_to_all | solution.py:44
  13.1 1.1 copy-start.1
  13.1 173.9 %reduce-scatter.4.cloned.1.call-start = ((), (), s32[]{:S(2)}) async-start(), calls=%async_computation.2 | async-start | bytes 327680
  13.3 0.7 copy-start.4
  14.5 0.7 copy-start.5
Sparse Core Ops, SparseCore 0:
  166.6 20.3 reduce-scatter.3
where the time goes:
time: 196 us; the launch traced here: 195 us
  matrix products  127 us (65%)
  local copies, waits for them, and re-layouts  22.8 us (12%)
  between operations  13.5 us (7%)
  blocking collectives  12.5 us (6%)
  waiting for transfers between devices  10.1 us (5%)
  other arithmetic  5.04 us (3%)
  starting transfers between devices  4.34 us (2%)
    conv_general_dilated x1, matrix products, normalized_scores(): lax.conv_general_dilated(segments[None], kernels.reshape(count, 1, tlen),...  127 us
    gather x32, local copies, waits for them, and re-layouts  16.4 us
    psum x1, blocking collectives, shards(): total = lax.psum(jnp.sum(weight * weight, axis=1), 'chan')  12.5 us
    unnamed x2, waiting for transfers between devices  8.03 us
    all_to_all x1, starting transfers between devices, shards(): lax.all_to_all(packed, 'tmpl', split_axis=0, concat_axis=0, tiled=True)  4.34 us
  transfers between devices with their start and end apart: 2, of which 2 were waited for; matrix products, arithmetic and copies ran while one was open for 0% of the time, Pallas kernels for 0%

commit v1 on v0

v1 whole, which is shorter than its diff:
```python
import functools

import jax
import jax.numpy as jnp
from jax import lax
from jax.experimental import pallas as pl
from jax.experimental.pallas import tpu as pltpu
from jax.sharding import PartitionSpec as P

LAGS = 512
EPS = 1e-06
LANES = 128
PAD = 16


def exchange(value, axis, distance):
    size = lax.axis_size(axis)
    return lax.ppermute(value, axis, [(i, i ^ distance) for i in range(size)])


def prepare(tlen, templates, weights, bands, box, scale, rows):
    count, slots, _ = templates.shape
    depth = box.shape[1]
    blocks = depth // LANES
    rows[...] = jnp.zeros_like(rows)
    for m in range(count):
        rows[m * slots : (m + 1) * slots, :tlen] = templates[m].astype(jnp.float32)
    row = lax.broadcasted_iota(jnp.int32, (LANES, LANES), 0)
    lane = lax.broadcasted_iota(jnp.int32, (LANES, LANES), 1)
    late = lane >= row
    zero = jnp.zeros((LANES, LANES), jnp.float32)
    values = rows[...]
    power = jnp.sum(values * values, axis=1, keepdims=True) / tlen
    factor = 1.0 / (jnp.sqrt(jnp.float32(tlen)) * jnp.sqrt(power + EPS))
    groups = LAGS // LANES
    for p in range(count * slots):
        before = zero
        for d in range(blocks):
            if d * LANES < tlen:
                part = jnp.broadcast_to(rows[p : p + 1, d * LANES : (d + 1) * LANES], (LANES, LANES))
                now = pltpu.roll(part, 0, axis=1, stride=1, stride_axis=0)
            else:
                now = zero
            bands[p * LANES : (p + 1) * LANES, d * LANES : (d + 1) * LANES] = jnp.where(late, now, before).astype(jnp.bfloat16)
            before = now
        weight = weights[p % slots, p // slots].astype(jnp.float32)
        scale[p * groups : (p + 1) * groups, :] = jnp.broadcast_to(factor[p : p + 1] * weight, (groups, LANES))
    tap = lax.broadcasted_iota(jnp.int32, (LANES, depth), 1) - lax.broadcasted_iota(jnp.int32, (LANES, depth), 0)
    box[...] = jnp.where((tap >= 0) & (tap < tlen), 1.0, 0.0).astype(jnp.bfloat16)


def correlate(owners, columns, tlen, capacity, spot, lists, moveouts, weights, *refs):
    selections, refs = refs[:owners], refs[owners:]
    records, refs = refs[:owners], refs[owners:]
    bands, box, scale = refs[:3]
    outs, (lanes, taps, squares, stacks, blocks) = refs[3 : 3 + columns], refs[3 + columns :]
    owner, column = spot[0], spot[1]
    slots, count = lists.shape
    depth = box.shape[1]
    pieces = records[0].shape[1] // LANES
    high = records[0].shape[0]
    groups = LAGS // LANES
    for k in range(owners):
        wide = records[k][...].astype(jnp.float32)
        for d in range(pieces):
            lanes[k, d * PAD : d * PAD + high, :] = wide[:, d * LANES : (d + 1) * LANES]
        lanes[k, pieces * PAD :, :] = jnp.zeros((lanes.shape[1] - pieces * PAD, LANES), jnp.float32)
    reach = groups + depth // LANES - 1
    lane = lax.broadcasted_iota(jnp.int32, (reach, LANES), 1)
    for p in range(count * slots):
        m, j = p // slots, p % slots
        entry = lists[j, m]
        k = (entry // capacity) ^ owner
        slot = entry % capacity
        local = jnp.int32(0)
        for other in range(owners):
            local = jnp.where(k == other, selections[other][0, 0, owner, slot], local)
        shift = moveouts[j, m]
        whole = shift // LANES
        rest = shift % LANES
        first = local + whole * PAD
        low = lanes[k, pl.ds(first, reach, stride=PAD), :]
        up = lanes[k, pl.ds(first + PAD, reach, stride=PAD), :]
        back = (LANES - rest) % LANES
        low = pltpu.roll(low, back, axis=1)
        up = pltpu.roll(up, back, axis=1)
        stacks[p, :reach, :] = jnp.where(lane < LANES - rest, low, up)
        for d in range(depth // LANES):
            piece = stacks[p, d : d + groups, :]
            taps[p * groups : (p + 1) * groups, d * LANES : (d + 1) * LANES] = piece
            squares[p * groups : (p + 1) * groups, d * LANES : (d + 1) * LANES] = piece * piece
    contract = (((1,), (1,)), ((), ()))
    square = squares[...]
    main = square.astype(jnp.bfloat16)
    left = (square - main.astype(jnp.float32)).astype(jnp.bfloat16)
    energy = lax.dot_general(main, box[...], contract, preferred_element_type=jnp.float32)
    energy += lax.dot_general(left, box[...], contract, preferred_element_type=jnp.float32)
    norm = scale[...] * lax.rsqrt(energy * (1.0 / tlen) + EPS)
    product = lax.dot_general(taps[...].astype(jnp.bfloat16), bands[...], contract, preferred_element_type=jnp.float32)
    for m in range(count):
        partial = jnp.zeros((groups, LANES), jnp.float32)
        total = jnp.int32(0)
        for j in range(slots):
            p = m * slots + j
            rows = slice(p * groups, (p + 1) * groups)
            partial += product[rows, p * LANES : (p + 1) * LANES] * norm[rows, :]
            total += weights[j, m] * weights[j, m]
        stacked = jnp.broadcast_to(total.astype(jnp.float32), (groups, LANES))
        blocks[:, m, :] = partial
        blocks[:, count + m, :] = stacked
    width = LAGS // columns
    if width == LANES:
        for k in range(columns):
            outs[k][...] = blocks[column ^ k]
    else:
        share = LANES // width
        for k in range(columns):
            target = column ^ k
            part = blocks[target // share]
            chosen = part[:, :width]
            for s in range(1, share):
                chosen = jnp.where(target % share == s, part[:, s * width : (s + 1) * width], chosen)
            outs[k][...] = chosen


def shards(waveforms, templates, selection, channel_list, moveouts, weights):
    owners = lax.axis_size("tmpl")
    columns = lax.axis_size("chan")
    capacity = selection.shape[3]
    count, slots, tlen = templates.shape
    pairs = count * slots
    groups = LAGS // LANES
    depth = -(-(tlen + LANES - 1) // LANES) * LANES
    pieces = waveforms.shape[1] // LANES
    smem = pl.BlockSpec(memory_space=pltpu.SMEM)
    vmem = pl.BlockSpec(memory_space=pltpu.VMEM)
    lists, offsets, factors = channel_list.T, moveouts.T, weights.T
    records, selections = [waveforms], [selection]
    distance = owners // 2
    reached = [0]
    while distance:
        records += [exchange(r, "tmpl", distance) for r in records]
        selections += [exchange(s, "tmpl", distance) for s in selections]
        reached += [k ^ distance for k in reached]
        distance //= 2
    order = [reached.index(k) for k in range(owners)]
    records = [records[i] for i in order]
    selections = [selections[i] for i in order]
    bands, box, scale = pl.pallas_call(
        functools.partial(prepare, tlen),
        out_shape=(
            jax.ShapeDtypeStruct((pairs * LANES, depth), jnp.bfloat16),
            jax.ShapeDtypeStruct((LANES, depth), jnp.bfloat16),
            jax.ShapeDtypeStruct((pairs * groups, LANES), jnp.float32),
        ),
        in_specs=[vmem, smem],
        out_specs=(vmem, vmem, vmem),
        scratch_shapes=[pltpu.VMEM((pairs, depth), jnp.float32)],
        name="prepare",
    )(templates, factors)
    spot = jnp.stack([lax.axis_index("tmpl"), lax.axis_index("chan")]).astype(jnp.int32)
    parts = pl.pallas_call(
        functools.partial(correlate, owners, columns, tlen, capacity),
        out_shape=tuple(jax.ShapeDtypeStruct((2 * count, LAGS // columns), jnp.float32) for _ in range(columns)),
        in_specs=[smem] * (4 + owners) + [vmem] * (owners + 3),
        out_specs=(vmem,) * columns,
        scratch_shapes=[
            pltpu.VMEM((owners, (pieces + 2) * PAD, LANES), jnp.float32),
            pltpu.VMEM((pairs * groups, depth), jnp.float32),
            pltpu.VMEM((pairs * groups, depth), jnp.float32),
            pltpu.VMEM((pairs, PAD, LANES), jnp.float32),
            pltpu.VMEM((groups, 2 * count, LANES), jnp.float32),
        ],
        name="correlate",
    )(spot, lists, offsets, factors, *selections, *records, bands, box, scale)
    parts = list(parts)
    distance = 1
    while distance < columns:
        kept = range(0, columns, 2 * distance)
        arrived = {k: exchange(parts[k + distance], "chan", distance) for k in kept}
        for k in kept:
            parts[k] = parts[k] + arrived[k]
        distance *= 2
    return parts[0][:count] / jnp.sqrt(parts[0][count:])


def solution(mesh):
    placed = (
        P(("parts", "tmpl", "chan"), None),
        P(("parts", "tmpl"), "chan", None),
        P(("parts", "tmpl"), "chan", None, None),
        P(("parts", "tmpl"), "chan"),
        P(("parts", "tmpl"), "chan"),
        P(("parts", "tmpl"), "chan"),
    )
    return jax.shard_map(
        shards, mesh=mesh, in_specs=placed, out_specs=P(("parts", "tmpl"), "chan"), check_vma=False
    )
```

time: 196 us -> 24.2 us (0.12)
  matrix products: 127 us -> 0 us
  local copies, waits for them, and re-layouts: 22.8 us -> 0.6 us
  between operations: 13.5 us -> 0.05 us
  blocking collectives: 12.5 us -> 0 us
  Pallas kernels: 0 us -> 5.58 us
  starting transfers between devices: 4.34 us -> 9.3 us
  waiting for transfers between devices: 10.1 us -> 5.89 us
  other arithmetic: 5.04 us -> 2.5 us
    conv_general_dilated x1 -> x0, matrix products: 127 us -> none  [normalized_scores(): lax.conv_general_dilated(segments[None], kernels.reshape(count, 1, tlen),...]
    gather x35 -> x0, local copies, waits for them, and re-layouts: 17.6 us -> none
    psum x1 -> x0, blocking collectives: 12.5 us -> none  [shards(): total = lax.psum(jnp.sum(weight * weight, axis=1), 'chan')]
    ppermute x0 -> x9, starting transfers between devices: none -> 9.3 us  [exchange(): return lax.ppermute(value, axis, [(i, i ^ distance) for i in range(size)])]
    unnamed x2 -> x0, waiting for transfers between devices: 8.03 us -> none
    ppermute x0 -> x9, waiting for transfers between devices: none -> 5.89 us  [exchange(): return lax.ppermute(value, axis, [(i, i ^ distance) for i in range(size)])]
    pallas_call x0 -> x2, Pallas kernels: none -> 5.58 us  [the longest x1 3.12 us: shards(): pl.pallas_call(functools.partial(correlate, owners, columns, tlen, capaci...]
    all_to_all x1 -> x0, starting transfers between devices: 4.34 us -> none  [shards(): lax.all_to_all(packed, 'tmpl', split_axis=0, concat_axis=0, tiled=True)]
  transfers between devices with their start and end apart: 2 -> 9, of which waited for: 2 -> 4; matrix products, arithmetic and copies ran while one was open for 0% -> 5% of each run, Pallas kernels for 0% -> 10%
where the time goes in v1:
time: 24.2 us; the launch traced here: 23.9 us
  starting transfers between devices  9.3 us (38%)
  waiting for transfers between devices  5.89 us (24%)
  Pallas kernels  5.58 us (23%)
  other arithmetic  2.5 us (10%)
  local copies, waits for them, and re-layouts  0.6 us (2%)
    ppermute x9, starting transfers between devices, exchange(): return lax.ppermute(value, axis, [(i, i ^ distance) for i in range(size)])  9.3 us
    ppermute x9, waiting for transfers between devices, exchange(): return lax.ppermute(value, axis, [(i, i ^ distance) for i in range(size)])  5.89 us
    pallas_call x1, Pallas kernels, shards(): pl.pallas_call(functools.partial(correlate, owners, columns, tlen, capaci...  3.12 us
    pallas_call x1, Pallas kernels, shards(): pl.pallas_call(functools.partial(prepare, tlen), out_shape=(jax.ShapeDtyp...  2.46 us
    add x2, other arithmetic, shards(): parts[k] = parts[k] + arrived[k]  1.36 us
    unnamed x12, local copies, waits for them, and re-layouts  0.6 us
    div x1, other arithmetic, shards(): return parts[0][:count] / jnp.sqrt(parts[0][count:])  0.59 us
    another operation x1, other arithmetic, shards(): jnp.stack([lax.axis_index('tmpl'), lax.axis_index('chan')])  0.56 us
  transfers between devices with their start and end apart: 9, of which 4 were waited for; matrix products, arithmetic and copies ran while one was open for 5% of the time, Pallas kernels for 10%

profile of v1, /device:TPU:0, one launch (start us, length us, event | category | flops | bytes accessed | tf_op | source)
XLA Modules:
  0.0 23.9 jit_solution(12043771146429279534)
XLA Ops:
  0.0 2.9 %collective-permute-start.4 = (bf16[12,1536]{1,0:T(8,128)(2,1)}, bf16[12,1536]{1,0:T(8,128)(2,1)S(1)}, u32[]{:S(2)}, u32[]{:S(2)}) collective-permute-start(bf16[12,1536]{1,0:T(8,128)(2,1)} %refs_4_.1), channel_id=1, source_target_pairs={{0,8},{4,12},{8,0},{12,4},{1,9},{5,13},{9,1},{13,5},{2,10},{6,14},... | collective-permute-start | bytes 110600 | tf_op jit(solution)/shard_map/ppermute | solution.py:18
  2.9 0.0 collective-permute-start
  2.9 0.1 collective-permute-start.1
  3.0 0.4 %collective-permute-start.3 = (bf16[12,1536]{1,0:T(8,128)(2,1)}, bf16[12,1536]{1,0:T(8,128)(2,1)S(1)}, u32[]{:S(2)}, u32[]{:S(2)}) collective-permute-start(bf16[12,1536]{1,0:T(8,128)(2,1)} %refs_4_.1), channel_id=1, source_target_pairs={{0,4},{4,0},{8,12},{12,8},{1,5},{5,1},{9,13},{13,9},{2,6},{6,2},{1... | collective-permute-start | bytes 110600 | tf_op jit(solution)/shard_map/ppermute | solution.py:18
  3.5 1.8 %collective-permute-done.4.refs_6_ = bf16[12,1536]{1,0:T(8,128)(2,1)S(1)} collective-permute-done((bf16[12,1536]{1,0:T(8,128)(2,1)}, bf16[12,1536]{1,0:T(8,128)(2,1)S(1)}, u32[]{:S(2)}, u32[]{:S(2)}) %collective-permute-start.4) | collective-permute-done | bytes 36896 | tf_op jit(solution)/shard_map/ppermute | solution.py:18
  5.2 0.0 copy-start
  5.2 0.0 collective-permute-start.5
  5.2 0.6 %pad_add_fusion.spot = s32[2]{0:T(128)} fusion(s32[1]{0:T(128)} %bitcast.1, s32[1]{0:T(128)} %bitcast), kind=kLoop, calls=%fused_computation.2 | loop fusion | flops 2 | bytes 16 | tf_op jit(solution)/shard_map/stack | solution.py:161
  5.8 2.5 %prepare.1 = (bf16[1024,768]{1,0:T(8,128)(2,1)}, bf16[128,768]{1,0:T(8,128)(2,1)}, f32[32,128]{1,0:T(8,128)}) custom-call(bf16[4,2,600]{2,1,0:T(2,128)(2,1)} %templates.1, s32[2,4]{1,0:T(2,128)} %bitcast.5), custom_call_target="tpu_custom_call" | custom-call | tf_op jit(solution)/shard_map/prepare/pallas_call | solution.py:149
  8.2 0.0 collective-permute-done.1.refs_2_
  8.2 0.0 copy-start.4
  8.2 0.6 %collective-permute-start.2 = (s32[1,1,4,6]{3,2,1,0:T(4,128)S(1)}, s32[1,1,4,6]{3,2,1,0:T(4,128)S(1)}, u32[]{:S(2)}, u32[]{:S(2)}) collective-permute-start(s32[1,1,4,6]{3,2,1,0:T(4,128)S(1)} %collective-permute-done.1.refs_2_), channel_id=1, source_target_pairs={{0,4},{4,0},{8,12},{12,8},{1,5},{5,1},{9,13},{13,9},{2,6},{6,2},{1... | collective-permute-start | bytes 296 | tf_op jit(solution)/shard_map/ppermute | solution.py:18
  8.8 0.0 collective-permute-done.refs_1_
  8.8 0.0 copy-start.3
  8.8 0.8 %collective-permute-done.2.refs_3_ = s32[1,1,4,6]{3,2,1,0:T(4,128)S(1)} collective-permute-done((s32[1,1,4,6]{3,2,1,0:T(4,128)S(1)}, s32[1,1,4,6]{3,2,1,0:T(4,128)S(1)}, u32[]{:S(2)}, u32[]{:S(2)}) %collective-permute-start.2) | collective-permute-done | bytes 128 | tf_op jit(solution)/shard_map/ppermute | solution.py:18
  9.6 0.0 copy-start.5
  9.6 0.0 collective-permute-done.3.refs_5_
  9.6 0.0 copy-start.1
  9.6 0.0 collective-permute-done.5.refs_7_
  9.6 0.0 copy-start.2
  9.7 0.0 copy-done
  9.7 0.0 copy-done.4
  9.7 0.0 copy-done.3
  9.7 0.5 %copy-done.5 = s32[1,1,4,6]{3,2,1,0:T(4,128)} copy-done((s32[1,1,4,6]{3,2,1,0:T(4,128)}, s32[1,1,4,6]{3,2,1,0:T(4,128)S(1)}, u32[]{:S(2)}) %copy-start.5) | copy-done | bytes 120
  10.2 0.0 copy-done.1
  10.3 0.0 copy-done.2
  10.3 3.1 %correlate.1 = (f32[8,128]{1,0:T(8,128)}, f32[8,128]{1,0:T(8,128)}, f32[8,128]{1,0:T(8,128)}, f32[8,128]{1,0:T(8,128)}) custom-call(s32[2]{0:T(128)} %pad_add_fusion.spot, s32[2,4]{1,0:T(2,128)} %bitcast.7, s32[2,4]{1,0:T(2,128)} %bitcast.8, s32[2,4]{1,0:T(2,128)} %bitcast.6, s32[1,1,4,6]{3,2,1,0:T(4,128)} %refs_0_.1, s32[1,1,4,6]{3,2,1,0:T(4,128)} %copy-done.3, ...), custom_call_target="tpu_custom_call" | custom-call | tf_op jit(solution)/shard_map/correlate/pallas_call | solution.py:162
  13.4 2.2 %collective-permute-start.7 = (f32[8,128]{1,0:T(8,128)}, f32[8,128]{1,0:T(8,128)S(1)}, u32[]{:S(2)}, u32[]{:S(2)}) collective-permute-start(f32[8,128]{1,0:T(8,128)} %get-tuple-element.18), channel_id=1, source_target_pairs={{0,1},{1,0},{2,3},{3,2},{4,5},{5,4},{6,7},{7,6},{8,9},{9,8},{10,11... | collective-permute-start | bytes 12296 | tf_op jit(solution)/shard_map/ppermute | solution.py:18
  15.6 0.1 collective-permute-start.6
  15.6 1.7 %collective-permute-done.7 = f32[8,128]{1,0:T(8,128)S(1)} collective-permute-done((f32[8,128]{1,0:T(8,128)}, f32[8,128]{1,0:T(8,128)S(1)}, u32[]{:S(2)}, u32[]{:S(2)}) %collective-permute-start.7) | collective-permute-done | bytes 4128 | tf_op jit(solution)/shard_map/ppermute | solution.py:18
  17.4 0.7 %add.10 = f32[8,128]{1,0:T(8,128)S(1)} add(f32[8,128]{1,0:T(8,128)} %get-tuple-element.17, f32[8,128]{1,0:T(8,128)S(1)} %collective-permute-done.7) | non-fusion elementwise | flops 1024 | bytes 12288 | tf_op jit(solution)/shard_map/add | solution.py:182
  18.0 3.0 %collective-permute-start.8 = (f32[8,128]{1,0:T(8,128)S(1)}, f32[8,128]{1,0:T(8,128)S(1)}, u32[]{:S(2)}, u32[]{:S(2)}) collective-permute-start(f32[8,128]{1,0:T(8,128)S(1)} %add.10), channel_id=1, source_target_pairs={{0,2},{1,3},{2,0},{3,1},{4,6},{5,7},{6,4},{7,5},{8,10},{9,11},{10,... | collective-permute-start | bytes 12296 | tf_op jit(solution)/shard_map/ppermute | solution.py:18
  21.1 0.0 collective-permute-done.6
  21.1 1.6 %collective-permute-done.8 = f32[8,128]{1,0:T(8,128)S(1)} collective-permute-done((f32[8,128]{1,0:T(8,128)S(1)}, f32[8,128]{1,0:T(8,128)S(1)}, u32[]{:S(2)}, u32[]{:S(2)}) %collective-permute-start.8) | collective-permute-done | bytes 4128 | tf_op jit(solution)/shard_map/ppermute | solution.py:18
  22.7 0.7 %add_add_fusion = f32[8,128]{1,0:T(8,128)S(1)} fusion(f32[8,128]{1,0:T(8,128)S(1)} %collective-permute-done.8, f32[8,128]{1,0:T(8,128)} %get-tuple-element.15, f32[8,128]{1,0:T(8,128)S(1)} %collective-permute-done.6), kind=kLoop, calls=%fused_computation | loop fusion | flops 2048 | bytes 16384 | tf_op jit(solution)/shard_map/add | solution.py:182
  23.3 0.6 %rsqrt_multiply_fusion = f32[4,128]{1,0:T(4,128)} fusion(f32[8,128]{1,0:T(8,128)S(1)} %add_add_fusion), kind=kLoop, calls=%fused_computation.1 | loop fusion | flops 512 | bytes 6144 | tf_op jit(solution)/shard_map/div | solution.py:184
Async XLA Ops:
  0.0 5.2 %collective-permute-start.4 = (bf16[12,1536]{1,0:T(8,128)(2,1)}, bf16[12,1536]{1,0:T(8,128)(2,1)S(1)}, u32[]{:S(2)}, u32[]{:S(2)}) collective-permute-start(bf16[12,1536]{1,0:T(8,128)(2,1)} %refs_4_.1), channel_id=1, source_target_pairs={{0,8},{4,12},{8,0},{12,4},{1,9},{5,13},{9,1},{13,5},{2,10},{6,14},... | collective-permute-start | bytes 110600 | tf_op jit(solution)/shard_map/ppermute | solution.py:18
  2.9 5.9 %collective-permute-start = (s32[1,1,4,6]{3,2,1,0:T(4,128)}, s32[1,1,4,6]{3,2,1,0:T(4,128)S(1)}, u32[]{:S(2)}, u32[]{:S(2)}) collective-permute-start(s32[1,1,4,6]{3,2,1,0:T(4,128)} %refs_0_.1), channel_id=1, source_target_pairs={{0,4},{4,0},{8,12},{12,8},{1,5},{5,1},{9,13},{13,9},{2,6},{6,2},{1... | collective-permute-start | bytes 296 | tf_op jit(solution)/shard_map/ppermute | solution.py:18
  2.9 5.3 %collective-permute-start.1 = (s32[1,1,4,6]{3,2,1,0:T(4,128)}, s32[1,1,4,6]{3,2,1,0:T(4,128)S(1)}, u32[]{:S(2)}, u32[]{:S(2)}) collective-permute-start(s32[1,1,4,6]{3,2,1,0:T(4,128)} %refs_0_.1), channel_id=1, source_target_pairs={{0,8},{4,12},{8,0},{12,4},{1,9},{5,13},{9,1},{13,5},{2,10},{6,14},... | collective-permute-start | bytes 296 | tf_op jit(solution)/shard_map/ppermute | solution.py:18
  3.0 6.6 %collective-permute-start.3 = (bf16[12,1536]{1,0:T(8,128)(2,1)}, bf16[12,1536]{1,0:T(8,128)(2,1)S(1)}, u32[]{:S(2)}, u32[]{:S(2)}) collective-permute-start(bf16[12,1536]{1,0:T(8,128)(2,1)} %refs_4_.1), channel_id=1, source_target_pairs={{0,4},{4,0},{8,12},{12,8},{1,5},{5,1},{9,13},{13,9},{2,6},{6,2},{1... | collective-permute-start | bytes 110600 | tf_op jit(solution)/shard_map/ppermute | solution.py:18
  5.2 4.4 %copy-start = (bf16[12,1536]{1,0:T(8,128)(2,1)}, bf16[12,1536]{1,0:T(8,128)(2,1)S(1)}, u32[]{:S(2)}) copy-start(bf16[12,1536]{1,0:T(8,128)(2,1)S(1)} %collective-permute-done.4.refs_6_) | copy-start | bytes 110596
  5.2 4.4 %collective-permute-start.5 = (bf16[12,1536]{1,0:T(8,128)(2,1)S(1)}, bf16[12,1536]{1,0:T(8,128)(2,1)S(1)}, u32[]{:S(2)}, u32[]{:S(2)}) collective-permute-start(bf16[12,1536]{1,0:T(8,128)(2,1)S(1)} %collective-permute-done.4.refs_6_), channel_id=1, source_target_pairs={{0,4},{4,0},{8,12},{12,8},{1,5},{5,1},{9,13},{13,9},{2,6},{6,2},{1... | collective-permute-start | bytes 110600 | tf_op jit(solution)/shard_map/ppermute | solution.py:18
  8.2 1.4 %copy-start.4 = (s32[1,1,4,6]{3,2,1,0:T(4,128)}, s32[1,1,4,6]{3,2,1,0:T(4,128)S(1)}, u32[]{:S(2)}) copy-start(s32[1,1,4,6]{3,2,1,0:T(4,128)S(1)} %collective-permute-done.1.refs_2_) | copy-start | bytes 292
  8.2 1.4 %collective-permute-start.2 = (s32[1,1,4,6]{3,2,1,0:T(4,128)S(1)}, s32[1,1,4,6]{3,2,1,0:T(4,128)S(1)}, u32[]{:S(2)}, u32[]{:S(2)}) collective-permute-start(s32[1,1,4,6]{3,2,1,0:T(4,128)S(1)} %collective-permute-done.1.refs_2_), channel_id=1, source_target_pairs={{0,4},{4,0},{8,12},{12,8},{1,5},{5,1},{9,13},{13,9},{2,6},{6,2},{1... | collective-permute-start | bytes 296 | tf_op jit(solution)/shard_map/ppermute | solution.py:18
  8.8 0.9 %copy-start.3 = (s32[1,1,4,6]{3,2,1,0:T(4,128)}, s32[1,1,4,6]{3,2,1,0:T(4,128)S(1)}, u32[]{:S(2)}) copy-start(s32[1,1,4,6]{3,2,1,0:T(4,128)S(1)} %collective-permute-done.refs_1_) | copy-start | bytes 292
  9.6 0.6 %copy-start.5 = (s32[1,1,4,6]{3,2,1,0:T(4,128)}, s32[1,1,4,6]{3,2,1,0:T(4,128)S(1)}, u32[]{:S(2)}) copy-start(s32[1,1,4,6]{3,2,1,0:T(4,128)S(1)} %collective-permute-done.2.refs_3_) | copy-start | bytes 292
  9.6 0.6 %copy-start.1 = (bf16[12,1536]{1,0:T(8,128)(2,1)}, bf16[12,1536]{1,0:T(8,128)(2,1)S(1)}, u32[]{:S(2)}) copy-start(bf16[12,1536]{1,0:T(8,128)(2,1)S(1)} %collective-permute-done.3.refs_5_) | copy-start | bytes 110596
  9.6 0.6 %copy-start.2 = (bf16[12,1536]{1,0:T(8,128)(2,1)}, bf16[12,1536]{1,0:T(8,128)(2,1)S(1)}, u32[]{:S(2)}) copy-start(bf16[12,1536]{1,0:T(8,128)(2,1)S(1)} %collective-permute-done.5.refs_7_) | copy-start | bytes 110596
  13.4 4.0 %collective-permute-start.7 = (f32[8,128]{1,0:T(8,128)}, f32[8,128]{1,0:T(8,128)S(1)}, u32[]{:S(2)}, u32[]{:S(2)}) collective-permute-start(f32[8,128]{1,0:T(8,128)} %get-tuple-element.18), channel_id=1, source_target_pairs={{0,1},{1,0},{2,3},{3,2},{4,5},{5,4},{6,7},{7,6},{8,9},{9,8},{10,11... | collective-permute-start | bytes 12296 | tf_op jit(solution)/shard_map/ppermute | solution.py:18
  15.6 5.5 %collective-permute-start.6 = (f32[8,128]{1,0:T(8,128)}, f32[8,128]{1,0:T(8,128)S(1)}, u32[]{:S(2)}, u32[]{:S(2)}) collective-permute-start(f32[8,128]{1,0:T(8,128)} %get-tuple-element.16), channel_id=1, source_target_pairs={{0,1},{1,0},{2,3},{3,2},{4,5},{5,4},{6,7},{7,6},{8,9},{9,8},{10,11... | collective-permute-start | bytes 12296 | tf_op jit(solution)/shard_map/ppermute | solution.py:18
  18.0 4.6 %collective-permute-start.8 = (f32[8,128]{1,0:T(8,128)S(1)}, f32[8,128]{1,0:T(8,128)S(1)}, u32[]{:S(2)}, u32[]{:S(2)}) collective-permute-start(f32[8,128]{1,0:T(8,128)S(1)} %add.10), channel_id=1, source_target_pairs={{0,2},{1,3},{2,0},{3,1},{4,6},{5,7},{6,4},{7,5},{8,10},{9,11},{10,... | collective-permute-start | bytes 12296 | tf_op jit(solution)/shard_map/ppermute | solution.py:18

commit v2 on v1

v2 whole, which is shorter than its diff:
```python
import functools

import jax
import jax.numpy as jnp
from jax import lax
from jax.experimental import pallas as pl
from jax.experimental.pallas import tpu as pltpu
from jax.sharding import PartitionSpec as P

LAGS = 512
EPS = 1e-06
LANES = 128
PAD = 16
PARAMS = pltpu.CompilerParams(vmem_limit_bytes=8 * 1024 * 1024)
NT = (((1,), (1,)), ((), ()))
VMEM = pl.BlockSpec(memory_space=pltpu.VMEM)
HBM = pl.BlockSpec(memory_space=pltpu.HBM)


def exchange(value, axis, distance):
    size = lax.axis_size(axis)
    return lax.ppermute(value, axis, [(i, i ^ distance) for i in range(size)])


def fetch(sources, targets, sems):
    copies = [pltpu.make_async_copy(a, b, sems.at[i]) for i, (a, b) in enumerate(zip(sources, targets))]
    for copy in copies:
        copy.start()
    return copies


def pack(waveforms, selection, packed, taken, choice, sems):
    high, samples = waveforms.shape
    _, _, owners, capacity = choice.shape
    for copy in fetch((waveforms, selection), (taken, choice), sems):
        copy.wait()
    notes = choice[0, 0].astype(jnp.float32)
    notes = jnp.pad(notes, ((0, packed.shape[0] - high - owners), (0, samples - capacity)))
    packed[...] = jnp.concatenate([taken[...].astype(jnp.float32), notes], axis=0).astype(jnp.bfloat16)


def prepare(
    tlen, templates, lists, moveouts, weights, bands, box, scale, totals, table, rows, taken, entries, shifts, factors, sems
):
    copies = fetch((templates, lists, moveouts, weights), (taken, entries, shifts, factors), sems)
    count, slots, _ = taken.shape
    pairs = count * slots
    depth = box.shape[1]
    groups = LAGS // LANES
    tap = lax.broadcasted_iota(jnp.int32, (LANES, depth), 1) - lax.broadcasted_iota(jnp.int32, (LANES, depth), 0)
    box[...] = jnp.where((tap >= 0) & (tap < tlen), 1.0, 0.0).astype(jnp.bfloat16)
    rows[...] = jnp.zeros_like(rows)
    for copy in copies:
        copy.wait()
    for m in range(count):
        rows[m * slots : (m + 1) * slots, :tlen] = taken[m].astype(jnp.float32)
    row = lax.broadcasted_iota(jnp.int32, (LANES, LANES), 0)
    lane = lax.broadcasted_iota(jnp.int32, (LANES, LANES), 1)
    late = lane >= row
    zero = jnp.zeros((LANES, LANES), jnp.float32)
    values = rows[...]
    power = jnp.sum(values * values, axis=1, keepdims=True) / tlen
    factor = 1.0 / (jnp.sqrt(jnp.float32(tlen)) * jnp.sqrt(power + EPS))
    for p in range(pairs):
        m, j = p // slots, p % slots
        table[p : p + 1, :] = jnp.full((1, LANES), entries[j, m])
        table[pairs + p : pairs + p + 1, :] = jnp.full((1, LANES), shifts[j, m])
        weight = factors[j, m].astype(jnp.float32)
        scale[p * groups : (p + 1) * groups, :] = jnp.broadcast_to(factor[p : p + 1] * weight, (groups, LANES))
        before = zero
        for d in range(depth // LANES):
            if d * LANES < tlen:
                part = jnp.broadcast_to(rows[p : p + 1, d * LANES : (d + 1) * LANES], (LANES, LANES))
                now = pltpu.roll(part, 0, axis=1, stride=1, stride_axis=0)
            else:
                now = zero
            bands[p * LANES : (p + 1) * LANES, d * LANES : (d + 1) * LANES] = jnp.where(late, now, before).astype(jnp.bfloat16)
            before = now
    for m in range(count):
        total = jnp.int32(0)
        for j in range(slots):
            total += factors[j, m] * factors[j, m]
        totals[m : m + 1, :] = jnp.full((1, LANES), total.astype(jnp.float32))


def correlate(owners, columns, tlen, high, capacity, count, slots, table, *refs):
    packed, refs = refs[:owners], refs[owners:]
    bands, box, scale, totals = refs[:4]
    outs, (gathered, lanes, taps, squares, stacks, blocks) = refs[4:-6], refs[-6:]
    owner, column = lax.axis_index("tmpl"), lax.axis_index("chan")
    pairs = count * slots
    depth = box.shape[1]
    tall, samples = packed[0].shape
    pieces = samples // LANES
    groups = LAGS // LANES
    reach = groups + depth // LANES - 1
    spot = lax.broadcasted_iota(jnp.int32, (pairs, LANES), 1)
    entry = table[:pairs, :]
    shifts = table[pairs:, :]
    mark = lax.broadcasted_iota(jnp.int32, (tall, LANES), 0) == high + owner
    found = jnp.zeros((pairs, LANES), jnp.float32)
    for k in range(owners):
        local = jnp.sum(jnp.where(mark, packed[k][:, :LANES].astype(jnp.float32), 0.0), axis=0, keepdims=True)
        start = (owner ^ k) * capacity
        found = jnp.where((entry == start + spot) & (spot < capacity), local + float(k * PAD), found)
        gathered[k * PAD : (k + 1) * PAD, :] = packed[k][:PAD, :]
    index = jnp.sum(found, axis=1, keepdims=True).astype(jnp.int32)
    picks = jnp.where(lax.broadcasted_iota(jnp.int32, (pairs, owners * PAD), 1) == index, 1.0, 0.0).astype(jnp.bfloat16)
    picked = jnp.dot(picks, gathered[...], preferred_element_type=jnp.float32)
    for d in range(pieces):
        lanes[d * pairs : (d + 1) * pairs, :] = picked[:, d * LANES : (d + 1) * LANES]
    lanes[pieces * pairs :, :] = jnp.zeros((lanes.shape[0] - pieces * pairs, LANES), jnp.float32)
    lane = lax.broadcasted_iota(jnp.int32, (reach, LANES), 1)
    for p in range(pairs):
        shift = shifts[p, 0]
        rest = shift % LANES
        first = p + (shift // LANES) * pairs
        back = (LANES - rest) % LANES
        low = pltpu.roll(lanes[pl.ds(first, reach, stride=pairs), :], back, axis=1)
        up = pltpu.roll(lanes[pl.ds(first + pairs, reach, stride=pairs), :], back, axis=1)
        stacks[p, :reach, :] = jnp.where(lane < LANES - rest, low, up)
        for d in range(depth // LANES):
            piece = stacks[p, d : d + groups, :]
            taps[p * groups : (p + 1) * groups, d * LANES : (d + 1) * LANES] = piece
            squares[p * groups : (p + 1) * groups, d * LANES : (d + 1) * LANES] = piece * piece
    square = squares[...]
    main = square.astype(jnp.bfloat16)
    left = (square - main.astype(jnp.float32)).astype(jnp.bfloat16)
    energy = lax.dot_general(main, box[...], NT, preferred_element_type=jnp.float32)
    energy += lax.dot_general(left, box[...], NT, preferred_element_type=jnp.float32)
    norm = scale[...] * lax.rsqrt(energy * (1.0 / tlen) + EPS)
    product = lax.dot_general(taps[...].astype(jnp.bfloat16), bands[...], NT, preferred_element_type=jnp.float32)
    for m in range(count):
        partial = jnp.zeros((groups, LANES), jnp.float32)
        for j in range(slots):
            p = m * slots + j
            rows = slice(p * groups, (p + 1) * groups)
            partial += product[rows, p * LANES : (p + 1) * LANES] * norm[rows, :]
        blocks[:, m, :] = partial
        blocks[:, count + m, :] = jnp.broadcast_to(totals[m : m + 1, :], (groups, LANES))
    width = LAGS // columns
    share = LANES // width

    def block(target):
        part = blocks[target // share]
        chosen = part[:, :width]
        for s in range(1, share):
            chosen = jnp.where(target % share == s, part[:, s * width : (s + 1) * width], chosen)
        return chosen

    outs[-1][...] = block(column)
    distance = 1
    for out in outs[:-1]:
        for q in range(out.shape[0]):
            out[q] = block(column ^ (distance * (2 * q + 1)))
        distance *= 2


def shards(waveforms, templates, selection, channel_list, moveouts, weights):
    owners = lax.axis_size("tmpl")
    columns = lax.axis_size("chan")
    count, slots, tlen = templates.shape
    pairs = count * slots
    groups = LAGS // LANES
    width = LAGS // columns
    high, samples = waveforms.shape
    capacity = selection.shape[3]
    depth = -(-(tlen + LANES - 1) // LANES) * LANES
    pieces = samples // LANES

    def call(kernel, name, ins, outs, scratch, arguments, cost=None):
        if ins is HBM:
            arguments = [pltpu.with_memory_space_constraint(x, pltpu.HBM) for x in arguments]
        single = not isinstance(outs, tuple)
        return pl.pallas_call(
            kernel,
            out_shape=outs,
            in_specs=[ins] * len(arguments),
            out_specs=VMEM if single else (VMEM,) * len(outs),
            scratch_shapes=scratch,
            compiler_params=PARAMS,
            cost_estimate=cost,
            name=name,
        )(*arguments)

    bundle = call(
        pack,
        "pack",
        HBM,
        jax.ShapeDtypeStruct((-(-(high + owners) // PAD) * PAD, samples), waveforms.dtype),
        [
            pltpu.VMEM(waveforms.shape, waveforms.dtype),
            pltpu.VMEM(selection.shape, selection.dtype),
            pltpu.SemaphoreType.DMA((2,)),
        ],
        (waveforms, selection),
    )
    packed, reached = [bundle], [0]
    distance = owners // 2
    while distance:
        packed += [exchange(x, "tmpl", distance) for x in packed]
        reached += [k ^ distance for k in reached]
        distance //= 2
    packed = [packed[reached.index(k)] for k in range(owners)]
    bands, box, scale, totals, table = call(
        functools.partial(prepare, tlen),
        "prepare",
        HBM,
        (
            jax.ShapeDtypeStruct((pairs * LANES, depth), jnp.bfloat16),
            jax.ShapeDtypeStruct((LANES, depth), jnp.bfloat16),
            jax.ShapeDtypeStruct((pairs * groups, LANES), jnp.float32),
            jax.ShapeDtypeStruct((count, LANES), jnp.float32),
            jax.ShapeDtypeStruct((2 * pairs, LANES), jnp.int32),
        ),
        [
            pltpu.VMEM((pairs, depth), jnp.float32),
            pltpu.VMEM(templates.shape, templates.dtype),
            pltpu.SMEM((slots, count), jnp.int32),
            pltpu.SMEM((slots, count), jnp.int32),
            pltpu.SMEM((slots, count), jnp.int32),
            pltpu.SemaphoreType.DMA((4,)),
        ],
        (templates, channel_list.T, moveouts.T, weights.T),
        pl.CostEstimate(flops=2_000_000, bytes_accessed=2_000_000, transcendentals=0),
    )
    sizes = []
    while (columns >> len(sizes)) > 1:
        sizes.append(columns >> (len(sizes) + 1))
    shapes = [(s, 2 * count, width) for s in sizes] + [(2 * count, width)]
    parts = call(
        functools.partial(correlate, owners, columns, tlen, high, capacity, count, slots),
        "correlate",
        VMEM,
        tuple(jax.ShapeDtypeStruct(s, jnp.float32) for s in shapes),
        [
            pltpu.VMEM((owners * PAD, samples), jnp.bfloat16),
            pltpu.VMEM(((pieces + 2) * pairs, LANES), jnp.float32),
            pltpu.VMEM((pairs * groups, depth), jnp.float32),
            pltpu.VMEM((pairs * groups, depth), jnp.float32),
            pltpu.VMEM((pairs, PAD, LANES), jnp.float32),
            pltpu.VMEM((groups, 2 * count, LANES), jnp.float32),
        ],
        (table, *packed, bands, box, scale, totals),
    )
    stages, own = list(parts[:-1]), [parts[-1]]
    for i in range(len(stages)):
        arrived = exchange(stages[i], "chan", 1 << i)
        own.append(arrived[0])
        for later in range(i + 1, len(stages)):
            step = 1 << (later - i)
            stages[later] = stages[later] + arrived[step // 2 :: step]
    top = sum(x[:count] for x in own)
    return top / jnp.sqrt(sum(x[count:] for x in own))


def solution(mesh):
    placed = (
        P(("parts", "tmpl", "chan"), None),
        P(("parts", "tmpl"), "chan", None),
        P(("parts", "tmpl"), "chan", None, None),
        P(("parts", "tmpl"), "chan"),
        P(("parts", "tmpl"), "chan"),
        P(("parts", "tmpl"), "chan"),
    )
    return jax.shard_map(
        shards, mesh=mesh, in_specs=placed, out_specs=P(("parts", "tmpl"), "chan"), check_vma=False
    )
```

time: 24.2 us -> 17.5 us (0.72)
  Pallas kernels: 5.58 us -> 3.18 us
  other arithmetic: 2.5 us -> 0.59 us
  starting transfers between devices: 9.3 us -> 8.21 us
  local copies, waits for them, and re-layouts: 0.6 us -> 0 us
  waiting for transfers between devices: 5.89 us -> 5.29 us
    pallas_call x2 -> x3, Pallas kernels: 5.58 us -> 3.18 us  [call(): pl.pallas_call(kernel, out_shape=outs, in_specs=[ins] * len(arguments), o...]
    add x2 -> x1, other arithmetic: 1.36 us -> 0.01 us  [shards(): stages[later] = stages[later] + arrived[step // 2::step]]
    ppermute x9 -> x5, starting transfers between devices: 9.3 us -> 8.21 us  [exchange(): return lax.ppermute(value, axis, [(i, i ^ distance) for i in range(size)])]
    ppermute x9 -> x5, waiting for transfers between devices: 5.89 us -> 5.29 us  [exchange(): return lax.ppermute(value, axis, [(i, i ^ distance) for i in range(size)])]
    unnamed x12 -> x0, local copies, waits for them, and re-layouts: 0.6 us -> none
    another operation x1 -> x0, other arithmetic: 0.56 us -> none  [shards(): jnp.stack([lax.axis_index('tmpl'), lax.axis_index('chan')])]
  transfers between devices with their start and end apart: 9 -> 5, of which waited for: 4 -> 3; matrix products, arithmetic and copies ran while one was open for 5% -> 0% of each run, Pallas kernels for 10% -> 8%
where the time goes in v2:
time: 17.5 us; the launch traced here: 17.3 us
  starting transfers between devices  8.21 us (47%)
  waiting for transfers between devices  5.29 us (30%)
  Pallas kernels  3.18 us (18%)
  other arithmetic  0.59 us (3%)
    ppermute x5, starting transfers between devices, exchange(): return lax.ppermute(value, axis, [(i, i ^ distance) for i in range(size)])  8.21 us
    ppermute x5, waiting for transfers between devices, exchange(): return lax.ppermute(value, axis, [(i, i ^ distance) for i in range(size)])  5.29 us
    pallas_call x3, Pallas kernels, call(): pl.pallas_call(kernel, out_shape=outs, in_specs=[ins] * len(arguments), o...  3.18 us
    div x1, other arithmetic, shards(): return top / jnp.sqrt(sum((x[count:] for x in own)))  0.59 us
  transfers between devices with their start and end apart: 5, of which 3 were waited for; matrix products, arithmetic and copies ran while one was open for 0% of the time, Pallas kernels for 8%

profile of v2, /device:TPU:0, one launch (start us, length us, event | category | flops | bytes accessed | tf_op | source)
XLA Modules:
  0.0 17.3 jit_solution(2016871580074187069)
XLA Ops:
  0.0 0.8 %pack.1.refs_0_ = bf16[16,1536]{1,0:T(8,128)(2,1)S(1)} custom-call(bf16[12,1536]{1,0:T(8,128)(2,1)} %waveforms.1, s32[1,1,4,6]{3,2,1,0:T(4,128)} %selection.1), custom_call_target="tpu_custom_call" | custom-call | tf_op jit(solution)/shard_map/pack/pallas_call | solution.py:175
  0.8 3.0 %collective-permute-start.1 = (bf16[16,1536]{1,0:T(8,128)(2,1)S(1)}, bf16[16,1536]{1,0:T(8,128)(2,1)S(1)}, u32[]{:S(2)}, u32[]{:S(2)}) collective-permute-start(bf16[16,1536]{1,0:T(8,128)(2,1)S(1)} %pack.1.refs_0_), channel_id=1, source_target_pairs={{0,8},{4,12},{8,0},{12,4},{1,9},{5,13},{9,1},{13,5},{2,10},{6,14},... | collective-permute-start | bytes 147464 | tf_op jit(solution)/shard_map/ppermute | solution.py:22
  3.8 0.0 collective-permute-start
  3.8 2.1 %collective-permute-done.1.refs_2_ = bf16[16,1536]{1,0:T(8,128)(2,1)S(1)} collective-permute-done((bf16[16,1536]{1,0:T(8,128)(2,1)S(1)}, bf16[16,1536]{1,0:T(8,128)(2,1)S(1)}, u32[]{:S(2)}, u32[]{:S(2)}) %collective-permute-start.1) | collective-permute-done | bytes 49184 | tf_op jit(solution)/shard_map/ppermute | solution.py:22
  5.9 0.0 collective-permute-start.2
  5.9 1.3 %prepare.1 = (bf16[1024,768]{1,0:T(8,128)(2,1)S(1)}, bf16[128,768]{1,0:T(8,128)(2,1)S(1)}, f32[32,128]{1,0:T(8,128)S(1)}, f32[4,128]{1,0:T(4,128)S(1)}, s32[16,128]{1,0:T(8,128)S(1)}) custom-call(bf16[4,2,600]{2,1,0:T(2,128)(2,1)} %templates.1, s32[2,4]{1,0:T(2,128)} %bitcast.25, s32[2,4]{1,0:T(2,128)} %bitcast.26, s32[2,4]{1,0:T(2,128)} %bitcast.27), custom_call_target="tpu_custom_call" | custom-call | flops 2000000 | bytes 2000000 | tf_op jit(solution)/shard_map/prepare/pallas_call | solution.py:175
  7.2 0.0 collective-permute-done.refs_1_
  7.3 0.0 collective-permute-done.2.refs_3_
  7.3 1.0 %correlate.1 = (f32[2,8,128]{2,1,0:T(8,128)S(1)}, f32[1,8,128]{2,1,0:T(8,128)S(1)}, f32[8,128]{1,0:T(8,128)S(1)}) custom-call(s32[16,128]{1,0:T(8,128)S(1)} %get-tuple-element.13.table, bf16[16,1536]{1,0:T(8,128)(2,1)S(1)} %pack.1.refs_0_, bf16[16,1536]{1,0:T(8,128)(2,1)S(1)} %collective-permute-done.refs_1_, ...), custom_call_target="tpu_custom_call" | custom-call | tf_op jit(solution)/shard_map/correlate/pallas_call | solution.py:175
  8.3 2.2 %collective-permute-start.3 = (f32[2,8,128]{2,1,0:T(8,128)S(1)}, f32[2,8,128]{2,1,0:T(8,128)S(1)}, u32[]{:S(2)}, u32[]{:S(2)}) collective-permute-start(f32[2,8,128]{2,1,0:T(8,128)S(1)} %get-tuple-element.19), channel_id=1, source_target_pairs={{0,1},{1,0},{2,3},{3,2},{4,5},{5,4},{6,7},{7,6},{8,9},{9,8},{10,11... | collective-permute-start | bytes 24584 | tf_op jit(solution)/shard_map/ppermute | solution.py:22
  10.5 1.6 %collective-permute-done.3 = f32[2,8,128]{2,1,0:T(8,128)S(1)} collective-permute-done((f32[2,8,128]{2,1,0:T(8,128)S(1)}, f32[2,8,128]{2,1,0:T(8,128)S(1)}, u32[]{:S(2)}, u32[]{:S(2)}) %collective-permute-start.3) | collective-permute-done | bytes 8224 | tf_op jit(solution)/shard_map/ppermute | solution.py:22
  12.1 3.0 %collective-permute-start.4 = (f32[1,8,128]{2,1,0:T(8,128)S(1)}, f32[1,8,128]{2,1,0:T(8,128)S(1)}, u32[]{:S(2)}, u32[]{:S(2)}) collective-permute-start(f32[1,8,128]{2,1,0:T(8,128)S(1)} %slice_add_fusion), channel_id=1, source_target_pairs={{0,2},{1,3},{2,0},{3,1},{4,6},{5,7},{6,4},{7,5},{8,10},{9,11},{10,... | collective-permute-start | bytes 12296 | tf_op jit(solution)/shard_map/ppermute | solution.py:22
  15.1 1.6 %collective-permute-done.4 = f32[1,8,128]{2,1,0:T(8,128)S(1)} collective-permute-done((f32[1,8,128]{2,1,0:T(8,128)S(1)}, f32[1,8,128]{2,1,0:T(8,128)S(1)}, u32[]{:S(2)}, u32[]{:S(2)}) %collective-permute-start.4) | collective-permute-done | bytes 4128 | tf_op jit(solution)/shard_map/ppermute | solution.py:22
  16.7 0.6 %fusion.3 = f32[4,128]{1,0:T(4,128)} fusion(f32[2,8,128]{2,1,0:T(8,128)S(1)} %collective-permute-done.3, f32[1,8,128]{2,1,0:T(8,128)S(1)} %collective-permute-done.4, f32[8,128]{1,0:T(8,128)S(1)} %get-tuple-element.18), kind=kLoop, calls=%fused_computation.5 | loop fusion | flops 2560 | bytes 14336 | tf_op jit(solution)/shard_map/div | solution.py:254
  (1 shorter events, 0.0 us)
Async XLA Ops:
  0.8 5.1 %collective-permute-start.1 = (bf16[16,1536]{1,0:T(8,128)(2,1)S(1)}, bf16[16,1536]{1,0:T(8,128)(2,1)S(1)}, u32[]{:S(2)}, u32[]{:S(2)}) collective-permute-start(bf16[16,1536]{1,0:T(8,128)(2,1)S(1)} %pack.1.refs_0_), channel_id=1, source_target_pairs={{0,8},{4,12},{8,0},{12,4},{1,9},{5,13},{9,1},{13,5},{2,10},{6,14},... | collective-permute-start | bytes 147464 | tf_op jit(solution)/shard_map/ppermute | solution.py:22
  3.8 3.4 %collective-permute-start = (bf16[16,1536]{1,0:T(8,128)(2,1)S(1)}, bf16[16,1536]{1,0:T(8,128)(2,1)S(1)}, u32[]{:S(2)}, u32[]{:S(2)}) collective-permute-start(bf16[16,1536]{1,0:T(8,128)(2,1)S(1)} %pack.1.refs_0_), channel_id=1, source_target_pairs={{0,4},{4,0},{8,12},{12,8},{1,5},{5,1},{9,13},{13,9},{2,6},{6,2},{1... | collective-permute-start | bytes 147464 | tf_op jit(solution)/shard_map/ppermute | solution.py:22
  5.9 1.4 %collective-permute-start.2 = (bf16[16,1536]{1,0:T(8,128)(2,1)S(1)}, bf16[16,1536]{1,0:T(8,128)(2,1)S(1)}, u32[]{:S(2)}, u32[]{:S(2)}) collective-permute-start(bf16[16,1536]{1,0:T(8,128)(2,1)S(1)} %collective-permute-done.1.refs_2_), channel_id=1, source_target_pairs={{0,4},{4,0},{8,12},{12,8},{1,5},{5,1},{9,13},{13,9},{2,6},{6,2},{1... | collective-permute-start | bytes 147464 | tf_op jit(solution)/shard_map/ppermute | solution.py:22
  8.3 3.8 %collective-permute-start.3 = (f32[2,8,128]{2,1,0:T(8,128)S(1)}, f32[2,8,128]{2,1,0:T(8,128)S(1)}, u32[]{:S(2)}, u32[]{:S(2)}) collective-permute-start(f32[2,8,128]{2,1,0:T(8,128)S(1)} %get-tuple-element.19), channel_id=1, source_target_pairs={{0,1},{1,0},{2,3},{3,2},{4,5},{5,4},{6,7},{7,6},{8,9},{9,8},{10,11... | collective-permute-start | bytes 24584 | tf_op jit(solution)/shard_map/ppermute | solution.py:22
  12.1 4.6 %collective-permute-start.4 = (f32[1,8,128]{2,1,0:T(8,128)S(1)}, f32[1,8,128]{2,1,0:T(8,128)S(1)}, u32[]{:S(2)}, u32[]{:S(2)}) collective-permute-start(f32[1,8,128]{2,1,0:T(8,128)S(1)} %slice_add_fusion), channel_id=1, source_target_pairs={{0,2},{1,3},{2,0},{3,1},{4,6},{5,7},{6,4},{7,5},{8,10},{9,11},{10,... | collective-permute-start | bytes 12296 | tf_op jit(solution)/shard_map/ppermute | solution.py:22

commit v3 on v2

--- a/solution.py
+++ b/solution.py
@@ -12,7 +12,7 @@
 LANES = 128
 PAD = 16
 PARAMS = pltpu.CompilerParams(vmem_limit_bytes=8 * 1024 * 1024)
-NT = (((1,), (1,)), ((), ()))
+STEP = 64
 VMEM = pl.BlockSpec(memory_space=pltpu.VMEM)
 HBM = pl.BlockSpec(memory_space=pltpu.HBM)
 
@@ -45,9 +45,9 @@
     copies = fetch((templates, lists, moveouts, weights), (taken, entries, shifts, factors), sems)
     count, slots, _ = taken.shape
     pairs = count * slots
-    depth = box.shape[1]
-    groups = LAGS // LANES
-    tap = lax.broadcasted_iota(jnp.int32, (LANES, depth), 1) - lax.broadcasted_iota(jnp.int32, (LANES, depth), 0)
+    depth = box.shape[0]
+    groups = LAGS // STEP
+    tap = lax.broadcasted_iota(jnp.int32, (depth, LANES), 0) - lax.broadcasted_iota(jnp.int32, (depth, LANES), 1) % STEP
     box[...] = jnp.where((tap >= 0) & (tap < tlen), 1.0, 0.0).astype(jnp.bfloat16)
     rows[...] = jnp.zeros_like(rows)
     for copy in copies:
@@ -56,7 +56,9 @@
         rows[m * slots : (m + 1) * slots, :tlen] = taken[m].astype(jnp.float32)
     row = lax.broadcasted_iota(jnp.int32, (LANES, LANES), 0)
     lane = lax.broadcasted_iota(jnp.int32, (LANES, LANES), 1)
-    late = lane >= row
+    late = row >= lane % STEP
+    front = lane < STEP
+    mirror = jnp.where(row + lane == LANES - 1, 1.0, 0.0).astype(jnp.bfloat16)
     zero = jnp.zeros((LANES, LANES), jnp.float32)
     values = rows[...]
     power = jnp.sum(values * values, axis=1, keepdims=True) / tlen
@@ -67,16 +69,23 @@
         table[pairs + p : pairs + p + 1, :] = jnp.full((1, LANES), shifts[j, m])
         weight = factors[j, m].astype(jnp.float32)
         scale[p * groups : (p + 1) * groups, :] = jnp.broadcast_to(factor[p : p + 1] * weight, (groups, LANES))
+    turned = [
+        jnp.dot(values[:, d * LANES : (d + 1) * LANES].astype(jnp.bfloat16), mirror, preferred_element_type=jnp.float32)
+        for d in range(-(-tlen // LANES))
+    ]
+    for m in range(count):
         before = zero
         for d in range(depth // LANES):
+            now = zero
             if d * LANES < tlen:
-                part = jnp.broadcast_to(rows[p : p + 1, d * LANES : (d + 1) * LANES], (LANES, LANES))
-                now = pltpu.roll(part, 0, axis=1, stride=1, stride_axis=0)
-            else:
-                now = zero
-            bands[p * LANES : (p + 1) * LANES, d * LANES : (d + 1) * LANES] = jnp.where(late, now, before).astype(jnp.bfloat16)
+                back = turned[d][m * slots : (m + 1) * slots, :]
+                now, other = (
+                    pltpu.roll(jnp.broadcast_to(back[j : j + 1], (LANES, LANES)), 1 + j * STEP, axis=1, stride=1, stride_axis=0)
+                    for j in range(slots)
+                )
+                now = jnp.where(front, now, other)
+            bands[d * LANES : (d + 1) * LANES, m * LANES : (m + 1) * LANES] = jnp.where(late, now, before).astype(jnp.bfloat16)
             before = now
-    for m in range(count):
         total = jnp.int32(0)
         for j in range(slots):
             total += factors[j, m] * factors[j, m]
@@ -86,14 +95,15 @@
 def correlate(owners, columns, tlen, high, capacity, count, slots, table, *refs):
     packed, refs = refs[:owners], refs[owners:]
     bands, box, scale, totals = refs[:4]
-    outs, (gathered, lanes, taps, squares, stacks, blocks) = refs[4:-6], refs[-6:]
+    outs, (gathered, lanes, taps, squares, stacks, sums, blocks) = refs[4:-7], refs[-7:]
     owner, column = lax.axis_index("tmpl"), lax.axis_index("chan")
     pairs = count * slots
-    depth = box.shape[1]
+    depth = box.shape[0]
     tall, samples = packed[0].shape
     pieces = samples // LANES
-    groups = LAGS // LANES
-    reach = groups + depth // LANES - 1
+    groups = LAGS // STEP
+    turns = LANES // STEP
+    reach = LAGS // LANES + depth // LANES - 1
     spot = lax.broadcasted_iota(jnp.int32, (pairs, LANES), 1)
     entry = table[:pairs, :]
     shifts = table[pairs:, :]
@@ -112,32 +122,34 @@
     lanes[pieces * pairs :, :] = jnp.zeros((lanes.shape[0] - pieces * pairs, LANES), jnp.float32)
     lane = lax.broadcasted_iota(jnp.int32, (reach, LANES), 1)
     for p in range(pairs):
-        shift = shifts[p, 0]
-        rest = shift % LANES
-        first = p + (shift // LANES) * pairs
-        back = (LANES - rest) % LANES
-        low = pltpu.roll(lanes[pl.ds(first, reach, stride=pairs), :], back, axis=1)
-        up = pltpu.roll(lanes[pl.ds(first + pairs, reach, stride=pairs), :], back, axis=1)
-        stacks[p, :reach, :] = jnp.where(lane < LANES - rest, low, up)
+        for h in range(turns):
+            shift = shifts[p, 0] + h * STEP
+            rest = shift % LANES
+            first = p + (shift // LANES) * pairs
+            back = (LANES - rest) % LANES
+            low = pltpu.roll(lanes[pl.ds(first, reach, stride=pairs), :], back, axis=1)
+            up = pltpu.roll(lanes[pl.ds(first + pairs, reach, stride=pairs), :], back, axis=1)
+            stacks[p, pl.ds(h, reach, stride=turns), :] = jnp.where(lane < LANES - rest, low, up)
         for d in range(depth // LANES):
-            piece = stacks[p, d : d + groups, :]
+            piece = stacks[p, d * turns : d * turns + groups, :]
             taps[p * groups : (p + 1) * groups, d * LANES : (d + 1) * LANES] = piece
             squares[p * groups : (p + 1) * groups, d * LANES : (d + 1) * LANES] = piece * piece
     square = squares[...]
     main = square.astype(jnp.bfloat16)
     left = (square - main.astype(jnp.float32)).astype(jnp.bfloat16)
-    energy = lax.dot_general(main, box[...], NT, preferred_element_type=jnp.float32)
-    energy += lax.dot_general(left, box[...], NT, preferred_element_type=jnp.float32)
+    energy = jnp.dot(main, box[...], preferred_element_type=jnp.float32)
+    energy += jnp.dot(left, box[...], preferred_element_type=jnp.float32)
     norm = scale[...] * lax.rsqrt(energy * (1.0 / tlen) + EPS)
-    product = lax.dot_general(taps[...].astype(jnp.bfloat16), bands[...], NT, preferred_element_type=jnp.float32)
+    product = jnp.dot(taps[...].astype(jnp.bfloat16), bands[...], preferred_element_type=jnp.float32)
+    front = lax.broadcasted_iota(jnp.int32, (LAGS // LANES, LANES), 1) < STEP
     for m in range(count):
-        partial = jnp.zeros((groups, LANES), jnp.float32)
-        for j in range(slots):
-            p = m * slots + j
-            rows = slice(p * groups, (p + 1) * groups)
-            partial += product[rows, p * LANES : (p + 1) * LANES] * norm[rows, :]
-        blocks[:, m, :] = partial
-        blocks[:, count + m, :] = jnp.broadcast_to(totals[m : m + 1, :], (groups, LANES))
+        first, second = (slice((m * slots + j) * groups, (m * slots + j + 1) * groups) for j in range(slots))
+        place = slice(m * LANES, (m + 1) * LANES)
+        sums[m] = product[first, place] * norm[first, :] + pltpu.roll(product[second, place] * norm[second, :], STEP, axis=1)
+        even = sums[m, pl.ds(0, LAGS // LANES, stride=turns), :]
+        odd = sums[m, pl.ds(1, LAGS // LANES, stride=turns), :]
+        blocks[:, m, :] = jnp.where(front, even, pltpu.roll(odd, STEP, axis=1))
+        blocks[:, count + m, :] = jnp.broadcast_to(totals[m : m + 1, :], (LAGS // LANES, LANES))
     width = LAGS // columns
     share = LANES // width
 
@@ -161,11 +173,11 @@
     columns = lax.axis_size("chan")
     count, slots, tlen = templates.shape
     pairs = count * slots
-    groups = LAGS // LANES
+    groups = LAGS // STEP
     width = LAGS // columns
     high, samples = waveforms.shape
     capacity = selection.shape[3]
-    depth = -(-(tlen + LANES - 1) // LANES) * LANES
+    depth = -(-(tlen + STEP - 1) // LANES) * LANES
     pieces = samples // LANES
 
     def call(kernel, name, ins, outs, scratch, arguments, cost=None):
@@ -195,20 +207,13 @@
         ],
         (waveforms, selection),
     )
-    packed, reached = [bundle], [0]
-    distance = owners // 2
-    while distance:
-        packed += [exchange(x, "tmpl", distance) for x in packed]
-        reached += [k ^ distance for k in reached]
-        distance //= 2
-    packed = [packed[reached.index(k)] for k in range(owners)]
     bands, box, scale, totals, table = call(
         functools.partial(prepare, tlen),
         "prepare",
         HBM,
         (
-            jax.ShapeDtypeStruct((pairs * LANES, depth), jnp.bfloat16),
-            jax.ShapeDtypeStruct((LANES, depth), jnp.bfloat16),
+            jax.ShapeDtypeStruct((depth, pairs * STEP), jnp.bfloat16),
+            jax.ShapeDtypeStruct((depth, LANES), jnp.bfloat16),
             jax.ShapeDtypeStruct((pairs * groups, LANES), jnp.float32),
             jax.ShapeDtypeStruct((count, LANES), jnp.float32),
             jax.ShapeDtypeStruct((2 * pairs, LANES), jnp.int32),
@@ -224,6 +229,15 @@
         (templates, channel_list.T, moveouts.T, weights.T),
         pl.CostEstimate(flops=2_000_000, bytes_accessed=2_000_000, transcendentals=0),
     )
+    packed, reached = [bundle], [0]
+    distance = owners // 2
+    while distance:
+        packed += [exchange(x, "tmpl", distance) for x in packed]
+        if distance == owners // 2:
+            packed[1], table = lax.optimization_barrier((packed[1], table))
+        reached += [k ^ distance for k in reached]
+        distance //= 2
+    packed = [packed[reached.index(k)] for k in range(owners)]
     sizes = []
     while (columns >> len(sizes)) > 1:
         sizes.append(columns >> (len(sizes) + 1))
@@ -238,8 +252,9 @@
             pltpu.VMEM(((pieces + 2) * pairs, LANES), jnp.float32),
             pltpu.VMEM((pairs * groups, depth), jnp.float32),
             pltpu.VMEM((pairs * groups, depth), jnp.float32),
-            pltpu.VMEM((pairs, PAD, LANES), jnp.float32),
-            pltpu.VMEM((groups, 2 * count, LANES), jnp.float32),
+            pltpu.VMEM((pairs, 2 * PAD, LANES), jnp.float32),
+            pltpu.VMEM((count, groups, LANES), jnp.float32),
+            pltpu.VMEM((LAGS // LANES, 2 * count, LANES), jnp.float32),
         ],
         (table, *packed, bands, box, scale, totals),
     )

time: 17.5 us -> 17.2 us (0.983)
  waiting for transfers between devices: 5.29 us -> 5.06 us
    ppermute x5, waiting for transfers between devices: 5.29 us -> 5.06 us  [exchange(): return lax.ppermute(value, axis, [(i, i ^ distance) for i in range(size)])]
  transfers between devices with their start and end apart: 5 -> 5, of which waited for: 3 -> 4; matrix products, arithmetic and copies ran while one was open for 0% -> 0% of each run, Pallas kernels for 8% -> 8%
where the time goes in v3:
time: 17.2 us; the launch traced here: 17 us
  starting transfers between devices  8.21 us (48%)
  waiting for transfers between devices  5.06 us (29%)
  Pallas kernels  3.1 us (18%)
  other arithmetic  0.59 us (3%)
    ppermute x5, starting transfers between devices, exchange(): return lax.ppermute(value, axis, [(i, i ^ distance) for i in range(size)])  8.21 us
    ppermute x5, waiting for transfers between devices, exchange(): return lax.ppermute(value, axis, [(i, i ^ distance) for i in range(size)])  5.06 us
    pallas_call x3, Pallas kernels, call(): pl.pallas_call(kernel, out_shape=outs, in_specs=[ins] * len(arguments), o...  3.1 us
    div x1, other arithmetic, shards(): return top / jnp.sqrt(sum((x[count:] for x in own)))  0.59 us
  transfers between devices with their start and end apart: 5, of which 4 were waited for; matrix products, arithmetic and copies ran while one was open for 0% of the time, Pallas kernels for 8%

profile of v3, /device:TPU:0, one launch (start us, length us, event | category | flops | bytes accessed | tf_op | source)
XLA Modules:
  0.0 17.0 jit_solution(15262498362149912166)
XLA Ops:
  0.0 0.8 %pack.1.refs_0_ = bf16[16,1536]{1,0:T(8,128)(2,1)S(1)} custom-call(bf16[12,1536]{1,0:T(8,128)(2,1)} %waveforms.1, s32[1,1,4,6]{3,2,1,0:T(4,128)} %selection.1), custom_call_target="tpu_custom_call" | custom-call | tf_op jit(solution)/shard_map/pack/pallas_call | solution.py:187
  0.8 3.0 %collective-permute-start = (bf16[16,1536]{1,0:T(8,128)(2,1)S(1)}, bf16[16,1536]{1,0:T(8,128)(2,1)S(1)}, u32[]{:S(2)}, u32[]{:S(2)}) collective-permute-start(bf16[16,1536]{1,0:T(8,128)(2,1)S(1)} %pack.1.refs_0_), channel_id=1, source_target_pairs={{0,8},{4,12},{8,0},{12,4},{1,9},{5,13},{9,1},{13,5},{2,10},{6,14},... | collective-permute-start | bytes 147464 | tf_op jit(solution)/shard_map/ppermute | solution.py:22
  3.8 0.0 collective-permute-start.1
  3.8 1.4 %prepare.1 = (bf16[768,512]{1,0:T(8,128)(2,1)S(1)}, bf16[768,128]{1,0:T(8,128)(2,1)S(1)}, f32[64,128]{1,0:T(8,128)S(1)}, f32[4,128]{1,0:T(4,128)S(1)}, s32[16,128]{1,0:T(8,128)S(1)}) custom-call(bf16[4,2,600]{2,1,0:T(2,128)(2,1)} %templates.1, s32[2,4]{1,0:T(2,128)} %bitcast.25, s32[2,4]{1,0:T(2,128)} %bitcast.26, s32[2,4]{1,0:T(2,128)} %bitcast.27), custom_call_target="tpu_custom_call" | custom-call | flops 2000000 | bytes 2000000 | tf_op jit(solution)/shard_map/prepare/pallas_call | solution.py:187
  5.3 0.6 %collective-permute-done.refs_2_ = bf16[16,1536]{1,0:T(8,128)(2,1)S(1)} collective-permute-done((bf16[16,1536]{1,0:T(8,128)(2,1)S(1)}, bf16[16,1536]{1,0:T(8,128)(2,1)S(1)}, u32[]{:S(2)}, u32[]{:S(2)}) %collective-permute-start) | collective-permute-done | bytes 49184 | tf_op jit(solution)/shard_map/ppermute | solution.py:22
  5.9 0.0 collective-permute-start.2
  5.9 0.0 collective-permute-done.1.refs_1_
  5.9 1.2 %collective-permute-done.2.refs_3_ = bf16[16,1536]{1,0:T(8,128)(2,1)S(1)} collective-permute-done((bf16[16,1536]{1,0:T(8,128)(2,1)S(1)}, bf16[16,1536]{1,0:T(8,128)(2,1)S(1)}, u32[]{:S(2)}, u32[]{:S(2)}) %collective-permute-start.2) | collective-permute-done | bytes 49184 | tf_op jit(solution)/shard_map/ppermute | solution.py:22
  7.1 0.8 %correlate.1 = (f32[2,8,128]{2,1,0:T(8,128)S(1)}, f32[1,8,128]{2,1,0:T(8,128)S(1)}, f32[8,128]{1,0:T(8,128)S(1)}) custom-call(s32[16,128]{1,0:T(8,128)S(1)} %get-tuple-element.16.table, bf16[16,1536]{1,0:T(8,128)(2,1)S(1)} %pack.1.refs_0_, bf16[16,1536]{1,0:T(8,128)(2,1)S(1)} %collective-permute-done.1.refs_1_, ...), custom_call_target="tpu_custom_call" | custom-call | tf_op jit(solution)/shard_map/correlate/pallas_call | solution.py:187
  8.0 2.2 %collective-permute-start.3 = (f32[2,8,128]{2,1,0:T(8,128)S(1)}, f32[2,8,128]{2,1,0:T(8,128)S(1)}, u32[]{:S(2)}, u32[]{:S(2)}) collective-permute-start(f32[2,8,128]{2,1,0:T(8,128)S(1)} %get-tuple-element.23), channel_id=1, source_target_pairs={{0,1},{1,0},{2,3},{3,2},{4,5},{5,4},{6,7},{7,6},{8,9},{9,8},{10,11... | collective-permute-start | bytes 24584 | tf_op jit(solution)/shard_map/ppermute | solution.py:22
  10.1 1.6 %collective-permute-done.3 = f32[2,8,128]{2,1,0:T(8,128)S(1)} collective-permute-done((f32[2,8,128]{2,1,0:T(8,128)S(1)}, f32[2,8,128]{2,1,0:T(8,128)S(1)}, u32[]{:S(2)}, u32[]{:S(2)}) %collective-permute-start.3) | collective-permute-done | bytes 8224 | tf_op jit(solution)/shard_map/ppermute | solution.py:22
  11.8 3.0 %collective-permute-start.4 = (f32[1,8,128]{2,1,0:T(8,128)S(1)}, f32[1,8,128]{2,1,0:T(8,128)S(1)}, u32[]{:S(2)}, u32[]{:S(2)}) collective-permute-start(f32[1,8,128]{2,1,0:T(8,128)S(1)} %slice_add_fusion), channel_id=1, source_target_pairs={{0,2},{1,3},{2,0},{3,1},{4,6},{5,7},{6,4},{7,5},{8,10},{9,11},{10,... | collective-permute-start | bytes 12296 | tf_op jit(solution)/shard_map/ppermute | solution.py:22
  14.8 1.6 %collective-permute-done.4 = f32[1,8,128]{2,1,0:T(8,128)S(1)} collective-permute-done((f32[1,8,128]{2,1,0:T(8,128)S(1)}, f32[1,8,128]{2,1,0:T(8,128)S(1)}, u32[]{:S(2)}, u32[]{:S(2)}) %collective-permute-start.4) | collective-permute-done | bytes 4128 | tf_op jit(solution)/shard_map/ppermute | solution.py:22
  16.4 0.6 %fusion.3 = f32[4,128]{1,0:T(4,128)} fusion(f32[2,8,128]{2,1,0:T(8,128)S(1)} %collective-permute-done.3, f32[1,8,128]{2,1,0:T(8,128)S(1)} %collective-permute-done.4, f32[8,128]{1,0:T(8,128)S(1)} %get-tuple-element.22), kind=kLoop, calls=%fused_computation.5 | loop fusion | flops 2560 | bytes 14336 | tf_op jit(solution)/shard_map/div | solution.py:269
  (1 shorter events, 0.0 us)
Async XLA Ops:
  0.8 5.1 %collective-permute-start = (bf16[16,1536]{1,0:T(8,128)(2,1)S(1)}, bf16[16,1536]{1,0:T(8,128)(2,1)S(1)}, u32[]{:S(2)}, u32[]{:S(2)}) collective-permute-start(bf16[16,1536]{1,0:T(8,128)(2,1)S(1)} %pack.1.refs_0_), channel_id=1, source_target_pairs={{0,8},{4,12},{8,0},{12,4},{1,9},{5,13},{9,1},{13,5},{2,10},{6,14},... | collective-permute-start | bytes 147464 | tf_op jit(solution)/shard_map/ppermute | solution.py:22
  3.8 2.1 %collective-permute-start.1 = (bf16[16,1536]{1,0:T(8,128)(2,1)S(1)}, bf16[16,1536]{1,0:T(8,128)(2,1)S(1)}, u32[]{:S(2)}, u32[]{:S(2)}) collective-permute-start(bf16[16,1536]{1,0:T(8,128)(2,1)S(1)} %pack.1.refs_0_), channel_id=1, source_target_pairs={{0,4},{4,0},{8,12},{12,8},{1,5},{5,1},{9,13},{13,9},{2,6},{6,2},{1... | collective-permute-start | bytes 147464 | tf_op jit(solution)/shard_map/ppermute | solution.py:22
  5.9 1.2 %collective-permute-start.2 = (bf16[16,1536]{1,0:T(8,128)(2,1)S(1)}, bf16[16,1536]{1,0:T(8,128)(2,1)S(1)}, u32[]{:S(2)}, u32[]{:S(2)}) collective-permute-start(bf16[16,1536]{1,0:T(8,128)(2,1)S(1)} %collective-permute-done.refs_2_), channel_id=1, source_target_pairs={{0,4},{4,0},{8,12},{12,8},{1,5},{5,1},{9,13},{13,9},{2,6},{6,2},{1... | collective-permute-start | bytes 147464 | tf_op jit(solution)/shard_map/ppermute | solution.py:22
  8.0 3.8 %collective-permute-start.3 = (f32[2,8,128]{2,1,0:T(8,128)S(1)}, f32[2,8,128]{2,1,0:T(8,128)S(1)}, u32[]{:S(2)}, u32[]{:S(2)}) collective-permute-start(f32[2,8,128]{2,1,0:T(8,128)S(1)} %get-tuple-element.23), channel_id=1, source_target_pairs={{0,1},{1,0},{2,3},{3,2},{4,5},{5,4},{6,7},{7,6},{8,9},{9,8},{10,11... | collective-permute-start | bytes 24584 | tf_op jit(solution)/shard_map/ppermute | solution.py:22
  11.8 4.6 %collective-permute-start.4 = (f32[1,8,128]{2,1,0:T(8,128)S(1)}, f32[1,8,128]{2,1,0:T(8,128)S(1)}, u32[]{:S(2)}, u32[]{:S(2)}) collective-permute-start(f32[1,8,128]{2,1,0:T(8,128)S(1)} %slice_add_fusion), channel_id=1, source_target_pairs={{0,2},{1,3},{2,0},{3,1},{4,6},{5,7},{6,4},{7,5},{8,10},{9,11},{10,... | collective-permute-start | bytes 12296 | tf_op jit(solution)/shard_map/ppermute | solution.py:22

commit v4 on v3

--- a/solution.py
+++ b/solution.py
@@ -13,6 +13,7 @@
 PAD = 16
 PARAMS = pltpu.CompilerParams(vmem_limit_bytes=8 * 1024 * 1024)
 STEP = 64
+ROUTES = {4: ((2, 3, 1, 0), (3, 2, 0, 1), (1, 0, 3, 2))}
 VMEM = pl.BlockSpec(memory_space=pltpu.VMEM)
 HBM = pl.BlockSpec(memory_space=pltpu.HBM)
 
@@ -161,6 +162,13 @@
         return chosen
 
     outs[-1][...] = block(column)
+    if columns in ROUTES:
+        for out, route in zip(outs, ROUTES[columns]):
+            target = jnp.int32(route[0])
+            for i in range(1, columns):
+                target = jnp.where(column == i, route[i], target)
+            out[...] = block(target)
+        return
     distance = 1
     for out in outs[:-1]:
         for q in range(out.shape[0]):
@@ -242,6 +250,8 @@
     while (columns >> len(sizes)) > 1:
         sizes.append(columns >> (len(sizes) + 1))
     shapes = [(s, 2 * count, width) for s in sizes] + [(2 * count, width)]
+    if columns in ROUTES:
+        shapes = [(2 * count, width)] * columns
     parts = call(
         functools.partial(correlate, owners, columns, tlen, high, capacity, count, slots),
         "correlate",
@@ -259,6 +269,10 @@
         (table, *packed, bands, box, scale, totals),
     )
     stages, own = list(parts[:-1]), [parts[-1]]
+    if columns in ROUTES:
+        for part, route in zip(stages, ROUTES[columns]):
+            own.append(lax.ppermute(part, "chan", list(enumerate(route))))
+        stages = []
     for i in range(len(stages)):
         arrived = exchange(stages[i], "chan", 1 << i)
         own.append(arrived[0])

time: 17.2 us -> 16.6 us (0.965)
  starting transfers between devices: 8.21 us -> 7.76 us
    ppermute x5 -> x3, starting transfers between devices: 8.21 us -> 3.01 us  [exchange(): return lax.ppermute(value, axis, [(i, i ^ distance) for i in range(size)])]
    ppermute x0 -> x3, starting transfers between devices: none -> 4.75 us  [shards(): own.append(lax.ppermute(part, 'chan', list(enumerate(route))))]
    ppermute x5 -> x3, waiting for transfers between devices: 5.06 us -> 1.84 us  [exchange(): return lax.ppermute(value, axis, [(i, i ^ distance) for i in range(size)])]
    ppermute x0 -> x3, waiting for transfers between devices: none -> 3.1 us  [shards(): own.append(lax.ppermute(part, 'chan', list(enumerate(route))))]
  transfers between devices with their start and end apart: 5 -> 6, of which waited for: 4 -> 5; matrix products, arithmetic and copies ran while one was open for 0% -> 0% of each run, Pallas kernels for 8% -> 9%
where the time goes in v4:
time: 16.6 us; the launch traced here: 16.4 us
  starting transfers between devices  7.76 us (47%)
  waiting for transfers between devices  4.95 us (30%)
  Pallas kernels  3.1 us (19%)
  other arithmetic  0.59 us (4%)
    ppermute x3, starting transfers between devices, shards(): own.append(lax.ppermute(part, 'chan', list(enumerate(route))))  4.75 us
    ppermute x3, waiting for transfers between devices, shards(): own.append(lax.ppermute(part, 'chan', list(enumerate(route))))  3.1 us
    pallas_call x3, Pallas kernels, call(): pl.pallas_call(kernel, out_shape=outs, in_specs=[ins] * len(arguments), o...  3.1 us
    ppermute x3, starting transfers between devices, exchange(): return lax.ppermute(value, axis, [(i, i ^ distance) for i in range(size)])  3.01 us
    ppermute x3, waiting for transfers between devices, exchange(): return lax.ppermute(value, axis, [(i, i ^ distance) for i in range(size)])  1.84 us
    div x1, other arithmetic, shards(): return top / jnp.sqrt(sum((x[count:] for x in own)))  0.59 us
  transfers between devices with their start and end apart: 6, of which 5 were waited for; matrix products, arithmetic and copies ran while one was open for 0% of the time, Pallas kernels for 9%

profile of v4, /device:TPU:0, one launch (start us, length us, event | category | flops | bytes accessed | tf_op | source)
XLA Modules:
  0.0 16.4 jit_solution(11218804049081052967)
XLA Ops:
  0.0 0.8 %pack.1.refs_0_ = bf16[16,1536]{1,0:T(8,128)(2,1)S(1)} custom-call(bf16[12,1536]{1,0:T(8,128)(2,1)} %waveforms.1, s32[1,1,4,6]{3,2,1,0:T(4,128)} %selection.1), custom_call_target="tpu_custom_call" | custom-call | tf_op jit(solution)/shard_map/pack/pallas_call | solution.py:195
  0.8 3.0 %collective-permute-start = (bf16[16,1536]{1,0:T(8,128)(2,1)S(1)}, bf16[16,1536]{1,0:T(8,128)(2,1)S(1)}, u32[]{:S(2)}, u32[]{:S(2)}) collective-permute-start(bf16[16,1536]{1,0:T(8,128)(2,1)S(1)} %pack.1.refs_0_), channel_id=1, source_target_pairs={{0,8},{4,12},{8,0},{12,4},{1,9},{5,13},{9,1},{13,5},{2,10},{6,14},... | collective-permute-start | bytes 147464 | tf_op jit(solution)/shard_map/ppermute | solution.py:23
  3.8 0.0 collective-permute-start.1
  3.8 1.4 %prepare.1 = (bf16[768,512]{1,0:T(8,128)(2,1)S(1)}, bf16[768,128]{1,0:T(8,128)(2,1)S(1)}, f32[64,128]{1,0:T(8,128)S(1)}, f32[4,128]{1,0:T(4,128)S(1)}, s32[16,128]{1,0:T(8,128)S(1)}) custom-call(bf16[4,2,600]{2,1,0:T(2,128)(2,1)} %templates.1, s32[2,4]{1,0:T(2,128)} %bitcast.3, s32[2,4]{1,0:T(2,128)} %bitcast.4, s32[2,4]{1,0:T(2,128)} %bitcast.5), custom_call_target="tpu_custom_call" | custom-call | flops 2000000 | bytes 2000000 | tf_op jit(solution)/shard_map/prepare/pallas_call | solution.py:195
  5.3 0.6 %collective-permute-done.refs_2_ = bf16[16,1536]{1,0:T(8,128)(2,1)S(1)} collective-permute-done((bf16[16,1536]{1,0:T(8,128)(2,1)S(1)}, bf16[16,1536]{1,0:T(8,128)(2,1)S(1)}, u32[]{:S(2)}, u32[]{:S(2)}) %collective-permute-start) | collective-permute-done | bytes 49184 | tf_op jit(solution)/shard_map/ppermute | solution.py:23
  5.9 0.0 collective-permute-start.2
  5.9 0.0 collective-permute-done.1.refs_1_
  5.9 1.2 %collective-permute-done.2.refs_3_ = bf16[16,1536]{1,0:T(8,128)(2,1)S(1)} collective-permute-done((bf16[16,1536]{1,0:T(8,128)(2,1)S(1)}, bf16[16,1536]{1,0:T(8,128)(2,1)S(1)}, u32[]{:S(2)}, u32[]{:S(2)}) %collective-permute-start.2) | collective-permute-done | bytes 49184 | tf_op jit(solution)/shard_map/ppermute | solution.py:23
  7.1 0.8 %correlate.1 = (f32[8,128]{1,0:T(8,128)S(1)}, f32[8,128]{1,0:T(8,128)S(1)}, f32[8,128]{1,0:T(8,128)S(1)}, f32[8,128]{1,0:T(8,128)S(1)}) custom-call(s32[16,128]{1,0:T(8,128)S(1)} %get-tuple-element.17.table, bf16[16,1536]{1,0:T(8,128)(2,1)S(1)} %pack.1.refs_0_, bf16[16,1536]{1,0:T(8,128)(2,1)S(1)} %collective-permute-done.1.refs_1_, ...), custom_call_target="tpu_custom_call" | custom-call | tf_op jit(solution)/shard_map/correlate/pallas_call | solution.py:195
  8.0 3.2 %collective-permute-start.3 = (f32[8,128]{1,0:T(8,128)S(1)}, f32[8,128]{1,0:T(8,128)S(1)}, u32[]{:S(2)}, u32[]{:S(2)}) collective-permute-start(f32[8,128]{1,0:T(8,128)S(1)} %get-tuple-element.24), channel_id=1, source_target_pairs={{0,2},{1,3},{2,1},{3,0},{4,6},{5,7},{6,5},{7,4},{8,10},{9,11},{10,... | collective-permute-start | bytes 12296 | tf_op jit(solution)/shard_map/ppermute | solution.py:274
  11.1 1.1 %collective-permute-start.4 = (f32[8,128]{1,0:T(8,128)S(1)}, f32[8,128]{1,0:T(8,128)S(1)}, u32[]{:S(2)}, u32[]{:S(2)}) collective-permute-start(f32[8,128]{1,0:T(8,128)S(1)} %get-tuple-element.25), channel_id=1, source_target_pairs={{0,3},{1,2},{2,0},{3,1},{4,7},{5,6},{6,4},{7,5},{8,11},{9,10},{10,... | collective-permute-start | bytes 12296 | tf_op jit(solution)/shard_map/ppermute | solution.py:274
  12.2 0.5 %collective-permute-start.5 = (f32[8,128]{1,0:T(8,128)S(1)}, f32[8,128]{1,0:T(8,128)S(1)}, u32[]{:S(2)}, u32[]{:S(2)}) collective-permute-start(f32[8,128]{1,0:T(8,128)S(1)} %get-tuple-element.26), channel_id=1, source_target_pairs={{0,1},{1,0},{2,3},{3,2},{4,5},{5,4},{6,7},{7,6},{8,9},{9,8},{10,11... | collective-permute-start | bytes 12296 | tf_op jit(solution)/shard_map/ppermute | solution.py:274
  12.7 1.0 %collective-permute-done.3 = f32[8,128]{1,0:T(8,128)S(1)} collective-permute-done((f32[8,128]{1,0:T(8,128)S(1)}, f32[8,128]{1,0:T(8,128)S(1)}, u32[]{:S(2)}, u32[]{:S(2)}) %collective-permute-start.3) | collective-permute-done | bytes 4128 | tf_op jit(solution)/shard_map/ppermute | solution.py:274
  13.7 1.9 %collective-permute-done.4 = f32[8,128]{1,0:T(8,128)S(1)} collective-permute-done((f32[8,128]{1,0:T(8,128)S(1)}, f32[8,128]{1,0:T(8,128)S(1)}, u32[]{:S(2)}, u32[]{:S(2)}) %collective-permute-start.4) | collective-permute-done | bytes 4128 | tf_op jit(solution)/shard_map/ppermute | solution.py:274
  15.7 0.2 %collective-permute-done.5 = f32[8,128]{1,0:T(8,128)S(1)} collective-permute-done((f32[8,128]{1,0:T(8,128)S(1)}, f32[8,128]{1,0:T(8,128)S(1)}, u32[]{:S(2)}, u32[]{:S(2)}) %collective-permute-start.5) | collective-permute-done | bytes 4128 | tf_op jit(solution)/shard_map/ppermute | solution.py:274
  15.8 0.6 %rsqrt_multiply_fusion = f32[4,128]{1,0:T(4,128)} fusion(f32[8,128]{1,0:T(8,128)S(1)} %collective-permute-done.5, f32[8,128]{1,0:T(8,128)S(1)} %collective-permute-done.4, f32[8,128]{1,0:T(8,128)S(1)} %collective-permute-done.3, f32[8,128]{1,0:T(8,128)S(1)} %get-tuple-element.23), kind=kLoop, calls=%fused_computation | loop fusion | flops 3584 | bytes 18432 | tf_op jit(solution)/shard_map/div | solution.py:283
Async XLA Ops:
  0.8 5.1 %collective-permute-start = (bf16[16,1536]{1,0:T(8,128)(2,1)S(1)}, bf16[16,1536]{1,0:T(8,128)(2,1)S(1)}, u32[]{:S(2)}, u32[]{:S(2)}) collective-permute-start(bf16[16,1536]{1,0:T(8,128)(2,1)S(1)} %pack.1.refs_0_), channel_id=1, source_target_pairs={{0,8},{4,12},{8,0},{12,4},{1,9},{5,13},{9,1},{13,5},{2,10},{6,14},... | collective-permute-start | bytes 147464 | tf_op jit(solution)/shard_map/ppermute | solution.py:23
  3.8 2.1 %collective-permute-start.1 = (bf16[16,1536]{1,0:T(8,128)(2,1)S(1)}, bf16[16,1536]{1,0:T(8,128)(2,1)S(1)}, u32[]{:S(2)}, u32[]{:S(2)}) collective-permute-start(bf16[16,1536]{1,0:T(8,128)(2,1)S(1)} %pack.1.refs_0_), channel_id=1, source_target_pairs={{0,4},{4,0},{8,12},{12,8},{1,5},{5,1},{9,13},{13,9},{2,6},{6,2},{1... | collective-permute-start | bytes 147464 | tf_op jit(solution)/shard_map/ppermute | solution.py:23
  5.9 1.2 %collective-permute-start.2 = (bf16[16,1536]{1,0:T(8,128)(2,1)S(1)}, bf16[16,1536]{1,0:T(8,128)(2,1)S(1)}, u32[]{:S(2)}, u32[]{:S(2)}) collective-permute-start(bf16[16,1536]{1,0:T(8,128)(2,1)S(1)} %collective-permute-done.refs_2_), channel_id=1, source_target_pairs={{0,4},{4,0},{8,12},{12,8},{1,5},{5,1},{9,13},{13,9},{2,6},{6,2},{1... | collective-permute-start | bytes 147464 | tf_op jit(solution)/shard_map/ppermute | solution.py:23
  8.0 5.8 %collective-permute-start.3 = (f32[8,128]{1,0:T(8,128)S(1)}, f32[8,128]{1,0:T(8,128)S(1)}, u32[]{:S(2)}, u32[]{:S(2)}) collective-permute-start(f32[8,128]{1,0:T(8,128)S(1)} %get-tuple-element.24), channel_id=1, source_target_pairs={{0,2},{1,3},{2,1},{3,0},{4,6},{5,7},{6,5},{7,4},{8,10},{9,11},{10,... | collective-permute-start | bytes 12296 | tf_op jit(solution)/shard_map/ppermute | solution.py:274
  11.1 4.5 %collective-permute-start.4 = (f32[8,128]{1,0:T(8,128)S(1)}, f32[8,128]{1,0:T(8,128)S(1)}, u32[]{:S(2)}, u32[]{:S(2)}) collective-permute-start(f32[8,128]{1,0:T(8,128)S(1)} %get-tuple-element.25), channel_id=1, source_target_pairs={{0,3},{1,2},{2,0},{3,1},{4,7},{5,6},{6,4},{7,5},{8,11},{9,10},{10,... | collective-permute-start | bytes 12296 | tf_op jit(solution)/shard_map/ppermute | solution.py:274
  12.2 3.6 %collective-permute-start.5 = (f32[8,128]{1,0:T(8,128)S(1)}, f32[8,128]{1,0:T(8,128)S(1)}, u32[]{:S(2)}, u32[]{:S(2)}) collective-permute-start(f32[8,128]{1,0:T(8,128)S(1)} %get-tuple-element.26), channel_id=1, source_target_pairs={{0,1},{1,0},{2,3},{3,2},{4,5},{5,4},{6,7},{7,6},{8,9},{9,8},{10,11... | collective-permute-start | bytes 12296 | tf_op jit(solution)/shard_map/ppermute | solution.py:274

commit v5 on v3

v5 whole, which is shorter than its diff:
```python
import functools

import jax
import jax.numpy as jnp
from jax import lax
from jax.experimental import pallas as pl
from jax.experimental.pallas import tpu as pltpu
from jax.sharding import PartitionSpec as P

LAGS = 512
EPS = 1e-06
LANES = 128
PARAMS = pltpu.CompilerParams(vmem_limit_bytes=8 * 1024 * 1024)
STEP = 64
ROUTES = {
    ("tmpl", 4): ((3, 2, 0, 1), (2, 3, 1, 0), (1, 0, 3, 2)),
    ("chan", 4): ((2, 3, 1, 0), (3, 2, 0, 1), (1, 0, 3, 2)),
}
ROWS = 8
VMEM = pl.BlockSpec(memory_space=pltpu.VMEM)
HBM = pl.BlockSpec(memory_space=pltpu.HBM)


def exchange(value, axis, distance):
    size = lax.axis_size(axis)
    return lax.ppermute(value, axis, [(i, i ^ distance) for i in range(size)])


def routes(axis, size):
    return ROUTES.get((axis, size), tuple(tuple(i ^ k for i in range(size)) for k in range(1, size)))


def send(value, axis, route):
    return lax.ppermute(value, axis, list(enumerate(route)))


def lookup(values, place):
    found = jnp.int32(values[0])
    for i in range(1, len(values)):
        found = jnp.where(place == i, values[i], found)
    return found


def fetch(sources, targets, sems):
    copies = [pltpu.make_async_copy(a, b, sems.at[i]) for i, (a, b) in enumerate(zip(sources, targets))]
    for copy in copies:
        copy.start()
    return copies


def pack(waveforms, selection, *refs):
    outs, (taken, choice, sems) = refs[:-3], refs[-3:]
    copies = fetch((waveforms, selection), (taken, choice), sems)
    high, samples = waveforms.shape
    _, _, owners, capacity = choice.shape
    me = lax.axis_index("tmpl")
    tall = -(-high // 16) * 16
    row = lax.broadcasted_iota(jnp.int32, (ROWS, tall), 0)
    column = lax.broadcasted_iota(jnp.int32, (ROWS, tall), 1)
    for copy in reversed(copies):
        copy.wait()
    picks = []
    for route in (tuple(range(owners)),) + routes("tmpl", owners):
        target = lookup(route, me)
        local = jnp.full((ROWS, tall), -1, jnp.int32)
        for j in range(capacity):
            local = jnp.where(row == j, choice[0, 0, target, j], local)
        picks.append(jnp.where(local == column, 1.0, 0.0))
    picks = jnp.concatenate(picks, axis=0).astype(jnp.bfloat16)
    records = jnp.pad(taken[...].astype(jnp.float32), ((0, tall - high), (0, 0))).astype(jnp.bfloat16)
    picked = jnp.dot(picks, records, preferred_element_type=jnp.float32)
    for i, out in enumerate(outs):
        out[...] = picked[i * ROWS : (i + 1) * ROWS].astype(jnp.bfloat16)


def prepare(
    owners, capacity, tlen, templates, lists, moveouts, weights, bands, box, scale, totals, table, rows, taken, entries, shifts, factors, sems
):
    copies = fetch((templates, lists, moveouts, weights), (taken, entries, shifts, factors), sems)
    count, slots, _ = taken.shape
    pairs = count * slots
    depth = box.shape[0]
    groups = LAGS // STEP
    tap = lax.broadcasted_iota(jnp.int32, (depth, LANES), 0) - lax.broadcasted_iota(jnp.int32, (depth, LANES), 1) % STEP
    box[...] = jnp.where((tap >= 0) & (tap < tlen), 1.0, 0.0).astype(jnp.bfloat16)
    rows[...] = jnp.zeros_like(rows)
    for copy in copies:
        copy.wait()
    for m in range(count):
        rows[m * slots : (m + 1) * slots, :tlen] = taken[m].astype(jnp.float32)
    row = lax.broadcasted_iota(jnp.int32, (LANES, LANES), 0)
    lane = lax.broadcasted_iota(jnp.int32, (LANES, LANES), 1)
    late = row >= lane % STEP
    mirror = jnp.where(row + lane == LANES - 1, 1.0, 0.0).astype(jnp.bfloat16)
    zero = jnp.zeros((LANES, LANES), jnp.float32)
    values = rows[...]
    power = jnp.sum(values * values, axis=1, keepdims=True) / tlen
    factor = 1.0 / (jnp.sqrt(jnp.float32(tlen)) * jnp.sqrt(power + EPS))
    me = lax.axis_index("tmpl")
    turns = LANES // STEP
    sources = [me] + [lookup([route.index(i) for i in range(owners)], me) for route in routes("tmpl", owners)]
    for p in range(pairs):
        m, j = p // slots, p % slots
        source, slot = entries[j, m] // capacity, entries[j, m] % capacity
        for i in range(owners):
            slot = jnp.where(source == sources[i], slot % capacity + i * ROWS, slot)
        for h in range(turns):
            shift = shifts[j, m] + h * STEP
            q = p * turns + h
            table[q : q + 1, :] = jnp.full((1, LANES), slot + (shift // LANES) * owners * ROWS)
            table[turns * pairs + q : turns * pairs + q + 1, :] = jnp.full((1, LANES), (LANES - shift % LANES) % LANES)
        weight = factors[j, m].astype(jnp.float32)
        scale[p * groups : (p + 1) * groups, :] = jnp.broadcast_to(factor[p : p + 1] * weight, (groups, LANES))
    turned = [
        jnp.dot(values[:, d * LANES : (d + 1) * LANES].astype(jnp.bfloat16), mirror, preferred_element_type=jnp.float32)
        for d in range(-(-tlen // LANES))
    ]
    for c in range(pairs // turns):
        j, m = c // (count // turns), c % (count // turns) * turns
        before = zero
        for d in range(depth // LANES):
            now = zero
            if d * LANES < tlen:
                for h in range(turns):
                    back = turned[d][(m + h) * slots + j : (m + h) * slots + j + 1, :]
                    other = pltpu.roll(jnp.broadcast_to(back, (LANES, LANES)), 1 + h * STEP, axis=1, stride=1, stride_axis=0)
                    now = jnp.where(lane < h * STEP, now, other)
            bands[d * LANES : (d + 1) * LANES, c * LANES : (c + 1) * LANES] = jnp.where(late, now, before).astype(jnp.bfloat16)
            before = now
    for m in range(count):
        total = jnp.int32(0)
        for j in range(slots):
            total += factors[j, m] * factors[j, m]
        totals[m : m + 1, :] = jnp.full((1, LANES), total.astype(jnp.float32))


def correlate(owners, columns, tlen, count, slots, table, *refs):
    packed, refs = refs[:owners], refs[owners:]
    bands, box, scale, totals = refs[:4]
    outs, (lanes, taps, squares, stacks, sums, blocks) = refs[4:-6], refs[-6:]
    column = lax.axis_index("chan")
    pairs = count * slots
    depth = box.shape[0]
    pieces = packed[0].shape[1] // LANES
    stride = owners * ROWS
    groups = LAGS // STEP
    turns = LANES // STEP
    reach = LAGS // LANES + depth // LANES - 1
    for i in range(owners):
        wide = packed[i][...].astype(jnp.float32)
        for d in range(pieces):
            lanes[d * stride + i * ROWS : d * stride + (i + 1) * ROWS, :] = wide[:, d * LANES : (d + 1) * LANES]
    lanes[pieces * stride :, :] = jnp.zeros((stride, LANES), jnp.float32)
    places = table[...]
    lane = lax.broadcasted_iota(jnp.int32, (reach, LANES), 1)
    for p in range(pairs):
        for h in range(turns):
            first = places[p * turns + h, 0]
            back = places[turns * pairs + p * turns + h, 0]
            low = pltpu.roll(lanes[pl.ds(first, reach, stride=stride), :], back, axis=1)
            up = pltpu.roll(lanes[pl.ds(first + stride, reach, stride=stride), :], back, axis=1)
            stacks[p, pl.ds(h, reach, stride=turns), :] = jnp.where((lane < back) | (back == 0), low, up)
        for d in range(depth // LANES):
            piece = stacks[p, d * turns : d * turns + groups, :]
            taps[p * groups : (p + 1) * groups, d * LANES : (d + 1) * LANES] = piece
            squares[p * groups : (p + 1) * groups, d * LANES : (d + 1) * LANES] = piece * piece
    square = squares[...]
    main = square.astype(jnp.bfloat16)
    left = (square - main.astype(jnp.float32)).astype(jnp.bfloat16)
    energy = jnp.dot(jnp.concatenate([main, left], axis=0), box[...], preferred_element_type=jnp.float32)
    energy = energy[: pairs * groups] + energy[pairs * groups :]
    norm = scale[...] * lax.rsqrt(energy * (1.0 / tlen) + EPS)
    product = jnp.dot(taps[...].astype(jnp.bfloat16), bands[...], preferred_element_type=jnp.float32)
    front = lax.broadcasted_iota(jnp.int32, (LAGS // LANES, LANES), 1) < STEP
    for m in range(count):
        both = jnp.zeros((groups, LANES), jnp.float32)
        for j in range(slots):
            rows = slice((m * slots + j) * groups, (m * slots + j + 1) * groups)
            c = j * (count // turns) + m // turns
            both += product[rows, c * LANES : (c + 1) * LANES] * norm[rows, :]
        sums[m] = both
        even = sums[m, pl.ds(0, LAGS // LANES, stride=turns), :]
        odd = sums[m, pl.ds(1, LAGS // LANES, stride=turns), :]
        if m % turns:
            even = pltpu.roll(even, STEP, axis=1)
        else:
            odd = pltpu.roll(odd, STEP, axis=1)
        blocks[:, m, :] = jnp.where(front, even, odd)
        blocks[:, count + m, :] = jnp.broadcast_to(totals[m : m + 1, :], (LAGS // LANES, LANES))
    width = LAGS // columns
    share = LANES // width

    def block(target):
        part = blocks[target // share]
        chosen = part[:, :width]
        for s in range(1, share):
            chosen = jnp.where(target % share == s, part[:, s * width : (s + 1) * width], chosen)
        return chosen

    outs[-1][...] = block(column)
    if ("chan", columns) in ROUTES:
        for out, route in zip(outs, routes("chan", columns)):
            out[...] = block(lookup(route, column))
        return
    distance = 1
    for out in outs[:-1]:
        for q in range(out.shape[0]):
            out[q] = block(column ^ (distance * (2 * q + 1)))
        distance *= 2


def shards(waveforms, templates, selection, channel_list, moveouts, weights):
    owners = lax.axis_size("tmpl")
    columns = lax.axis_size("chan")
    count, slots, tlen = templates.shape
    pairs = count * slots
    groups = LAGS // STEP
    width = LAGS // columns
    samples = waveforms.shape[1]
    capacity = selection.shape[3]
    depth = -(-(tlen + STEP - 1) // LANES) * LANES
    pieces = samples // LANES

    def call(kernel, name, ins, outs, scratch, arguments, cost=None):
        if ins is HBM:
            arguments = [pltpu.with_memory_space_constraint(x, pltpu.HBM) for x in arguments]
        single = not isinstance(outs, tuple)
        return pl.pallas_call(
            kernel,
            out_shape=outs,
            in_specs=[ins] * len(arguments),
            out_specs=VMEM if single else (VMEM,) * len(outs),
            scratch_shapes=scratch,
            compiler_params=PARAMS,
            cost_estimate=cost,
            name=name,
        )(*arguments)

    rows = jax.ShapeDtypeStruct((ROWS, samples), waveforms.dtype)
    own, *outgoing = call(
        pack,
        "pack",
        HBM,
        (rows,) * owners,
        [
            pltpu.VMEM(waveforms.shape, waveforms.dtype),
            pltpu.SMEM(selection.shape, selection.dtype),
            pltpu.SemaphoreType.DMA((2,)),
        ],
        (waveforms, selection),
    )
    bands, box, scale, totals, table = call(
        functools.partial(prepare, owners, capacity, tlen),
        "prepare",
        HBM,
        (
            jax.ShapeDtypeStruct((depth, pairs * STEP), jnp.bfloat16),
            jax.ShapeDtypeStruct((depth, LANES), jnp.bfloat16),
            jax.ShapeDtypeStruct((pairs * groups, LANES), jnp.float32),
            jax.ShapeDtypeStruct((count, LANES), jnp.float32),
            jax.ShapeDtypeStruct((2 * pairs * (LANES // STEP), LANES), jnp.int32),
        ),
        [
            pltpu.VMEM((pairs, depth), jnp.float32),
            pltpu.VMEM(templates.shape, templates.dtype),
            pltpu.SMEM((slots, count), jnp.int32),
            pltpu.SMEM((slots, count), jnp.int32),
            pltpu.SMEM((slots, count), jnp.int32),
            pltpu.SemaphoreType.DMA((4,)),
        ],
        (templates, channel_list.T, moveouts.T, weights.T),
        pl.CostEstimate(flops=2_000_000, bytes_accessed=2_000_000, transcendentals=0),
    )
    packed = [own] + [send(x, "tmpl", route) for x, route in zip(outgoing, routes("tmpl", owners))]
    sizes = []
    while (columns >> len(sizes)) > 1:
        sizes.append(columns >> (len(sizes) + 1))
    shapes = [(s, 2 * count, width) for s in sizes] + [(2 * count, width)]
    if ("chan", columns) in ROUTES:
        shapes = [(2 * count, width)] * columns
    parts = call(
        functools.partial(correlate, owners, columns, tlen, count, slots),
        "correlate",
        VMEM,
        tuple(jax.ShapeDtypeStruct(s, jnp.float32) for s in shapes),
        [
            pltpu.VMEM(((pieces + 1) * owners * ROWS, LANES), jnp.float32),
            pltpu.VMEM((pairs * groups, depth), jnp.float32),
            pltpu.VMEM((pairs * groups, depth), jnp.float32),
            pltpu.VMEM((pairs, 32, LANES), jnp.float32),
            pltpu.VMEM((count, groups, LANES), jnp.float32),
            pltpu.VMEM((LAGS // LANES, 2 * count, LANES), jnp.float32),
        ],
        (table, *packed, bands, box, scale, totals),
    )
    stages, own = list(parts[:-1]), [parts[-1]]
    if ("chan", columns) in ROUTES:
        for part, route in zip(stages, routes("chan", columns)):
            own.append(send(part, "chan", route))
        stages = []
    for i in range(len(stages)):
        arrived = exchange(stages[i], "chan", 1 << i)
        own.append(arrived[0])
        for later in range(i + 1, len(stages)):
            step = 1 << (later - i)
            stages[later] = stages[later] + arrived[step // 2 :: step]
    top = sum(x[:count] for x in own)
    return top / jnp.sqrt(sum(x[count:] for x in own))


def solution(mesh):
    placed = (
        P(("parts", "tmpl", "chan"), None),
        P(("parts", "tmpl"), "chan", None),
        P(("parts", "tmpl"), "chan", None, None),
        P(("parts", "tmpl"), "chan"),
        P(("parts", "tmpl"), "chan"),
        P(("parts", "tmpl"), "chan"),
    )
    return jax.shard_map(
        shards, mesh=mesh, in_specs=placed, out_specs=P(("parts", "tmpl"), "chan"), check_vma=False
    )
```

time: 17.2 us -> 15.6 us (0.907)
  starting transfers between devices: 8.21 us -> 7.32 us
  waiting for transfers between devices: 5.06 us -> 4.34 us
    ppermute x5 -> x6, starting transfers between devices: 8.21 us -> 7.32 us  [send(): return lax.ppermute(value, axis, list(enumerate(route)))]
    ppermute x5 -> x6, waiting for transfers between devices: 5.06 us -> 4.34 us  [send(): return lax.ppermute(value, axis, list(enumerate(route)))]
  transfers between devices with their start and end apart: 5 -> 6, of which waited for: 4 -> 5; matrix products, arithmetic and copies ran while one was open for 0% -> 0% of each run, Pallas kernels for 8% -> 10%
where the time goes in v5:
time: 15.6 us; the launch traced here: 15.4 us
  starting transfers between devices  7.32 us (47%)
  waiting for transfers between devices  4.34 us (28%)
  Pallas kernels  3.12 us (20%)
  other arithmetic  0.59 us (4%)
    ppermute x6, starting transfers between devices, send(): return lax.ppermute(value, axis, list(enumerate(route)))  7.32 us
    ppermute x6, waiting for transfers between devices, send(): return lax.ppermute(value, axis, list(enumerate(route)))  4.34 us
    pallas_call x3, Pallas kernels, call(): pl.pallas_call(kernel, out_shape=outs, in_specs=[ins] * len(arguments), o...  3.12 us
    div x1, other arithmetic, shards(): return top / jnp.sqrt(sum((x[count:] for x in own)))  0.59 us
  transfers between devices with their start and end apart: 6, of which 5 were waited for; matrix products, arithmetic and copies ran while one was open for 0% of the time, Pallas kernels for 10%

profile of v5, /device:TPU:0, one launch (start us, length us, event | category | flops | bytes accessed | tf_op | source)
XLA Modules:
  0.0 15.4 jit_solution(558225933037823039)
XLA Ops:
  0.0 1.0 %pack.1 = (bf16[8,1536]{1,0:T(8,128)(2,1)S(1)}, bf16[8,1536]{1,0:T(8,128)(2,1)S(1)}, bf16[8,1536]{1,0:T(8,128)(2,1)S(1)}, bf16[8,1536]{1,0:T(8,128)(2,1)S(1)}) custom-call(bf16[12,1536]{1,0:T(8,128)(2,1)} %waveforms.1, s32[1,1,4,6]{3,2,1,0:T(4,128)} %selection.1), custom_call_target="tpu_custom_call" | custom-call | tf_op jit(solution)/shard_map/pack/pallas_call | solution.py:228
  1.0 2.4 %collective-permute-start = (bf16[8,1536]{1,0:T(8,128)(2,1)S(1)}, bf16[8,1536]{1,0:T(8,128)(2,1)S(1)}, u32[]{:S(2)}, u32[]{:S(2)}) collective-permute-start(bf16[8,1536]{1,0:T(8,128)(2,1)S(1)} %get-tuple-element.20), channel_id=1, source_target_pairs={{0,12},{4,8},{8,0},{12,4},{1,13},{5,9},{9,1},{13,5},{2,14},{6,10},... | collective-permute-start | bytes 73736 | tf_op jit(solution)/shard_map/ppermute | solution.py:34
  3.4 0.6 %collective-permute-start.1 = (bf16[8,1536]{1,0:T(8,128)(2,1)S(1)}, bf16[8,1536]{1,0:T(8,128)(2,1)S(1)}, u32[]{:S(2)}, u32[]{:S(2)}) collective-permute-start(bf16[8,1536]{1,0:T(8,128)(2,1)S(1)} %get-tuple-element.21), channel_id=1, source_target_pairs={{0,8},{4,12},{8,4},{12,0},{1,9},{5,13},{9,5},{13,1},{2,10},{6,14},... | collective-permute-start | bytes 73736 | tf_op jit(solution)/shard_map/ppermute | solution.py:34
  4.1 0.1 collective-permute-start.2
  4.1 1.5 %prepare.1 = (bf16[768,512]{1,0:T(8,128)(2,1)S(1)}, bf16[768,128]{1,0:T(8,128)(2,1)S(1)}, f32[64,128]{1,0:T(8,128)S(1)}, f32[4,128]{1,0:T(4,128)S(1)}, s32[32,128]{1,0:T(8,128)S(1)}) custom-call(bf16[4,2,600]{2,1,0:T(2,128)(2,1)} %templates.1, s32[2,4]{1,0:T(2,128)} %bitcast.3, s32[2,4]{1,0:T(2,128)} %bitcast.4, s32[2,4]{1,0:T(2,128)} %bitcast.5), custom_call_target="tpu_custom_call" | custom-call | flops 2000000 | bytes 2000000 | tf_op jit(solution)/shard_map/prepare/pallas_call | solution.py:228
  5.6 0.2 %collective-permute-done.refs_1_ = bf16[8,1536]{1,0:T(8,128)(2,1)S(1)} collective-permute-done((bf16[8,1536]{1,0:T(8,128)(2,1)S(1)}, bf16[8,1536]{1,0:T(8,128)(2,1)S(1)}, u32[]{:S(2)}, u32[]{:S(2)}) %collective-permute-start) | collective-permute-done | bytes 24608 | tf_op jit(solution)/shard_map/ppermute | solution.py:34
  5.8 0.9 %collective-permute-done.1.refs_2_ = bf16[8,1536]{1,0:T(8,128)(2,1)S(1)} collective-permute-done((bf16[8,1536]{1,0:T(8,128)(2,1)S(1)}, bf16[8,1536]{1,0:T(8,128)(2,1)S(1)}, u32[]{:S(2)}, u32[]{:S(2)}) %collective-permute-start.1) | collective-permute-done | bytes 24608 | tf_op jit(solution)/shard_map/ppermute | solution.py:34
  6.7 0.0 collective-permute-done.2.refs_3_
  6.7 0.6 %correlate.1 = (f32[8,128]{1,0:T(8,128)S(1)}, f32[8,128]{1,0:T(8,128)S(1)}, f32[8,128]{1,0:T(8,128)S(1)}, f32[8,128]{1,0:T(8,128)S(1)}) custom-call(s32[32,128]{1,0:T(8,128)S(1)} %get-tuple-element.18.table, bf16[8,1536]{1,0:T(8,128)(2,1)S(1)} %get-tuple-element.19.refs_0_, bf16[8,1536]{1,0:T(8,128)(2,1)S(1)} %collective-permute-done.refs_1_, ...), custom_call_target="tpu_custom_call" | custom-call | tf_op jit(solution)/shard_map/correlate/pallas_call | solution.py:228
  7.3 2.6 %collective-permute-start.3 = (f32[8,128]{1,0:T(8,128)S(1)}, f32[8,128]{1,0:T(8,128)S(1)}, u32[]{:S(2)}, u32[]{:S(2)}) collective-permute-start(f32[8,128]{1,0:T(8,128)S(1)} %get-tuple-element.28), channel_id=1, source_target_pairs={{0,2},{1,3},{2,1},{3,0},{4,6},{5,7},{6,5},{7,4},{8,10},{9,11},{10,... | collective-permute-start | bytes 12296 | tf_op jit(solution)/shard_map/ppermute | solution.py:34
  10.0 1.2 %collective-permute-start.4 = (f32[8,128]{1,0:T(8,128)S(1)}, f32[8,128]{1,0:T(8,128)S(1)}, u32[]{:S(2)}, u32[]{:S(2)}) collective-permute-start(f32[8,128]{1,0:T(8,128)S(1)} %get-tuple-element.29), channel_id=1, source_target_pairs={{0,3},{1,2},{2,0},{3,1},{4,7},{5,6},{6,4},{7,5},{8,11},{9,10},{10,... | collective-permute-start | bytes 12296 | tf_op jit(solution)/shard_map/ppermute | solution.py:34
  11.2 0.3 %collective-permute-start.5 = (f32[8,128]{1,0:T(8,128)S(1)}, f32[8,128]{1,0:T(8,128)S(1)}, u32[]{:S(2)}, u32[]{:S(2)}) collective-permute-start(f32[8,128]{1,0:T(8,128)S(1)} %get-tuple-element.30), channel_id=1, source_target_pairs={{0,1},{1,0},{2,3},{3,2},{4,5},{5,4},{6,7},{7,6},{8,9},{9,8},{10,11... | collective-permute-start | bytes 12296 | tf_op jit(solution)/shard_map/ppermute | solution.py:34
  11.5 1.2 %collective-permute-done.3 = f32[8,128]{1,0:T(8,128)S(1)} collective-permute-done((f32[8,128]{1,0:T(8,128)S(1)}, f32[8,128]{1,0:T(8,128)S(1)}, u32[]{:S(2)}, u32[]{:S(2)}) %collective-permute-start.3) | collective-permute-done | bytes 4128 | tf_op jit(solution)/shard_map/ppermute | solution.py:34
  12.8 1.7 %collective-permute-done.4 = f32[8,128]{1,0:T(8,128)S(1)} collective-permute-done((f32[8,128]{1,0:T(8,128)S(1)}, f32[8,128]{1,0:T(8,128)S(1)}, u32[]{:S(2)}, u32[]{:S(2)}) %collective-permute-start.4) | collective-permute-done | bytes 4128 | tf_op jit(solution)/shard_map/ppermute | solution.py:34
  14.5 0.3 %collective-permute-done.5 = f32[8,128]{1,0:T(8,128)S(1)} collective-permute-done((f32[8,128]{1,0:T(8,128)S(1)}, f32[8,128]{1,0:T(8,128)S(1)}, u32[]{:S(2)}, u32[]{:S(2)}) %collective-permute-start.5) | collective-permute-done | bytes 4128 | tf_op jit(solution)/shard_map/ppermute | solution.py:34
  14.8 0.6 %rsqrt_multiply_fusion = f32[4,128]{1,0:T(4,128)} fusion(f32[8,128]{1,0:T(8,128)S(1)} %collective-permute-done.5, f32[8,128]{1,0:T(8,128)S(1)} %collective-permute-done.4, f32[8,128]{1,0:T(8,128)S(1)} %collective-permute-done.3, f32[8,128]{1,0:T(8,128)S(1)} %get-tuple-element.27), kind=kLoop, calls=%fused_computation | loop fusion | flops 3584 | bytes 18432 | tf_op jit(solution)/shard_map/div | solution.py:308
Async XLA Ops:
  1.0 4.8 %collective-permute-start = (bf16[8,1536]{1,0:T(8,128)(2,1)S(1)}, bf16[8,1536]{1,0:T(8,128)(2,1)S(1)}, u32[]{:S(2)}, u32[]{:S(2)}) collective-permute-start(bf16[8,1536]{1,0:T(8,128)(2,1)S(1)} %get-tuple-element.20), channel_id=1, source_target_pairs={{0,12},{4,8},{8,0},{12,4},{1,13},{5,9},{9,1},{13,5},{2,14},{6,10},... | collective-permute-start | bytes 73736 | tf_op jit(solution)/shard_map/ppermute | solution.py:34
  3.4 3.3 %collective-permute-start.1 = (bf16[8,1536]{1,0:T(8,128)(2,1)S(1)}, bf16[8,1536]{1,0:T(8,128)(2,1)S(1)}, u32[]{:S(2)}, u32[]{:S(2)}) collective-permute-start(bf16[8,1536]{1,0:T(8,128)(2,1)S(1)} %get-tuple-element.21), channel_id=1, source_target_pairs={{0,8},{4,12},{8,4},{12,0},{1,9},{5,13},{9,5},{13,1},{2,10},{6,14},... | collective-permute-start | bytes 73736 | tf_op jit(solution)/shard_map/ppermute | solution.py:34
  4.1 2.6 %collective-permute-start.2 = (bf16[8,1536]{1,0:T(8,128)(2,1)S(1)}, bf16[8,1536]{1,0:T(8,128)(2,1)S(1)}, u32[]{:S(2)}, u32[]{:S(2)}) collective-permute-start(bf16[8,1536]{1,0:T(8,128)(2,1)S(1)} %get-tuple-element.22), channel_id=1, source_target_pairs={{0,4},{4,0},{8,12},{12,8},{1,5},{5,1},{9,13},{13,9},{2,6},{6,2},{1... | collective-permute-start | bytes 73736 | tf_op jit(solution)/shard_map/ppermute | solution.py:34
  7.3 5.5 %collective-permute-start.3 = (f32[8,128]{1,0:T(8,128)S(1)}, f32[8,128]{1,0:T(8,128)S(1)}, u32[]{:S(2)}, u32[]{:S(2)}) collective-permute-start(f32[8,128]{1,0:T(8,128)S(1)} %get-tuple-element.28), channel_id=1, source_target_pairs={{0,2},{1,3},{2,1},{3,0},{4,6},{5,7},{6,5},{7,4},{8,10},{9,11},{10,... | collective-permute-start | bytes 12296 | tf_op jit(solution)/shard_map/ppermute | solution.py:34
  10.0 4.5 %collective-permute-start.4 = (f32[8,128]{1,0:T(8,128)S(1)}, f32[8,128]{1,0:T(8,128)S(1)}, u32[]{:S(2)}, u32[]{:S(2)}) collective-permute-start(f32[8,128]{1,0:T(8,128)S(1)} %get-tuple-element.29), channel_id=1, source_target_pairs={{0,3},{1,2},{2,0},{3,1},{4,7},{5,6},{6,4},{7,5},{8,11},{9,10},{10,... | collective-permute-start | bytes 12296 | tf_op jit(solution)/shard_map/ppermute | solution.py:34
  11.2 3.6 %collective-permute-start.5 = (f32[8,128]{1,0:T(8,128)S(1)}, f32[8,128]{1,0:T(8,128)S(1)}, u32[]{:S(2)}, u32[]{:S(2)}) collective-permute-start(f32[8,128]{1,0:T(8,128)S(1)} %get-tuple-element.30), channel_id=1, source_target_pairs={{0,1},{1,0},{2,3},{3,2},{4,5},{5,4},{6,7},{7,6},{8,9},{9,8},{10,11... | collective-permute-start | bytes 12296 | tf_op jit(solution)/shard_map/ppermute | solution.py:34

commit v6 on v5

--- a/solution.py
+++ b/solution.py
@@ -57,8 +57,7 @@
     tall = -(-high // 16) * 16
     row = lax.broadcasted_iota(jnp.int32, (ROWS, tall), 0)
     column = lax.broadcasted_iota(jnp.int32, (ROWS, tall), 1)
-    for copy in reversed(copies):
-        copy.wait()
+    copies[1].wait()
     picks = []
     for route in (tuple(range(owners)),) + routes("tmpl", owners):
         target = lookup(route, me)
@@ -67,6 +66,7 @@
             local = jnp.where(row == j, choice[0, 0, target, j], local)
         picks.append(jnp.where(local == column, 1.0, 0.0))
     picks = jnp.concatenate(picks, axis=0).astype(jnp.bfloat16)
+    copies[0].wait()
     records = jnp.pad(taken[...].astype(jnp.float32), ((0, tall - high), (0, 0))).astype(jnp.bfloat16)
     picked = jnp.dot(picks, records, preferred_element_type=jnp.float32)
     for i, out in enumerate(outs):
@@ -137,7 +137,7 @@
 def correlate(owners, columns, tlen, count, slots, table, *refs):
     packed, refs = refs[:owners], refs[owners:]
     bands, box, scale, totals = refs[:4]
-    outs, (lanes, taps, squares, stacks, sums, blocks) = refs[4:-6], refs[-6:]
+    outs, (lanes, stacks, sums, blocks) = refs[4:-4], refs[-4:]
     column = lax.axis_index("chan")
     pairs = count * slots
     depth = box.shape[0]
@@ -150,7 +150,7 @@
         wide = packed[i][...].astype(jnp.float32)
         for d in range(pieces):
             lanes[d * stride + i * ROWS : d * stride + (i + 1) * ROWS, :] = wide[:, d * LANES : (d + 1) * LANES]
-    lanes[pieces * stride :, :] = jnp.zeros((stride, LANES), jnp.float32)
+    lanes[pieces * stride : (pieces + 1) * stride, :] = jnp.zeros((stride, LANES), jnp.float32)
     places = table[...]
     lane = lax.broadcasted_iota(jnp.int32, (reach, LANES), 1)
     for p in range(pairs):
@@ -160,17 +160,17 @@
             low = pltpu.roll(lanes[pl.ds(first, reach, stride=stride), :], back, axis=1)
             up = pltpu.roll(lanes[pl.ds(first + stride, reach, stride=stride), :], back, axis=1)
             stacks[p, pl.ds(h, reach, stride=turns), :] = jnp.where((lane < back) | (back == 0), low, up)
-        for d in range(depth // LANES):
-            piece = stacks[p, d * turns : d * turns + groups, :]
-            taps[p * groups : (p + 1) * groups, d * LANES : (d + 1) * LANES] = piece
-            squares[p * groups : (p + 1) * groups, d * LANES : (d + 1) * LANES] = piece * piece
-    square = squares[...]
+    taps = [
+        jnp.concatenate([stacks[p, d * turns : d * turns + groups, :] for d in range(depth // LANES)], axis=1) for p in range(pairs)
+    ]
+    taps = jnp.concatenate(taps, axis=0)
+    square = taps * taps
     main = square.astype(jnp.bfloat16)
     left = (square - main.astype(jnp.float32)).astype(jnp.bfloat16)
     energy = jnp.dot(jnp.concatenate([main, left], axis=0), box[...], preferred_element_type=jnp.float32)
     energy = energy[: pairs * groups] + energy[pairs * groups :]
     norm = scale[...] * lax.rsqrt(energy * (1.0 / tlen) + EPS)
-    product = jnp.dot(taps[...].astype(jnp.bfloat16), bands[...], preferred_element_type=jnp.float32)
+    product = jnp.dot(taps.astype(jnp.bfloat16), bands[...], preferred_element_type=jnp.float32)
     front = lax.broadcasted_iota(jnp.int32, (LAGS // LANES, LANES), 1) < STEP
     for m in range(count):
         both = jnp.zeros((groups, LANES), jnp.float32)
@@ -178,15 +178,15 @@
             rows = slice((m * slots + j) * groups, (m * slots + j + 1) * groups)
             c = j * (count // turns) + m // turns
             both += product[rows, c * LANES : (c + 1) * LANES] * norm[rows, :]
-        sums[m] = both
+        sums[m, :groups, :] = both
         even = sums[m, pl.ds(0, LAGS // LANES, stride=turns), :]
         odd = sums[m, pl.ds(1, LAGS // LANES, stride=turns), :]
         if m % turns:
             even = pltpu.roll(even, STEP, axis=1)
         else:
             odd = pltpu.roll(odd, STEP, axis=1)
-        blocks[:, m, :] = jnp.where(front, even, odd)
-        blocks[:, count + m, :] = jnp.broadcast_to(totals[m : m + 1, :], (LAGS // LANES, LANES))
+        blocks[: LAGS // LANES, m, :] = jnp.where(front, even, odd)
+        blocks[: LAGS // LANES, count + m, :] = jnp.broadcast_to(totals[m : m + 1, :], (LAGS // LANES, LANES))
     width = LAGS // columns
     share = LANES // width
 
@@ -284,12 +284,10 @@
         VMEM,
         tuple(jax.ShapeDtypeStruct(s, jnp.float32) for s in shapes),
         [
-            pltpu.VMEM(((pieces + 1) * owners * ROWS, LANES), jnp.float32),
-            pltpu.VMEM((pairs * groups, depth), jnp.float32),
-            pltpu.VMEM((pairs * groups, depth), jnp.float32),
+            pltpu.VMEM(((pieces + 8) * owners * ROWS, LANES), jnp.float32),
             pltpu.VMEM((pairs, 32, LANES), jnp.float32),
-            pltpu.VMEM((count, groups, LANES), jnp.float32),
-            pltpu.VMEM((LAGS // LANES, 2 * count, LANES), jnp.float32),
+            pltpu.VMEM((count, 2 * groups, LANES), jnp.float32),
+            pltpu.VMEM((2 * LAGS // LANES, 2 * count, LANES), jnp.float32),
         ],
         (table, *packed, bands, box, scale, totals),
     )

time: 15.6 us -> 15.6 us (level)
  no operation moved by 1% of the time
where the time goes in v6:
time: 15.6 us; the launch traced here: 15.4 us
  starting transfers between devices  7.36 us (47%)
  waiting for transfers between devices  4.3 us (28%)
  Pallas kernels  3.13 us (20%)
  other arithmetic  0.59 us (4%)
    ppermute x6, starting transfers between devices, send(): return lax.ppermute(value, axis, list(enumerate(route)))  7.36 us
    ppermute x6, waiting for transfers between devices, send(): return lax.ppermute(value, axis, list(enumerate(route)))  4.3 us
    pallas_call x3, Pallas kernels, call(): pl.pallas_call(kernel, out_shape=outs, in_specs=[ins] * len(arguments), o...  3.13 us
    div x1, other arithmetic, shards(): return top / jnp.sqrt(sum((x[count:] for x in own)))  0.59 us
  transfers between devices with their start and end apart: 6, of which 5 were waited for; matrix products, arithmetic and copies ran while one was open for 0% of the time, Pallas kernels for 10%

profile of v6, /device:TPU:0, one launch (start us, length us, event | category | flops | bytes accessed | tf_op | source)
XLA Modules:
  0.0 15.4 jit_solution(9741553296134133758)
XLA Ops:
  0.0 1.0 %pack.1 = (bf16[8,1536]{1,0:T(8,128)(2,1)S(1)}, bf16[8,1536]{1,0:T(8,128)(2,1)S(1)}, bf16[8,1536]{1,0:T(8,128)(2,1)S(1)}, bf16[8,1536]{1,0:T(8,128)(2,1)S(1)}) custom-call(bf16[12,1536]{1,0:T(8,128)(2,1)} %waveforms.1, s32[1,1,4,6]{3,2,1,0:T(4,128)} %selection.1), custom_call_target="tpu_custom_call" | custom-call | tf_op jit(solution)/shard_map/pack/pallas_call | solution.py:228
  1.0 2.4 %collective-permute-start = (bf16[8,1536]{1,0:T(8,128)(2,1)S(1)}, bf16[8,1536]{1,0:T(8,128)(2,1)S(1)}, u32[]{:S(2)}, u32[]{:S(2)}) collective-permute-start(bf16[8,1536]{1,0:T(8,128)(2,1)S(1)} %get-tuple-element.20), channel_id=1, source_target_pairs={{0,12},{4,8},{8,0},{12,4},{1,13},{5,9},{9,1},{13,5},{2,14},{6,10},... | collective-permute-start | bytes 73736 | tf_op jit(solution)/shard_map/ppermute | solution.py:34
  3.5 0.6 %collective-permute-start.1 = (bf16[8,1536]{1,0:T(8,128)(2,1)S(1)}, bf16[8,1536]{1,0:T(8,128)(2,1)S(1)}, u32[]{:S(2)}, u32[]{:S(2)}) collective-permute-start(bf16[8,1536]{1,0:T(8,128)(2,1)S(1)} %get-tuple-element.21), channel_id=1, source_target_pairs={{0,8},{4,12},{8,4},{12,0},{1,9},{5,13},{9,5},{13,1},{2,10},{6,14},... | collective-permute-start | bytes 73736 | tf_op jit(solution)/shard_map/ppermute | solution.py:34
  4.1 0.1 collective-permute-start.2
  4.1 1.5 %prepare.1 = (bf16[768,512]{1,0:T(8,128)(2,1)S(1)}, bf16[768,128]{1,0:T(8,128)(2,1)S(1)}, f32[64,128]{1,0:T(8,128)S(1)}, f32[4,128]{1,0:T(4,128)S(1)}, s32[32,128]{1,0:T(8,128)S(1)}) custom-call(bf16[4,2,600]{2,1,0:T(2,128)(2,1)} %templates.1, s32[2,4]{1,0:T(2,128)} %bitcast.3, s32[2,4]{1,0:T(2,128)} %bitcast.4, s32[2,4]{1,0:T(2,128)} %bitcast.5), custom_call_target="tpu_custom_call" | custom-call | flops 2000000 | bytes 2000000 | tf_op jit(solution)/shard_map/prepare/pallas_call | solution.py:228
  5.6 0.2 %collective-permute-done.refs_1_ = bf16[8,1536]{1,0:T(8,128)(2,1)S(1)} collective-permute-done((bf16[8,1536]{1,0:T(8,128)(2,1)S(1)}, bf16[8,1536]{1,0:T(8,128)(2,1)S(1)}, u32[]{:S(2)}, u32[]{:S(2)}) %collective-permute-start) | collective-permute-done | bytes 24608 | tf_op jit(solution)/shard_map/ppermute | solution.py:34
  5.8 0.9 %collective-permute-done.1.refs_2_ = bf16[8,1536]{1,0:T(8,128)(2,1)S(1)} collective-permute-done((bf16[8,1536]{1,0:T(8,128)(2,1)S(1)}, bf16[8,1536]{1,0:T(8,128)(2,1)S(1)}, u32[]{:S(2)}, u32[]{:S(2)}) %collective-permute-start.1) | collective-permute-done | bytes 24608 | tf_op jit(solution)/shard_map/ppermute | solution.py:34
  6.7 0.0 collective-permute-done.2.refs_3_
  6.7 0.6 %correlate.1 = (f32[8,128]{1,0:T(8,128)S(1)}, f32[8,128]{1,0:T(8,128)S(1)}, f32[8,128]{1,0:T(8,128)S(1)}, f32[8,128]{1,0:T(8,128)S(1)}) custom-call(s32[32,128]{1,0:T(8,128)S(1)} %get-tuple-element.18.table, bf16[8,1536]{1,0:T(8,128)(2,1)S(1)} %get-tuple-element.19.refs_0_, bf16[8,1536]{1,0:T(8,128)(2,1)S(1)} %collective-permute-done.refs_1_, ...), custom_call_target="tpu_custom_call" | custom-call | tf_op jit(solution)/shard_map/correlate/pallas_call | solution.py:228
  7.3 2.6 %collective-permute-start.3 = (f32[8,128]{1,0:T(8,128)S(1)}, f32[8,128]{1,0:T(8,128)S(1)}, u32[]{:S(2)}, u32[]{:S(2)}) collective-permute-start(f32[8,128]{1,0:T(8,128)S(1)} %get-tuple-element.28), channel_id=1, source_target_pairs={{0,2},{1,3},{2,1},{3,0},{4,6},{5,7},{6,5},{7,4},{8,10},{9,11},{10,... | collective-permute-start | bytes 12296 | tf_op jit(solution)/shard_map/ppermute | solution.py:34
  10.0 1.2 %collective-permute-start.4 = (f32[8,128]{1,0:T(8,128)S(1)}, f32[8,128]{1,0:T(8,128)S(1)}, u32[]{:S(2)}, u32[]{:S(2)}) collective-permute-start(f32[8,128]{1,0:T(8,128)S(1)} %get-tuple-element.29), channel_id=1, source_target_pairs={{0,3},{1,2},{2,0},{3,1},{4,7},{5,6},{6,4},{7,5},{8,11},{9,10},{10,... | collective-permute-start | bytes 12296 | tf_op jit(solution)/shard_map/ppermute | solution.py:34
  11.2 0.4 %collective-permute-start.5 = (f32[8,128]{1,0:T(8,128)S(1)}, f32[8,128]{1,0:T(8,128)S(1)}, u32[]{:S(2)}, u32[]{:S(2)}) collective-permute-start(f32[8,128]{1,0:T(8,128)S(1)} %get-tuple-element.30), channel_id=1, source_target_pairs={{0,1},{1,0},{2,3},{3,2},{4,5},{5,4},{6,7},{7,6},{8,9},{9,8},{10,11... | collective-permute-start | bytes 12296 | tf_op jit(solution)/shard_map/ppermute | solution.py:34
  11.6 1.2 %collective-permute-done.3 = f32[8,128]{1,0:T(8,128)S(1)} collective-permute-done((f32[8,128]{1,0:T(8,128)S(1)}, f32[8,128]{1,0:T(8,128)S(1)}, u32[]{:S(2)}, u32[]{:S(2)}) %collective-permute-start.3) | collective-permute-done | bytes 4128 | tf_op jit(solution)/shard_map/ppermute | solution.py:34
  12.8 1.7 %collective-permute-done.4 = f32[8,128]{1,0:T(8,128)S(1)} collective-permute-done((f32[8,128]{1,0:T(8,128)S(1)}, f32[8,128]{1,0:T(8,128)S(1)}, u32[]{:S(2)}, u32[]{:S(2)}) %collective-permute-start.4) | collective-permute-done | bytes 4128 | tf_op jit(solution)/shard_map/ppermute | solution.py:34
  14.5 0.3 %collective-permute-done.5 = f32[8,128]{1,0:T(8,128)S(1)} collective-permute-done((f32[8,128]{1,0:T(8,128)S(1)}, f32[8,128]{1,0:T(8,128)S(1)}, u32[]{:S(2)}, u32[]{:S(2)}) %collective-permute-start.5) | collective-permute-done | bytes 4128 | tf_op jit(solution)/shard_map/ppermute | solution.py:34
  14.8 0.6 %rsqrt_multiply_fusion = f32[4,128]{1,0:T(4,128)} fusion(f32[8,128]{1,0:T(8,128)S(1)} %collective-permute-done.5, f32[8,128]{1,0:T(8,128)S(1)} %collective-permute-done.4, f32[8,128]{1,0:T(8,128)S(1)} %collective-permute-done.3, f32[8,128]{1,0:T(8,128)S(1)} %get-tuple-element.27), kind=kLoop, calls=%fused_computation | loop fusion | flops 3584 | bytes 18432 | tf_op jit(solution)/shard_map/div | solution.py:306
Async XLA Ops:
  1.0 4.8 %collective-permute-start = (bf16[8,1536]{1,0:T(8,128)(2,1)S(1)}, bf16[8,1536]{1,0:T(8,128)(2,1)S(1)}, u32[]{:S(2)}, u32[]{:S(2)}) collective-permute-start(bf16[8,1536]{1,0:T(8,128)(2,1)S(1)} %get-tuple-element.20), channel_id=1, source_target_pairs={{0,12},{4,8},{8,0},{12,4},{1,13},{5,9},{9,1},{13,5},{2,14},{6,10},... | collective-permute-start | bytes 73736 | tf_op jit(solution)/shard_map/ppermute | solution.py:34
  3.5 3.3 %collective-permute-start.1 = (bf16[8,1536]{1,0:T(8,128)(2,1)S(1)}, bf16[8,1536]{1,0:T(8,128)(2,1)S(1)}, u32[]{:S(2)}, u32[]{:S(2)}) collective-permute-start(bf16[8,1536]{1,0:T(8,128)(2,1)S(1)} %get-tuple-element.21), channel_id=1, source_target_pairs={{0,8},{4,12},{8,4},{12,0},{1,9},{5,13},{9,5},{13,1},{2,10},{6,14},... | collective-permute-start | bytes 73736 | tf_op jit(solution)/shard_map/ppermute | solution.py:34
  4.1 2.6 %collective-permute-start.2 = (bf16[8,1536]{1,0:T(8,128)(2,1)S(1)}, bf16[8,1536]{1,0:T(8,128)(2,1)S(1)}, u32[]{:S(2)}, u32[]{:S(2)}) collective-permute-start(bf16[8,1536]{1,0:T(8,128)(2,1)S(1)} %get-tuple-element.22), channel_id=1, source_target_pairs={{0,4},{4,0},{8,12},{12,8},{1,5},{5,1},{9,13},{13,9},{2,6},{6,2},{1... | collective-permute-start | bytes 73736 | tf_op jit(solution)/shard_map/ppermute | solution.py:34
  7.3 5.5 %collective-permute-start.3 = (f32[8,128]{1,0:T(8,128)S(1)}, f32[8,128]{1,0:T(8,128)S(1)}, u32[]{:S(2)}, u32[]{:S(2)}) collective-permute-start(f32[8,128]{1,0:T(8,128)S(1)} %get-tuple-element.28), channel_id=1, source_target_pairs={{0,2},{1,3},{2,1},{3,0},{4,6},{5,7},{6,5},{7,4},{8,10},{9,11},{10,... | collective-permute-start | bytes 12296 | tf_op jit(solution)/shard_map/ppermute | solution.py:34
  10.0 4.5 %collective-permute-start.4 = (f32[8,128]{1,0:T(8,128)S(1)}, f32[8,128]{1,0:T(8,128)S(1)}, u32[]{:S(2)}, u32[]{:S(2)}) collective-permute-start(f32[8,128]{1,0:T(8,128)S(1)} %get-tuple-element.29), channel_id=1, source_target_pairs={{0,3},{1,2},{2,0},{3,1},{4,7},{5,6},{6,4},{7,5},{8,11},{9,10},{10,... | collective-permute-start | bytes 12296 | tf_op jit(solution)/shard_map/ppermute | solution.py:34
  11.2 3.6 %collective-permute-start.5 = (f32[8,128]{1,0:T(8,128)S(1)}, f32[8,128]{1,0:T(8,128)S(1)}, u32[]{:S(2)}, u32[]{:S(2)}) collective-permute-start(f32[8,128]{1,0:T(8,128)S(1)} %get-tuple-element.30), channel_id=1, source_target_pairs={{0,1},{1,0},{2,3},{3,2},{4,5},{5,4},{6,7},{7,6},{8,9},{9,8},{10,11... | collective-permute-start | bytes 12296 | tf_op jit(solution)/shard_map/ppermute | solution.py:34

commit v7 on v6

--- a/solution.py
+++ b/solution.py
@@ -104,11 +104,9 @@
         source, slot = entries[j, m] // capacity, entries[j, m] % capacity
         for i in range(owners):
             slot = jnp.where(source == sources[i], slot % capacity + i * ROWS, slot)
-        for h in range(turns):
-            shift = shifts[j, m] + h * STEP
-            q = p * turns + h
-            table[q : q + 1, :] = jnp.full((1, LANES), slot + (shift // LANES) * owners * ROWS)
-            table[turns * pairs + q : turns * pairs + q + 1, :] = jnp.full((1, LANES), (LANES - shift % LANES) % LANES)
+        shift = shifts[j, m]
+        row_of = slot + (shift // LANES) * owners * ROWS
+        table[p : p + 1, :] = jnp.full((1, LANES), row_of * LANES + (LANES - shift % LANES) % LANES)
         weight = factors[j, m].astype(jnp.float32)
         scale[p * groups : (p + 1) * groups, :] = jnp.broadcast_to(factor[p : p + 1] * weight, (groups, LANES))
     turned = [
@@ -154,12 +152,16 @@
     places = table[...]
     lane = lax.broadcasted_iota(jnp.int32, (reach, LANES), 1)
     for p in range(pairs):
+        place = places[p, 0]
+        first, back = lax.shift_right_logical(place, 7), lax.bitwise_and(place, LANES - 1)
         for h in range(turns):
-            first = places[p * turns + h, 0]
-            back = places[turns * pairs + p * turns + h, 0]
-            low = pltpu.roll(lanes[pl.ds(first, reach, stride=stride), :], back, axis=1)
-            up = pltpu.roll(lanes[pl.ds(first + stride, reach, stride=stride), :], back, axis=1)
-            stacks[p, pl.ds(h, reach, stride=turns), :] = jnp.where((lane < back) | (back == 0), low, up)
+            if h:
+                first = jnp.where((back > 0) & (back <= STEP), first + stride, first)
+                back = lax.bitwise_xor(back, STEP)
+            low = lanes[pl.ds(first, reach, stride=stride), :]
+            up = lanes[pl.ds(first + stride, reach, stride=stride), :]
+            rest = lax.bitwise_and(LANES - back, LANES - 1)
+            stacks[p, pl.ds(h, reach, stride=turns), :] = pltpu.roll(jnp.where(lane >= rest, low, up), back, axis=1)
     taps = [
         jnp.concatenate([stacks[p, d * turns : d * turns + groups, :] for d in range(depth // LANES)], axis=1) for p in range(pairs)
     ]
@@ -258,7 +260,7 @@
             jax.ShapeDtypeStruct((depth, LANES), jnp.bfloat16),
             jax.ShapeDtypeStruct((pairs * groups, LANES), jnp.float32),
             jax.ShapeDtypeStruct((count, LANES), jnp.float32),
-            jax.ShapeDtypeStruct((2 * pairs * (LANES // STEP), LANES), jnp.int32),
+            jax.ShapeDtypeStruct((pairs, LANES), jnp.int32),
         ),
         [
             pltpu.VMEM((pairs, depth), jnp.float32),

time: 15.6 us -> 15.6 us (level)
  transfers between devices with their start and end apart: 6 -> 6, of which waited for: 5 -> 5; matrix products, arithmetic and copies ran while one was open for 0% -> 0% of each run, Pallas kernels for 10% -> 9%
where the time goes in v7:
time: 15.6 us; the launch traced here: 15.4 us
  starting transfers between devices  7.37 us (47%)
  waiting for transfers between devices  4.35 us (28%)
  Pallas kernels  3.07 us (20%)
  other arithmetic  0.59 us (4%)
    ppermute x6, starting transfers between devices, send(): return lax.ppermute(value, axis, list(enumerate(route)))  7.37 us
    ppermute x6, waiting for transfers between devices, send(): return lax.ppermute(value, axis, list(enumerate(route)))  4.35 us
    pallas_call x3, Pallas kernels, call(): pl.pallas_call(kernel, out_shape=outs, in_specs=[ins] * len(arguments), o...  3.07 us
    div x1, other arithmetic, shards(): return top / jnp.sqrt(sum((x[count:] for x in own)))  0.59 us
  transfers between devices with their start and end apart: 6, of which 5 were waited for; matrix products, arithmetic and copies ran while one was open for 0% of the time, Pallas kernels for 9%

profile of v7, /device:TPU:0, one launch (start us, length us, event | category | flops | bytes accessed | tf_op | source)
XLA Modules:
  0.0 15.4 jit_solution(18007176025418648002)
XLA Ops:
  0.0 1.0 %pack.1 = (bf16[8,1536]{1,0:T(8,128)(2,1)S(1)}, bf16[8,1536]{1,0:T(8,128)(2,1)S(1)}, bf16[8,1536]{1,0:T(8,128)(2,1)S(1)}, bf16[8,1536]{1,0:T(8,128)(2,1)S(1)}) custom-call(bf16[12,1536]{1,0:T(8,128)(2,1)} %waveforms.1, s32[1,1,4,6]{3,2,1,0:T(4,128)} %selection.1), custom_call_target="tpu_custom_call" | custom-call | tf_op jit(solution)/shard_map/pack/pallas_call | solution.py:230
  1.0 2.4 %collective-permute-start = (bf16[8,1536]{1,0:T(8,128)(2,1)S(1)}, bf16[8,1536]{1,0:T(8,128)(2,1)S(1)}, u32[]{:S(2)}, u32[]{:S(2)}) collective-permute-start(bf16[8,1536]{1,0:T(8,128)(2,1)S(1)} %get-tuple-element.20), channel_id=1, source_target_pairs={{0,12},{4,8},{8,0},{12,4},{1,13},{5,9},{9,1},{13,5},{2,14},{6,10},... | collective-permute-start | bytes 73736 | tf_op jit(solution)/shard_map/ppermute | solution.py:34
  3.5 0.6 %collective-permute-start.1 = (bf16[8,1536]{1,0:T(8,128)(2,1)S(1)}, bf16[8,1536]{1,0:T(8,128)(2,1)S(1)}, u32[]{:S(2)}, u32[]{:S(2)}) collective-permute-start(bf16[8,1536]{1,0:T(8,128)(2,1)S(1)} %get-tuple-element.21), channel_id=1, source_target_pairs={{0,8},{4,12},{8,4},{12,0},{1,9},{5,13},{9,5},{13,1},{2,10},{6,14},... | collective-permute-start | bytes 73736 | tf_op jit(solution)/shard_map/ppermute | solution.py:34
  4.1 0.1 collective-permute-start.2
  4.1 1.4 %prepare.1 = (bf16[768,512]{1,0:T(8,128)(2,1)S(1)}, bf16[768,128]{1,0:T(8,128)(2,1)S(1)}, f32[64,128]{1,0:T(8,128)S(1)}, f32[4,128]{1,0:T(4,128)S(1)}, s32[8,128]{1,0:T(8,128)S(1)}) custom-call(bf16[4,2,600]{2,1,0:T(2,128)(2,1)} %templates.1, s32[2,4]{1,0:T(2,128)} %bitcast.3, s32[2,4]{1,0:T(2,128)} %bitcast.4, s32[2,4]{1,0:T(2,128)} %bitcast.5), custom_call_target="tpu_custom_call" | custom-call | flops 2000000 | bytes 2000000 | tf_op jit(solution)/shard_map/prepare/pallas_call | solution.py:230
  5.6 0.2 %collective-permute-done.refs_1_ = bf16[8,1536]{1,0:T(8,128)(2,1)S(1)} collective-permute-done((bf16[8,1536]{1,0:T(8,128)(2,1)S(1)}, bf16[8,1536]{1,0:T(8,128)(2,1)S(1)}, u32[]{:S(2)}, u32[]{:S(2)}) %collective-permute-start) | collective-permute-done | bytes 24608 | tf_op jit(solution)/shard_map/ppermute | solution.py:34
  5.8 0.9 %collective-permute-done.1.refs_2_ = bf16[8,1536]{1,0:T(8,128)(2,1)S(1)} collective-permute-done((bf16[8,1536]{1,0:T(8,128)(2,1)S(1)}, bf16[8,1536]{1,0:T(8,128)(2,1)S(1)}, u32[]{:S(2)}, u32[]{:S(2)}) %collective-permute-start.1) | collective-permute-done | bytes 24608 | tf_op jit(solution)/shard_map/ppermute | solution.py:34
  6.7 0.0 collective-permute-done.2.refs_3_
  6.7 0.6 %correlate.1 = (f32[8,128]{1,0:T(8,128)S(1)}, f32[8,128]{1,0:T(8,128)S(1)}, f32[8,128]{1,0:T(8,128)S(1)}, f32[8,128]{1,0:T(8,128)S(1)}) custom-call(s32[8,128]{1,0:T(8,128)S(1)} %get-tuple-element.18.table, bf16[8,1536]{1,0:T(8,128)(2,1)S(1)} %get-tuple-element.19.refs_0_, bf16[8,1536]{1,0:T(8,128)(2,1)S(1)} %collective-permute-done.refs_1_, ...), custom_call_target="tpu_custom_call" | custom-call | tf_op jit(solution)/shard_map/correlate/pallas_call | solution.py:230
  7.3 2.6 %collective-permute-start.3 = (f32[8,128]{1,0:T(8,128)S(1)}, f32[8,128]{1,0:T(8,128)S(1)}, u32[]{:S(2)}, u32[]{:S(2)}) collective-permute-start(f32[8,128]{1,0:T(8,128)S(1)} %get-tuple-element.28), channel_id=1, source_target_pairs={{0,2},{1,3},{2,1},{3,0},{4,6},{5,7},{6,5},{7,4},{8,10},{9,11},{10,... | collective-permute-start | bytes 12296 | tf_op jit(solution)/shard_map/ppermute | solution.py:34
  10.0 1.2 %collective-permute-start.4 = (f32[8,128]{1,0:T(8,128)S(1)}, f32[8,128]{1,0:T(8,128)S(1)}, u32[]{:S(2)}, u32[]{:S(2)}) collective-permute-start(f32[8,128]{1,0:T(8,128)S(1)} %get-tuple-element.29), channel_id=1, source_target_pairs={{0,3},{1,2},{2,0},{3,1},{4,7},{5,6},{6,4},{7,5},{8,11},{9,10},{10,... | collective-permute-start | bytes 12296 | tf_op jit(solution)/shard_map/ppermute | solution.py:34
  11.2 0.4 %collective-permute-start.5 = (f32[8,128]{1,0:T(8,128)S(1)}, f32[8,128]{1,0:T(8,128)S(1)}, u32[]{:S(2)}, u32[]{:S(2)}) collective-permute-start(f32[8,128]{1,0:T(8,128)S(1)} %get-tuple-element.30), channel_id=1, source_target_pairs={{0,1},{1,0},{2,3},{3,2},{4,5},{5,4},{6,7},{7,6},{8,9},{9,8},{10,11... | collective-permute-start | bytes 12296 | tf_op jit(solution)/shard_map/ppermute | solution.py:34
  11.6 1.2 %collective-permute-done.3 = f32[8,128]{1,0:T(8,128)S(1)} collective-permute-done((f32[8,128]{1,0:T(8,128)S(1)}, f32[8,128]{1,0:T(8,128)S(1)}, u32[]{:S(2)}, u32[]{:S(2)}) %collective-permute-start.3) | collective-permute-done | bytes 4128 | tf_op jit(solution)/shard_map/ppermute | solution.py:34
  12.8 1.7 %collective-permute-done.4 = f32[8,128]{1,0:T(8,128)S(1)} collective-permute-done((f32[8,128]{1,0:T(8,128)S(1)}, f32[8,128]{1,0:T(8,128)S(1)}, u32[]{:S(2)}, u32[]{:S(2)}) %collective-permute-start.4) | collective-permute-done | bytes 4128 | tf_op jit(solution)/shard_map/ppermute | solution.py:34
  14.5 0.3 %collective-permute-done.5 = f32[8,128]{1,0:T(8,128)S(1)} collective-permute-done((f32[8,128]{1,0:T(8,128)S(1)}, f32[8,128]{1,0:T(8,128)S(1)}, u32[]{:S(2)}, u32[]{:S(2)}) %collective-permute-start.5) | collective-permute-done | bytes 4128 | tf_op jit(solution)/shard_map/ppermute | solution.py:34
  14.8 0.6 %rsqrt_multiply_fusion = f32[4,128]{1,0:T(4,128)} fusion(f32[8,128]{1,0:T(8,128)S(1)} %collective-permute-done.5, f32[8,128]{1,0:T(8,128)S(1)} %collective-permute-done.4, f32[8,128]{1,0:T(8,128)S(1)} %collective-permute-done.3, f32[8,128]{1,0:T(8,128)S(1)} %get-tuple-element.27), kind=kLoop, calls=%fused_computation | loop fusion | flops 3584 | bytes 18432 | tf_op jit(solution)/shard_map/div | solution.py:308
Async XLA Ops:
  1.0 4.8 %collective-permute-start = (bf16[8,1536]{1,0:T(8,128)(2,1)S(1)}, bf16[8,1536]{1,0:T(8,128)(2,1)S(1)}, u32[]{:S(2)}, u32[]{:S(2)}) collective-permute-start(bf16[8,1536]{1,0:T(8,128)(2,1)S(1)} %get-tuple-element.20), channel_id=1, source_target_pairs={{0,12},{4,8},{8,0},{12,4},{1,13},{5,9},{9,1},{13,5},{2,14},{6,10},... | collective-permute-start | bytes 73736 | tf_op jit(solution)/shard_map/ppermute | solution.py:34
  3.5 3.3 %collective-permute-start.1 = (bf16[8,1536]{1,0:T(8,128)(2,1)S(1)}, bf16[8,1536]{1,0:T(8,128)(2,1)S(1)}, u32[]{:S(2)}, u32[]{:S(2)}) collective-permute-start(bf16[8,1536]{1,0:T(8,128)(2,1)S(1)} %get-tuple-element.21), channel_id=1, source_target_pairs={{0,8},{4,12},{8,4},{12,0},{1,9},{5,13},{9,5},{13,1},{2,10},{6,14},... | collective-permute-start | bytes 73736 | tf_op jit(solution)/shard_map/ppermute | solution.py:34
  4.1 2.6 %collective-permute-start.2 = (bf16[8,1536]{1,0:T(8,128)(2,1)S(1)}, bf16[8,1536]{1,0:T(8,128)(2,1)S(1)}, u32[]{:S(2)}, u32[]{:S(2)}) collective-permute-start(bf16[8,1536]{1,0:T(8,128)(2,1)S(1)} %get-tuple-element.22), channel_id=1, source_target_pairs={{0,4},{4,0},{8,12},{12,8},{1,5},{5,1},{9,13},{13,9},{2,6},{6,2},{1... | collective-permute-start | bytes 73736 | tf_op jit(solution)/shard_map/ppermute | solution.py:34
  7.3 5.5 %collective-permute-start.3 = (f32[8,128]{1,0:T(8,128)S(1)}, f32[8,128]{1,0:T(8,128)S(1)}, u32[]{:S(2)}, u32[]{:S(2)}) collective-permute-start(f32[8,128]{1,0:T(8,128)S(1)} %get-tuple-element.28), channel_id=1, source_target_pairs={{0,2},{1,3},{2,1},{3,0},{4,6},{5,7},{6,5},{7,4},{8,10},{9,11},{10,... | collective-permute-start | bytes 12296 | tf_op jit(solution)/shard_map/ppermute | solution.py:34
  10.0 4.5 %collective-permute-start.4 = (f32[8,128]{1,0:T(8,128)S(1)}, f32[8,128]{1,0:T(8,128)S(1)}, u32[]{:S(2)}, u32[]{:S(2)}) collective-permute-start(f32[8,128]{1,0:T(8,128)S(1)} %get-tuple-element.29), channel_id=1, source_target_pairs={{0,3},{1,2},{2,0},{3,1},{4,7},{5,6},{6,4},{7,5},{8,11},{9,10},{10,... | collective-permute-start | bytes 12296 | tf_op jit(solution)/shard_map/ppermute | solution.py:34
  11.2 3.6 %collective-permute-start.5 = (f32[8,128]{1,0:T(8,128)S(1)}, f32[8,128]{1,0:T(8,128)S(1)}, u32[]{:S(2)}, u32[]{:S(2)}) collective-permute-start(f32[8,128]{1,0:T(8,128)S(1)} %get-tuple-element.30), channel_id=1, source_target_pairs={{0,1},{1,0},{2,3},{3,2},{4,5},{5,4},{6,7},{7,6},{8,9},{9,8},{10,11... | collective-permute-start | bytes 12296 | tf_op jit(solution)/shard_map/ppermute | solution.py:34

commit v8 on v7

--- a/solution.py
+++ b/solution.py
@@ -166,13 +166,13 @@
         jnp.concatenate([stacks[p, d * turns : d * turns + groups, :] for d in range(depth // LANES)], axis=1) for p in range(pairs)
     ]
     taps = jnp.concatenate(taps, axis=0)
+    product = jnp.dot(taps.astype(jnp.bfloat16), bands[...], preferred_element_type=jnp.float32)
     square = taps * taps
     main = square.astype(jnp.bfloat16)
     left = (square - main.astype(jnp.float32)).astype(jnp.bfloat16)
     energy = jnp.dot(jnp.concatenate([main, left], axis=0), box[...], preferred_element_type=jnp.float32)
     energy = energy[: pairs * groups] + energy[pairs * groups :]
     norm = scale[...] * lax.rsqrt(energy * (1.0 / tlen) + EPS)
-    product = jnp.dot(taps.astype(jnp.bfloat16), bands[...], preferred_element_type=jnp.float32)
     front = lax.broadcasted_iota(jnp.int32, (LAGS // LANES, LANES), 1) < STEP
     for m in range(count):
         both = jnp.zeros((groups, LANES), jnp.float32)

time: 15.6 us -> 15.6 us (level)
  no operation moved by 1% of the time
where the time goes in v8:
time: 15.6 us; the launch traced here: 15.4 us
  starting transfers between devices  7.32 us (47%)
  waiting for transfers between devices  4.39 us (28%)
  Pallas kernels  3.07 us (20%)
  other arithmetic  0.59 us (4%)
    ppermute x6, starting transfers between devices, send(): return lax.ppermute(value, axis, list(enumerate(route)))  7.32 us
    ppermute x6, waiting for transfers between devices, send(): return lax.ppermute(value, axis, list(enumerate(route)))  4.39 us
    pallas_call x3, Pallas kernels, call(): pl.pallas_call(kernel, out_shape=outs, in_specs=[ins] * len(arguments), o...  3.07 us
    div x1, other arithmetic, shards(): return top / jnp.sqrt(sum((x[count:] for x in own)))  0.59 us
  transfers between devices with their start and end apart: 6, of which 5 were waited for; matrix products, arithmetic and copies ran while one was open for 0% of the time, Pallas kernels for 9%

profile of v8, /device:TPU:0, one launch (start us, length us, event | category | flops | bytes accessed | tf_op | source)
XLA Modules:
  0.0 15.4 jit_solution(743079680497587196)
XLA Ops:
  0.0 1.0 %pack.1 = (bf16[8,1536]{1,0:T(8,128)(2,1)S(1)}, bf16[8,1536]{1,0:T(8,128)(2,1)S(1)}, bf16[8,1536]{1,0:T(8,128)(2,1)S(1)}, bf16[8,1536]{1,0:T(8,128)(2,1)S(1)}) custom-call(bf16[12,1536]{1,0:T(8,128)(2,1)} %waveforms.1, s32[1,1,4,6]{3,2,1,0:T(4,128)} %selection.1), custom_call_target="tpu_custom_call" | custom-call | tf_op jit(solution)/shard_map/pack/pallas_call | solution.py:230
  1.0 2.4 %collective-permute-start = (bf16[8,1536]{1,0:T(8,128)(2,1)S(1)}, bf16[8,1536]{1,0:T(8,128)(2,1)S(1)}, u32[]{:S(2)}, u32[]{:S(2)}) collective-permute-start(bf16[8,1536]{1,0:T(8,128)(2,1)S(1)} %get-tuple-element.20), channel_id=1, source_target_pairs={{0,12},{4,8},{8,0},{12,4},{1,13},{5,9},{9,1},{13,5},{2,14},{6,10},... | collective-permute-start | bytes 73736 | tf_op jit(solution)/shard_map/ppermute | solution.py:34
  3.5 0.6 %collective-permute-start.1 = (bf16[8,1536]{1,0:T(8,128)(2,1)S(1)}, bf16[8,1536]{1,0:T(8,128)(2,1)S(1)}, u32[]{:S(2)}, u32[]{:S(2)}) collective-permute-start(bf16[8,1536]{1,0:T(8,128)(2,1)S(1)} %get-tuple-element.21), channel_id=1, source_target_pairs={{0,8},{4,12},{8,4},{12,0},{1,9},{5,13},{9,5},{13,1},{2,10},{6,14},... | collective-permute-start | bytes 73736 | tf_op jit(solution)/shard_map/ppermute | solution.py:34
  4.1 0.1 collective-permute-start.2
  4.1 1.4 %prepare.1 = (bf16[768,512]{1,0:T(8,128)(2,1)S(1)}, bf16[768,128]{1,0:T(8,128)(2,1)S(1)}, f32[64,128]{1,0:T(8,128)S(1)}, f32[4,128]{1,0:T(4,128)S(1)}, s32[8,128]{1,0:T(8,128)S(1)}) custom-call(bf16[4,2,600]{2,1,0:T(2,128)(2,1)} %templates.1, s32[2,4]{1,0:T(2,128)} %bitcast.3, s32[2,4]{1,0:T(2,128)} %bitcast.4, s32[2,4]{1,0:T(2,128)} %bitcast.5), custom_call_target="tpu_custom_call" | custom-call | flops 2000000 | bytes 2000000 | tf_op jit(solution)/shard_map/prepare/pallas_call | solution.py:230
  5.6 0.2 %collective-permute-done.refs_1_ = bf16[8,1536]{1,0:T(8,128)(2,1)S(1)} collective-permute-done((bf16[8,1536]{1,0:T(8,128)(2,1)S(1)}, bf16[8,1536]{1,0:T(8,128)(2,1)S(1)}, u32[]{:S(2)}, u32[]{:S(2)}) %collective-permute-start) | collective-permute-done | bytes 24608 | tf_op jit(solution)/shard_map/ppermute | solution.py:34
  5.8 0.9 %collective-permute-done.1.refs_2_ = bf16[8,1536]{1,0:T(8,128)(2,1)S(1)} collective-permute-done((bf16[8,1536]{1,0:T(8,128)(2,1)S(1)}, bf16[8,1536]{1,0:T(8,128)(2,1)S(1)}, u32[]{:S(2)}, u32[]{:S(2)}) %collective-permute-start.1) | collective-permute-done | bytes 24608 | tf_op jit(solution)/shard_map/ppermute | solution.py:34
  6.7 0.0 collective-permute-done.2.refs_3_
  6.7 0.6 %correlate.1 = (f32[8,128]{1,0:T(8,128)S(1)}, f32[8,128]{1,0:T(8,128)S(1)}, f32[8,128]{1,0:T(8,128)S(1)}, f32[8,128]{1,0:T(8,128)S(1)}) custom-call(s32[8,128]{1,0:T(8,128)S(1)} %get-tuple-element.18.table, bf16[8,1536]{1,0:T(8,128)(2,1)S(1)} %get-tuple-element.19.refs_0_, bf16[8,1536]{1,0:T(8,128)(2,1)S(1)} %collective-permute-done.refs_1_, ...), custom_call_target="tpu_custom_call" | custom-call | tf_op jit(solution)/shard_map/correlate/pallas_call | solution.py:230
  7.3 2.6 %collective-permute-start.3 = (f32[8,128]{1,0:T(8,128)S(1)}, f32[8,128]{1,0:T(8,128)S(1)}, u32[]{:S(2)}, u32[]{:S(2)}) collective-permute-start(f32[8,128]{1,0:T(8,128)S(1)} %get-tuple-element.28), channel_id=1, source_target_pairs={{0,2},{1,3},{2,1},{3,0},{4,6},{5,7},{6,5},{7,4},{8,10},{9,11},{10,... | collective-permute-start | bytes 12296 | tf_op jit(solution)/shard_map/ppermute | solution.py:34
  10.0 1.2 %collective-permute-start.4 = (f32[8,128]{1,0:T(8,128)S(1)}, f32[8,128]{1,0:T(8,128)S(1)}, u32[]{:S(2)}, u32[]{:S(2)}) collective-permute-start(f32[8,128]{1,0:T(8,128)S(1)} %get-tuple-element.29), channel_id=1, source_target_pairs={{0,3},{1,2},{2,0},{3,1},{4,7},{5,6},{6,4},{7,5},{8,11},{9,10},{10,... | collective-permute-start | bytes 12296 | tf_op jit(solution)/shard_map/ppermute | solution.py:34
  11.2 0.3 %collective-permute-start.5 = (f32[8,128]{1,0:T(8,128)S(1)}, f32[8,128]{1,0:T(8,128)S(1)}, u32[]{:S(2)}, u32[]{:S(2)}) collective-permute-start(f32[8,128]{1,0:T(8,128)S(1)} %get-tuple-element.30), channel_id=1, source_target_pairs={{0,1},{1,0},{2,3},{3,2},{4,5},{5,4},{6,7},{7,6},{8,9},{9,8},{10,11... | collective-permute-start | bytes 12296 | tf_op jit(solution)/shard_map/ppermute | solution.py:34
  11.5 1.2 %collective-permute-done.3 = f32[8,128]{1,0:T(8,128)S(1)} collective-permute-done((f32[8,128]{1,0:T(8,128)S(1)}, f32[8,128]{1,0:T(8,128)S(1)}, u32[]{:S(2)}, u32[]{:S(2)}) %collective-permute-start.3) | collective-permute-done | bytes 4128 | tf_op jit(solution)/shard_map/ppermute | solution.py:34
  12.8 1.7 %collective-permute-done.4 = f32[8,128]{1,0:T(8,128)S(1)} collective-permute-done((f32[8,128]{1,0:T(8,128)S(1)}, f32[8,128]{1,0:T(8,128)S(1)}, u32[]{:S(2)}, u32[]{:S(2)}) %collective-permute-start.4) | collective-permute-done | bytes 4128 | tf_op jit(solution)/shard_map/ppermute | solution.py:34
  14.5 0.3 %collective-permute-done.5 = f32[8,128]{1,0:T(8,128)S(1)} collective-permute-done((f32[8,128]{1,0:T(8,128)S(1)}, f32[8,128]{1,0:T(8,128)S(1)}, u32[]{:S(2)}, u32[]{:S(2)}) %collective-permute-start.5) | collective-permute-done | bytes 4128 | tf_op jit(solution)/shard_map/ppermute | solution.py:34
  14.8 0.6 %rsqrt_multiply_fusion = f32[4,128]{1,0:T(4,128)} fusion(f32[8,128]{1,0:T(8,128)S(1)} %collective-permute-done.5, f32[8,128]{1,0:T(8,128)S(1)} %collective-permute-done.4, f32[8,128]{1,0:T(8,128)S(1)} %collective-permute-done.3, f32[8,128]{1,0:T(8,128)S(1)} %get-tuple-element.27), kind=kLoop, calls=%fused_computation | loop fusion | flops 3584 | bytes 18432 | tf_op jit(solution)/shard_map/div | solution.py:308
Async XLA Ops:
  1.0 4.8 %collective-permute-start = (bf16[8,1536]{1,0:T(8,128)(2,1)S(1)}, bf16[8,1536]{1,0:T(8,128)(2,1)S(1)}, u32[]{:S(2)}, u32[]{:S(2)}) collective-permute-start(bf16[8,1536]{1,0:T(8,128)(2,1)S(1)} %get-tuple-element.20), channel_id=1, source_target_pairs={{0,12},{4,8},{8,0},{12,4},{1,13},{5,9},{9,1},{13,5},{2,14},{6,10},... | collective-permute-start | bytes 73736 | tf_op jit(solution)/shard_map/ppermute | solution.py:34
  3.5 3.3 %collective-permute-start.1 = (bf16[8,1536]{1,0:T(8,128)(2,1)S(1)}, bf16[8,1536]{1,0:T(8,128)(2,1)S(1)}, u32[]{:S(2)}, u32[]{:S(2)}) collective-permute-start(bf16[8,1536]{1,0:T(8,128)(2,1)S(1)} %get-tuple-element.21), channel_id=1, source_target_pairs={{0,8},{4,12},{8,4},{12,0},{1,9},{5,13},{9,5},{13,1},{2,10},{6,14},... | collective-permute-start | bytes 73736 | tf_op jit(solution)/shard_map/ppermute | solution.py:34
  4.1 2.6 %collective-permute-start.2 = (bf16[8,1536]{1,0:T(8,128)(2,1)S(1)}, bf16[8,1536]{1,0:T(8,128)(2,1)S(1)}, u32[]{:S(2)}, u32[]{:S(2)}) collective-permute-start(bf16[8,1536]{1,0:T(8,128)(2,1)S(1)} %get-tuple-element.22), channel_id=1, source_target_pairs={{0,4},{4,0},{8,12},{12,8},{1,5},{5,1},{9,13},{13,9},{2,6},{6,2},{1... | collective-permute-start | bytes 73736 | tf_op jit(solution)/shard_map/ppermute | solution.py:34
  7.3 5.5 %collective-permute-start.3 = (f32[8,128]{1,0:T(8,128)S(1)}, f32[8,128]{1,0:T(8,128)S(1)}, u32[]{:S(2)}, u32[]{:S(2)}) collective-permute-start(f32[8,128]{1,0:T(8,128)S(1)} %get-tuple-element.28), channel_id=1, source_target_pairs={{0,2},{1,3},{2,1},{3,0},{4,6},{5,7},{6,5},{7,4},{8,10},{9,11},{10,... | collective-permute-start | bytes 12296 | tf_op jit(solution)/shard_map/ppermute | solution.py:34
  10.0 4.5 %collective-permute-start.4 = (f32[8,128]{1,0:T(8,128)S(1)}, f32[8,128]{1,0:T(8,128)S(1)}, u32[]{:S(2)}, u32[]{:S(2)}) collective-permute-start(f32[8,128]{1,0:T(8,128)S(1)} %get-tuple-element.29), channel_id=1, source_target_pairs={{0,3},{1,2},{2,0},{3,1},{4,7},{5,6},{6,4},{7,5},{8,11},{9,10},{10,... | collective-permute-start | bytes 12296 | tf_op jit(solution)/shard_map/ppermute | solution.py:34
  11.2 3.6 %collective-permute-start.5 = (f32[8,128]{1,0:T(8,128)S(1)}, f32[8,128]{1,0:T(8,128)S(1)}, u32[]{:S(2)}, u32[]{:S(2)}) collective-permute-start(f32[8,128]{1,0:T(8,128)S(1)} %get-tuple-element.30), channel_id=1, source_target_pairs={{0,1},{1,0},{2,3},{3,2},{4,5},{5,4},{6,7},{7,6},{8,9},{9,8},{10,11... | collective-permute-start | bytes 12296 | tf_op jit(solution)/shard_map/ppermute | solution.py:34

commit v9 on v8

--- a/solution.py
+++ b/solution.py
@@ -165,12 +165,13 @@
     taps = [
         jnp.concatenate([stacks[p, d * turns : d * turns + groups, :] for d in range(depth // LANES)], axis=1) for p in range(pairs)
     ]
-    taps = jnp.concatenate(taps, axis=0)
-    product = jnp.dot(taps.astype(jnp.bfloat16), bands[...], preferred_element_type=jnp.float32)
+    used = -(-(tlen + STEP - 1) // 16) * 16
+    taps = jnp.concatenate(taps, axis=0)[:, :used]
+    product = jnp.dot(taps.astype(jnp.bfloat16), bands[:used, :], preferred_element_type=jnp.float32)
     square = taps * taps
     main = square.astype(jnp.bfloat16)
     left = (square - main.astype(jnp.float32)).astype(jnp.bfloat16)
-    energy = jnp.dot(jnp.concatenate([main, left], axis=0), box[...], preferred_element_type=jnp.float32)
+    energy = jnp.dot(jnp.concatenate([main, left], axis=0), box[:used, :], preferred_element_type=jnp.float32)
     energy = energy[: pairs * groups] + energy[pairs * groups :]
     norm = scale[...] * lax.rsqrt(energy * (1.0 / tlen) + EPS)
     front = lax.broadcasted_iota(jnp.int32, (LAGS // LANES, LANES), 1) < STEP

time: 15.6 us -> 15.6 us (level)
  no operation moved by 1% of the time
where the time goes in v9:
time: 15.6 us; the launch traced here: 15.4 us
  starting transfers between devices  7.35 us (47%)
  waiting for transfers between devices  4.36 us (28%)
  Pallas kernels  3.05 us (20%)
  other arithmetic  0.59 us (4%)
    ppermute x6, starting transfers between devices, send(): return lax.ppermute(value, axis, list(enumerate(route)))  7.35 us
    ppermute x6, waiting for transfers between devices, send(): return lax.ppermute(value, axis, list(enumerate(route)))  4.36 us
    pallas_call x3, Pallas kernels, call(): pl.pallas_call(kernel, out_shape=outs, in_specs=[ins] * len(arguments), o...  3.05 us
    div x1, other arithmetic, shards(): return top / jnp.sqrt(sum((x[count:] for x in own)))  0.59 us
  transfers between devices with their start and end apart: 6, of which 5 were waited for; matrix products, arithmetic and copies ran while one was open for 0% of the time, Pallas kernels for 9%

profile of v9, /device:TPU:0, one launch (start us, length us, event | category | flops | bytes accessed | tf_op | source)
XLA Modules:
  0.0 15.4 jit_solution(11846300831211925097)
XLA Ops:
  0.0 1.0 %pack.1 = (bf16[8,1536]{1,0:T(8,128)(2,1)S(1)}, bf16[8,1536]{1,0:T(8,128)(2,1)S(1)}, bf16[8,1536]{1,0:T(8,128)(2,1)S(1)}, bf16[8,1536]{1,0:T(8,128)(2,1)S(1)}) custom-call(bf16[12,1536]{1,0:T(8,128)(2,1)} %waveforms.1, s32[1,1,4,6]{3,2,1,0:T(4,128)} %selection.1), custom_call_target="tpu_custom_call" | custom-call | tf_op jit(solution)/shard_map/pack/pallas_call | solution.py:231
  1.0 2.4 %collective-permute-start = (bf16[8,1536]{1,0:T(8,128)(2,1)S(1)}, bf16[8,1536]{1,0:T(8,128)(2,1)S(1)}, u32[]{:S(2)}, u32[]{:S(2)}) collective-permute-start(bf16[8,1536]{1,0:T(8,128)(2,1)S(1)} %get-tuple-element.20), channel_id=1, source_target_pairs={{0,12},{4,8},{8,0},{12,4},{1,13},{5,9},{9,1},{13,5},{2,14},{6,10},... | collective-permute-start | bytes 73736 | tf_op jit(solution)/shard_map/ppermute | solution.py:34
  3.5 0.6 %collective-permute-start.1 = (bf16[8,1536]{1,0:T(8,128)(2,1)S(1)}, bf16[8,1536]{1,0:T(8,128)(2,1)S(1)}, u32[]{:S(2)}, u32[]{:S(2)}) collective-permute-start(bf16[8,1536]{1,0:T(8,128)(2,1)S(1)} %get-tuple-element.21), channel_id=1, source_target_pairs={{0,8},{4,12},{8,4},{12,0},{1,9},{5,13},{9,5},{13,1},{2,10},{6,14},... | collective-permute-start | bytes 73736 | tf_op jit(solution)/shard_map/ppermute | solution.py:34
  4.1 0.1 collective-permute-start.2
  4.1 1.4 %prepare.1 = (bf16[768,512]{1,0:T(8,128)(2,1)S(1)}, bf16[768,128]{1,0:T(8,128)(2,1)S(1)}, f32[64,128]{1,0:T(8,128)S(1)}, f32[4,128]{1,0:T(4,128)S(1)}, s32[8,128]{1,0:T(8,128)S(1)}) custom-call(bf16[4,2,600]{2,1,0:T(2,128)(2,1)} %templates.1, s32[2,4]{1,0:T(2,128)} %bitcast.3, s32[2,4]{1,0:T(2,128)} %bitcast.4, s32[2,4]{1,0:T(2,128)} %bitcast.5), custom_call_target="tpu_custom_call" | custom-call | flops 2000000 | bytes 2000000 | tf_op jit(solution)/shard_map/prepare/pallas_call | solution.py:231
  5.6 0.2 %collective-permute-done.refs_1_ = bf16[8,1536]{1,0:T(8,128)(2,1)S(1)} collective-permute-done((bf16[8,1536]{1,0:T(8,128)(2,1)S(1)}, bf16[8,1536]{1,0:T(8,128)(2,1)S(1)}, u32[]{:S(2)}, u32[]{:S(2)}) %collective-permute-start) | collective-permute-done | bytes 24608 | tf_op jit(solution)/shard_map/ppermute | solution.py:34
  5.8 0.9 %collective-permute-done.1.refs_2_ = bf16[8,1536]{1,0:T(8,128)(2,1)S(1)} collective-permute-done((bf16[8,1536]{1,0:T(8,128)(2,1)S(1)}, bf16[8,1536]{1,0:T(8,128)(2,1)S(1)}, u32[]{:S(2)}, u32[]{:S(2)}) %collective-permute-start.1) | collective-permute-done | bytes 24608 | tf_op jit(solution)/shard_map/ppermute | solution.py:34
  6.7 0.0 collective-permute-done.2.refs_3_
  6.7 0.6 %correlate.1 = (f32[8,128]{1,0:T(8,128)S(1)}, f32[8,128]{1,0:T(8,128)S(1)}, f32[8,128]{1,0:T(8,128)S(1)}, f32[8,128]{1,0:T(8,128)S(1)}) custom-call(s32[8,128]{1,0:T(8,128)S(1)} %get-tuple-element.18.table, bf16[8,1536]{1,0:T(8,128)(2,1)S(1)} %get-tuple-element.19.refs_0_, bf16[8,1536]{1,0:T(8,128)(2,1)S(1)} %collective-permute-done.refs_1_, ...), custom_call_target="tpu_custom_call" | custom-call | tf_op jit(solution)/shard_map/correlate/pallas_call | solution.py:231
  7.3 2.6 %collective-permute-start.3 = (f32[8,128]{1,0:T(8,128)S(1)}, f32[8,128]{1,0:T(8,128)S(1)}, u32[]{:S(2)}, u32[]{:S(2)}) collective-permute-start(f32[8,128]{1,0:T(8,128)S(1)} %get-tuple-element.28), channel_id=1, source_target_pairs={{0,2},{1,3},{2,1},{3,0},{4,6},{5,7},{6,5},{7,4},{8,10},{9,11},{10,... | collective-permute-start | bytes 12296 | tf_op jit(solution)/shard_map/ppermute | solution.py:34
  9.9 1.2 %collective-permute-start.4 = (f32[8,128]{1,0:T(8,128)S(1)}, f32[8,128]{1,0:T(8,128)S(1)}, u32[]{:S(2)}, u32[]{:S(2)}) collective-permute-start(f32[8,128]{1,0:T(8,128)S(1)} %get-tuple-element.29), channel_id=1, source_target_pairs={{0,3},{1,2},{2,0},{3,1},{4,7},{5,6},{6,4},{7,5},{8,11},{9,10},{10,... | collective-permute-start | bytes 12296 | tf_op jit(solution)/shard_map/ppermute | solution.py:34
  11.2 0.4 %collective-permute-start.5 = (f32[8,128]{1,0:T(8,128)S(1)}, f32[8,128]{1,0:T(8,128)S(1)}, u32[]{:S(2)}, u32[]{:S(2)}) collective-permute-start(f32[8,128]{1,0:T(8,128)S(1)} %get-tuple-element.30), channel_id=1, source_target_pairs={{0,1},{1,0},{2,3},{3,2},{4,5},{5,4},{6,7},{7,6},{8,9},{9,8},{10,11... | collective-permute-start | bytes 12296 | tf_op jit(solution)/shard_map/ppermute | solution.py:34
  11.5 1.2 %collective-permute-done.3 = f32[8,128]{1,0:T(8,128)S(1)} collective-permute-done((f32[8,128]{1,0:T(8,128)S(1)}, f32[8,128]{1,0:T(8,128)S(1)}, u32[]{:S(2)}, u32[]{:S(2)}) %collective-permute-start.3) | collective-permute-done | bytes 4128 | tf_op jit(solution)/shard_map/ppermute | solution.py:34
  12.8 1.7 %collective-permute-done.4 = f32[8,128]{1,0:T(8,128)S(1)} collective-permute-done((f32[8,128]{1,0:T(8,128)S(1)}, f32[8,128]{1,0:T(8,128)S(1)}, u32[]{:S(2)}, u32[]{:S(2)}) %collective-permute-start.4) | collective-permute-done | bytes 4128 | tf_op jit(solution)/shard_map/ppermute | solution.py:34
  14.4 0.3 %collective-permute-done.5 = f32[8,128]{1,0:T(8,128)S(1)} collective-permute-done((f32[8,128]{1,0:T(8,128)S(1)}, f32[8,128]{1,0:T(8,128)S(1)}, u32[]{:S(2)}, u32[]{:S(2)}) %collective-permute-start.5) | collective-permute-done | bytes 4128 | tf_op jit(solution)/shard_map/ppermute | solution.py:34
  14.8 0.6 %rsqrt_multiply_fusion = f32[4,128]{1,0:T(4,128)} fusion(f32[8,128]{1,0:T(8,128)S(1)} %collective-permute-done.5, f32[8,128]{1,0:T(8,128)S(1)} %collective-permute-done.4, f32[8,128]{1,0:T(8,128)S(1)} %collective-permute-done.3, f32[8,128]{1,0:T(8,128)S(1)} %get-tuple-element.27), kind=kLoop, calls=%fused_computation | loop fusion | flops 3584 | bytes 18432 | tf_op jit(solution)/shard_map/div | solution.py:309
Async XLA Ops:
  1.0 4.8 %collective-permute-start = (bf16[8,1536]{1,0:T(8,128)(2,1)S(1)}, bf16[8,1536]{1,0:T(8,128)(2,1)S(1)}, u32[]{:S(2)}, u32[]{:S(2)}) collective-permute-start(bf16[8,1536]{1,0:T(8,128)(2,1)S(1)} %get-tuple-element.20), channel_id=1, source_target_pairs={{0,12},{4,8},{8,0},{12,4},{1,13},{5,9},{9,1},{13,5},{2,14},{6,10},... | collective-permute-start | bytes 73736 | tf_op jit(solution)/shard_map/ppermute | solution.py:34
  3.5 3.3 %collective-permute-start.1 = (bf16[8,1536]{1,0:T(8,128)(2,1)S(1)}, bf16[8,1536]{1,0:T(8,128)(2,1)S(1)}, u32[]{:S(2)}, u32[]{:S(2)}) collective-permute-start(bf16[8,1536]{1,0:T(8,128)(2,1)S(1)} %get-tuple-element.21), channel_id=1, source_target_pairs={{0,8},{4,12},{8,4},{12,0},{1,9},{5,13},{9,5},{13,1},{2,10},{6,14},... | collective-permute-start | bytes 73736 | tf_op jit(solution)/shard_map/ppermute | solution.py:34
  4.1 2.6 %collective-permute-start.2 = (bf16[8,1536]{1,0:T(8,128)(2,1)S(1)}, bf16[8,1536]{1,0:T(8,128)(2,1)S(1)}, u32[]{:S(2)}, u32[]{:S(2)}) collective-permute-start(bf16[8,1536]{1,0:T(8,128)(2,1)S(1)} %get-tuple-element.22), channel_id=1, source_target_pairs={{0,4},{4,0},{8,12},{12,8},{1,5},{5,1},{9,13},{13,9},{2,6},{6,2},{1... | collective-permute-start | bytes 73736 | tf_op jit(solution)/shard_map/ppermute | solution.py:34
  7.3 5.5 %collective-permute-start.3 = (f32[8,128]{1,0:T(8,128)S(1)}, f32[8,128]{1,0:T(8,128)S(1)}, u32[]{:S(2)}, u32[]{:S(2)}) collective-permute-start(f32[8,128]{1,0:T(8,128)S(1)} %get-tuple-element.28), channel_id=1, source_target_pairs={{0,2},{1,3},{2,1},{3,0},{4,6},{5,7},{6,5},{7,4},{8,10},{9,11},{10,... | collective-permute-start | bytes 12296 | tf_op jit(solution)/shard_map/ppermute | solution.py:34
  9.9 4.5 %collective-permute-start.4 = (f32[8,128]{1,0:T(8,128)S(1)}, f32[8,128]{1,0:T(8,128)S(1)}, u32[]{:S(2)}, u32[]{:S(2)}) collective-permute-start(f32[8,128]{1,0:T(8,128)S(1)} %get-tuple-element.29), channel_id=1, source_target_pairs={{0,3},{1,2},{2,0},{3,1},{4,7},{5,6},{6,4},{7,5},{8,11},{9,10},{10,... | collective-permute-start | bytes 12296 | tf_op jit(solution)/shard_map/ppermute | solution.py:34
  11.2 3.6 %collective-permute-start.5 = (f32[8,128]{1,0:T(8,128)S(1)}, f32[8,128]{1,0:T(8,128)S(1)}, u32[]{:S(2)}, u32[]{:S(2)}) collective-permute-start(f32[8,128]{1,0:T(8,128)S(1)} %get-tuple-element.30), channel_id=1, source_target_pairs={{0,1},{1,0},{2,3},{3,2},{4,5},{5,4},{6,7},{7,6},{8,9},{9,8},{10,11... | collective-permute-start | bytes 12296 | tf_op jit(solution)/shard_map/ppermute | solution.py:34

commit v10 on v9

--- a/solution.py
+++ b/solution.py
@@ -57,7 +57,8 @@
     tall = -(-high // 16) * 16
     row = lax.broadcasted_iota(jnp.int32, (ROWS, tall), 0)
     column = lax.broadcasted_iota(jnp.int32, (ROWS, tall), 1)
-    copies[1].wait()
+    for copy in copies:
+        copy.wait()
     picks = []
     for route in (tuple(range(owners)),) + routes("tmpl", owners):
         target = lookup(route, me)
@@ -66,7 +67,6 @@
             local = jnp.where(row == j, choice[0, 0, target, j], local)
         picks.append(jnp.where(local == column, 1.0, 0.0))
     picks = jnp.concatenate(picks, axis=0).astype(jnp.bfloat16)
-    copies[0].wait()
     records = jnp.pad(taken[...].astype(jnp.float32), ((0, tall - high), (0, 0))).astype(jnp.bfloat16)
     picked = jnp.dot(picks, records, preferred_element_type=jnp.float32)
     for i, out in enumerate(outs):
@@ -167,7 +167,10 @@
     ]
     used = -(-(tlen + STEP - 1) // 16) * 16
     taps = jnp.concatenate(taps, axis=0)[:, :used]
-    product = jnp.dot(taps.astype(jnp.bfloat16), bands[:used, :], preferred_element_type=jnp.float32)
+    short = taps.astype(jnp.bfloat16)
+    half = pairs * STEP // 2
+    product = [jnp.dot(short, bands[:used, i * half : (i + 1) * half], preferred_element_type=jnp.float32) for i in range(2)]
+    product = jnp.concatenate(product, axis=1)
     square = taps * taps
     main = square.astype(jnp.bfloat16)
     left = (square - main.astype(jnp.float32)).astype(jnp.bfloat16)

time: 15.6 us -> 15.6 us (level)
  no operation moved by 1% of the time
where the time goes in v10:
time: 15.6 us; the launch traced here: 15.4 us
  starting transfers between devices  7.33 us (47%)
  waiting for transfers between devices  4.38 us (28%)
  Pallas kernels  3.03 us (19%)
  other arithmetic  0.59 us (4%)
    ppermute x6, starting transfers between devices, send(): return lax.ppermute(value, axis, list(enumerate(route)))  7.33 us
    ppermute x6, waiting for transfers between devices, send(): return lax.ppermute(value, axis, list(enumerate(route)))  4.38 us
    pallas_call x3, Pallas kernels, call(): pl.pallas_call(kernel, out_shape=outs, in_specs=[ins] * len(arguments), o...  3.03 us
    div x1, other arithmetic, shards(): return top / jnp.sqrt(sum((x[count:] for x in own)))  0.59 us
  transfers between devices with their start and end apart: 6, of which 5 were waited for; matrix products, arithmetic and copies ran while one was open for 0% of the time, Pallas kernels for 9%

profile of v10, /device:TPU:0, one launch (start us, length us, event | category | flops | bytes accessed | tf_op | source)
XLA Modules:
  0.0 15.4 jit_solution(18132083929837507062)
XLA Ops:
  0.0 1.0 %pack.1 = (bf16[8,1536]{1,0:T(8,128)(2,1)S(1)}, bf16[8,1536]{1,0:T(8,128)(2,1)S(1)}, bf16[8,1536]{1,0:T(8,128)(2,1)S(1)}, bf16[8,1536]{1,0:T(8,128)(2,1)S(1)}) custom-call(bf16[12,1536]{1,0:T(8,128)(2,1)} %waveforms.1, s32[1,1,4,6]{3,2,1,0:T(4,128)} %selection.1), custom_call_target="tpu_custom_call" | custom-call | tf_op jit(solution)/shard_map/pack/pallas_call | solution.py:234
  1.0 2.4 %collective-permute-start = (bf16[8,1536]{1,0:T(8,128)(2,1)S(1)}, bf16[8,1536]{1,0:T(8,128)(2,1)S(1)}, u32[]{:S(2)}, u32[]{:S(2)}) collective-permute-start(bf16[8,1536]{1,0:T(8,128)(2,1)S(1)} %get-tuple-element.20), channel_id=1, source_target_pairs={{0,12},{4,8},{8,0},{12,4},{1,13},{5,9},{9,1},{13,5},{2,14},{6,10},... | collective-permute-start | bytes 73736 | tf_op jit(solution)/shard_map/ppermute | solution.py:34
  3.4 0.6 %collective-permute-start.1 = (bf16[8,1536]{1,0:T(8,128)(2,1)S(1)}, bf16[8,1536]{1,0:T(8,128)(2,1)S(1)}, u32[]{:S(2)}, u32[]{:S(2)}) collective-permute-start(bf16[8,1536]{1,0:T(8,128)(2,1)S(1)} %get-tuple-element.21), channel_id=1, source_target_pairs={{0,8},{4,12},{8,4},{12,0},{1,9},{5,13},{9,5},{13,1},{2,10},{6,14},... | collective-permute-start | bytes 73736 | tf_op jit(solution)/shard_map/ppermute | solution.py:34
  4.1 0.1 collective-permute-start.2
  4.1 1.4 %prepare.1 = (bf16[768,512]{1,0:T(8,128)(2,1)S(1)}, bf16[768,128]{1,0:T(8,128)(2,1)S(1)}, f32[64,128]{1,0:T(8,128)S(1)}, f32[4,128]{1,0:T(4,128)S(1)}, s32[8,128]{1,0:T(8,128)S(1)}) custom-call(bf16[4,2,600]{2,1,0:T(2,128)(2,1)} %templates.1, s32[2,4]{1,0:T(2,128)} %bitcast.3, s32[2,4]{1,0:T(2,128)} %bitcast.4, s32[2,4]{1,0:T(2,128)} %bitcast.5), custom_call_target="tpu_custom_call" | custom-call | flops 2000000 | bytes 2000000 | tf_op jit(solution)/shard_map/prepare/pallas_call | solution.py:234
  5.6 0.2 %collective-permute-done.refs_1_ = bf16[8,1536]{1,0:T(8,128)(2,1)S(1)} collective-permute-done((bf16[8,1536]{1,0:T(8,128)(2,1)S(1)}, bf16[8,1536]{1,0:T(8,128)(2,1)S(1)}, u32[]{:S(2)}, u32[]{:S(2)}) %collective-permute-start) | collective-permute-done | bytes 24608 | tf_op jit(solution)/shard_map/ppermute | solution.py:34
  5.8 0.9 %collective-permute-done.1.refs_2_ = bf16[8,1536]{1,0:T(8,128)(2,1)S(1)} collective-permute-done((bf16[8,1536]{1,0:T(8,128)(2,1)S(1)}, bf16[8,1536]{1,0:T(8,128)(2,1)S(1)}, u32[]{:S(2)}, u32[]{:S(2)}) %collective-permute-start.1) | collective-permute-done | bytes 24608 | tf_op jit(solution)/shard_map/ppermute | solution.py:34
  6.7 0.0 collective-permute-done.2.refs_3_
  6.7 0.6 %correlate.1 = (f32[8,128]{1,0:T(8,128)S(1)}, f32[8,128]{1,0:T(8,128)S(1)}, f32[8,128]{1,0:T(8,128)S(1)}, f32[8,128]{1,0:T(8,128)S(1)}) custom-call(s32[8,128]{1,0:T(8,128)S(1)} %get-tuple-element.18.table, bf16[8,1536]{1,0:T(8,128)(2,1)S(1)} %get-tuple-element.19.refs_0_, bf16[8,1536]{1,0:T(8,128)(2,1)S(1)} %collective-permute-done.refs_1_, ...), custom_call_target="tpu_custom_call" | custom-call | tf_op jit(solution)/shard_map/correlate/pallas_call | solution.py:234
  7.3 2.6 %collective-permute-start.3 = (f32[8,128]{1,0:T(8,128)S(1)}, f32[8,128]{1,0:T(8,128)S(1)}, u32[]{:S(2)}, u32[]{:S(2)}) collective-permute-start(f32[8,128]{1,0:T(8,128)S(1)} %get-tuple-element.28), channel_id=1, source_target_pairs={{0,2},{1,3},{2,1},{3,0},{4,6},{5,7},{6,5},{7,4},{8,10},{9,11},{10,... | collective-permute-start | bytes 12296 | tf_op jit(solution)/shard_map/ppermute | solution.py:34
  9.9 1.2 %collective-permute-start.4 = (f32[8,128]{1,0:T(8,128)S(1)}, f32[8,128]{1,0:T(8,128)S(1)}, u32[]{:S(2)}, u32[]{:S(2)}) collective-permute-start(f32[8,128]{1,0:T(8,128)S(1)} %get-tuple-element.29), channel_id=1, source_target_pairs={{0,3},{1,2},{2,0},{3,1},{4,7},{5,6},{6,4},{7,5},{8,11},{9,10},{10,... | collective-permute-start | bytes 12296 | tf_op jit(solution)/shard_map/ppermute | solution.py:34
  11.2 0.3 %collective-permute-start.5 = (f32[8,128]{1,0:T(8,128)S(1)}, f32[8,128]{1,0:T(8,128)S(1)}, u32[]{:S(2)}, u32[]{:S(2)}) collective-permute-start(f32[8,128]{1,0:T(8,128)S(1)} %get-tuple-element.30), channel_id=1, source_target_pairs={{0,1},{1,0},{2,3},{3,2},{4,5},{5,4},{6,7},{7,6},{8,9},{9,8},{10,11... | collective-permute-start | bytes 12296 | tf_op jit(solution)/shard_map/ppermute | solution.py:34
  11.5 1.2 %collective-permute-done.3 = f32[8,128]{1,0:T(8,128)S(1)} collective-permute-done((f32[8,128]{1,0:T(8,128)S(1)}, f32[8,128]{1,0:T(8,128)S(1)}, u32[]{:S(2)}, u32[]{:S(2)}) %collective-permute-start.3) | collective-permute-done | bytes 4128 | tf_op jit(solution)/shard_map/ppermute | solution.py:34
  12.7 1.7 %collective-permute-done.4 = f32[8,128]{1,0:T(8,128)S(1)} collective-permute-done((f32[8,128]{1,0:T(8,128)S(1)}, f32[8,128]{1,0:T(8,128)S(1)}, u32[]{:S(2)}, u32[]{:S(2)}) %collective-permute-start.4) | collective-permute-done | bytes 4128 | tf_op jit(solution)/shard_map/ppermute | solution.py:34
  14.4 0.3 %collective-permute-done.5 = f32[8,128]{1,0:T(8,128)S(1)} collective-permute-done((f32[8,128]{1,0:T(8,128)S(1)}, f32[8,128]{1,0:T(8,128)S(1)}, u32[]{:S(2)}, u32[]{:S(2)}) %collective-permute-start.5) | collective-permute-done | bytes 4128 | tf_op jit(solution)/shard_map/ppermute | solution.py:34
  14.8 0.6 %rsqrt_multiply_fusion = f32[4,128]{1,0:T(4,128)} fusion(f32[8,128]{1,0:T(8,128)S(1)} %collective-permute-done.5, f32[8,128]{1,0:T(8,128)S(1)} %collective-permute-done.4, f32[8,128]{1,0:T(8,128)S(1)} %collective-permute-done.3, f32[8,128]{1,0:T(8,128)S(1)} %get-tuple-element.27), kind=kLoop, calls=%fused_computation | loop fusion | flops 3584 | bytes 18432 | tf_op jit(solution)/shard_map/div | solution.py:312
Async XLA Ops:
  1.0 4.8 %collective-permute-start = (bf16[8,1536]{1,0:T(8,128)(2,1)S(1)}, bf16[8,1536]{1,0:T(8,128)(2,1)S(1)}, u32[]{:S(2)}, u32[]{:S(2)}) collective-permute-start(bf16[8,1536]{1,0:T(8,128)(2,1)S(1)} %get-tuple-element.20), channel_id=1, source_target_pairs={{0,12},{4,8},{8,0},{12,4},{1,13},{5,9},{9,1},{13,5},{2,14},{6,10},... | collective-permute-start | bytes 73736 | tf_op jit(solution)/shard_map/ppermute | solution.py:34
  3.4 3.3 %collective-permute-start.1 = (bf16[8,1536]{1,0:T(8,128)(2,1)S(1)}, bf16[8,1536]{1,0:T(8,128)(2,1)S(1)}, u32[]{:S(2)}, u32[]{:S(2)}) collective-permute-start(bf16[8,1536]{1,0:T(8,128)(2,1)S(1)} %get-tuple-element.21), channel_id=1, source_target_pairs={{0,8},{4,12},{8,4},{12,0},{1,9},{5,13},{9,5},{13,1},{2,10},{6,14},... | collective-permute-start | bytes 73736 | tf_op jit(solution)/shard_map/ppermute | solution.py:34
  4.1 2.6 %collective-permute-start.2 = (bf16[8,1536]{1,0:T(8,128)(2,1)S(1)}, bf16[8,1536]{1,0:T(8,128)(2,1)S(1)}, u32[]{:S(2)}, u32[]{:S(2)}) collective-permute-start(bf16[8,1536]{1,0:T(8,128)(2,1)S(1)} %get-tuple-element.22), channel_id=1, source_target_pairs={{0,4},{4,0},{8,12},{12,8},{1,5},{5,1},{9,13},{13,9},{2,6},{6,2},{1... | collective-permute-start | bytes 73736 | tf_op jit(solution)/shard_map/ppermute | solution.py:34
  7.3 5.5 %collective-permute-start.3 = (f32[8,128]{1,0:T(8,128)S(1)}, f32[8,128]{1,0:T(8,128)S(1)}, u32[]{:S(2)}, u32[]{:S(2)}) collective-permute-start(f32[8,128]{1,0:T(8,128)S(1)} %get-tuple-element.28), channel_id=1, source_target_pairs={{0,2},{1,3},{2,1},{3,0},{4,6},{5,7},{6,5},{7,4},{8,10},{9,11},{10,... | collective-permute-start | bytes 12296 | tf_op jit(solution)/shard_map/ppermute | solution.py:34
  9.9 4.5 %collective-permute-start.4 = (f32[8,128]{1,0:T(8,128)S(1)}, f32[8,128]{1,0:T(8,128)S(1)}, u32[]{:S(2)}, u32[]{:S(2)}) collective-permute-start(f32[8,128]{1,0:T(8,128)S(1)} %get-tuple-element.29), channel_id=1, source_target_pairs={{0,3},{1,2},{2,0},{3,1},{4,7},{5,6},{6,4},{7,5},{8,11},{9,10},{10,... | collective-permute-start | bytes 12296 | tf_op jit(solution)/shard_map/ppermute | solution.py:34
  11.2 3.6 %collective-permute-start.5 = (f32[8,128]{1,0:T(8,128)S(1)}, f32[8,128]{1,0:T(8,128)S(1)}, u32[]{:S(2)}, u32[]{:S(2)}) collective-permute-start(f32[8,128]{1,0:T(8,128)S(1)} %get-tuple-element.30), channel_id=1, source_target_pairs={{0,1},{1,0},{2,3},{3,2},{4,5},{5,4},{6,7},{7,6},{8,9},{9,8},{10,11... | collective-permute-start | bytes 12296 | tf_op jit(solution)/shard_map/ppermute | solution.py:34
